TPU v7x, 128 devices: a whole 4x4x4 slice. The times are simulated.
128 devices in a mesh: segment: 8 (over x, core), tp: 16 (over z, y).
Axes of the slice: x: 4, y: 4, z: 4, core: 2. Of those that a mesh axis runs over, the one named last changes fastest.
Arguments:
- latents: bfloat16 [2, 128, 3072], P(None, 'tp'), may hold values from -6 to 6
- cotangent: bfloat16 [2, 128, 3072], P(None, 'tp'), may hold values from -1.5 to 1.5
- token_counts: int32 [2], replicated, may hold values from 32 to 128, as said below
- job_ids: int32 [2], replicated, may hold values from 0 to 15
- modulation: float32 [8, 2, 3, 3072], P('segment'), may hold values from -3 to 3
- w_in: bfloat16 [8, 3072, 12288], P('segment', None, 'tp'), may hold values from -0.109375 to 0.109375
- w_out: bfloat16 [8, 12288, 3072], P('segment', 'tp'), may hold values from -0.0546875 to 0.0546875
- down_in: bfloat16 [8, 16, 16, 3072], P('segment'), may hold values from -0.109375 to 0.109375
- up_in: bfloat16 [8, 16, 16, 12288], P('segment', None, None, 'tp'), may hold values from -0.69921875 to 0.69921875
- down_out: bfloat16 [8, 16, 16, 12288], P('segment', None, None, 'tp'), may hold values from -0.0546875 to 0.0546875
- up_out: bfloat16 [8, 16, 16, 3072], P('segment'), may hold values from -0.69921875 to 0.69921875
Outputs:
- grad_down_in: float32 [8, 16, 16, 3072], P('segment', 'tp')
- grad_up_in: float32 [8, 16, 16, 12288], P('segment', None, None, 'tp')
- grad_down_out: float32 [8, 16, 16, 12288], P('segment', None, None, 'tp')
- grad_up_out: float32 [8, 16, 16, 3072], P('segment', 'tp')
Inputs may be any that keep to these rules, and one draw needn't show every extreme that they name: `token_counts`: at least 32; some micro-batch holds exactly 128 tokens.
All inputs are finite; a program needn't handle non-finite values.
Results may differ from a plain program's by a relative error of at most 0.035.
Values may be sent and summed in bfloat16 or wider, within the bound.
No kernel may reach another device: no remote copies, remote signals or barrier semaphores. Data moves between devices by JAX's collectives and lax.ppermute only.
A program may use at most 128 MiB of HBM per device.

v0:
```python
import math

import jax
import jax.numpy as jnp
from jax import lax
from jax.sharding import PartitionSpec as P

EPS = 1e-06
ROOT_TWO_PI = math.sqrt(2.0 / math.pi)


def shifted(value, axis, by):
    length = lax.axis_size(axis)
    pairs = [(i, i + by) for i in range(length) if 0 <= i + by < length]
    return lax.ppermute(value, axis, pairs)


def gelu_tanh(values):
    inner = ROOT_TWO_PI * (values + 0.044715 * values * values * values)
    return 0.5 * values * (1.0 + jnp.tanh(inner))


def gelu_slope(values):
    inner = ROOT_TWO_PI * (values + 0.044715 * values * values * values)
    tangent = jnp.tanh(inner)
    return 0.5 * (1.0 + tangent) + 0.5 * values * (1.0 - tangent * tangent) * ROOT_TWO_PI * (
        1.0 + 3.0 * 0.044715 * values * values
    )


def rms_stats(resid):
    wide = resid.astype(jnp.float32)
    inv_rms = lax.rsqrt(jnp.mean(wide * wide, axis=-1, keepdims=True) + EPS)
    return (wide, wide * inv_rms, inv_rms)


def stored(store, value, slot, valid):
    previous = store[slot]
    return lax.dynamic_update_index_in_dim(store, jnp.where(valid, value, previous), slot, 0)


def added(store, value, slot):
    return lax.dynamic_update_index_in_dim(store, store[slot] + value, slot, 0)


def shards(
    latents,
    cotangent,
    token_counts,
    job_ids,
    modulation,
    w_in,
    w_out,
    down_in,
    up_in,
    down_out,
    up_out,
):
    tp_count = lax.axis_size("tp")
    phase_count = lax.axis_size("segment")
    phase_pos = lax.axis_index("segment")
    tp_pos = lax.axis_index("tp")
    micro = latents.shape[0]
    width = latents.shape[2]
    w_first = w_in[0]
    w_second = w_out[0]
    mods = modulation[0]
    down_first = down_in[0]
    up_first = up_in[0]
    down_second = down_out[0]
    up_second = up_out[0]
    jobs = down_first.shape[0]
    owned = jobs // tp_count
    rank = down_first.shape[1]
    block_cols = w_first.shape[1]
    full_rows = latents.shape[1] * tp_count
    entry_x, entry_dy = (
        lax.all_gather(latents, "tp", axis=1, tiled=True),
        lax.all_gather(cotangent, "tp", axis=1, tiled=True),
    )
    rows = entry_x.shape[1]
    row_index = lax.iota(jnp.int32, rows)
    masks = (row_index[None, :] < token_counts[:, None]).astype(jnp.float32)[:, :, None]
    entry_x = (entry_x.astype(jnp.float32) * masks).astype(jnp.bfloat16)
    entry_dy = (entry_dy.astype(jnp.float32) * masks).astype(jnp.bfloat16)
    ticks = micro + phase_count - 1

    def forward_tick(tick, carry):
        carried, store_x, store_u, store_pre, store_low_in, store_low_out = carry
        micro_id = tick - phase_pos
        valid = (micro_id >= 0) & (micro_id < micro)
        slot = jnp.clip(micro_id, 0, micro - 1)
        job_id = job_ids[slot]
        mod_row = mods[slot]
        resid = jnp.where(phase_pos == 0, entry_x[slot], carried)
        wide, normed, inv_rms = rms_stats(resid)
        normed_rows = (normed * (1.0 + mod_row[1]) + mod_row[0]).astype(jnp.bfloat16)
        job_down_first = down_first[job_id]
        job_up_first = up_first[job_id]
        job_down_second = down_second[job_id]

        def project(operand):
            low_in = jnp.dot(operand, job_down_first.T, preferred_element_type=jnp.float32).astype(
                jnp.bfloat16
            )
            pre_act = jnp.dot(operand, w_first, preferred_element_type=jnp.float32) + jnp.dot(
                low_in, job_up_first, preferred_element_type=jnp.float32
            )
            activ = gelu_tanh(pre_act).astype(jnp.bfloat16)
            main_part = jnp.dot(activ, w_second, preferred_element_type=jnp.float32)
            low_part = jnp.dot(activ, job_down_second.T, preferred_element_type=jnp.float32)
            return (low_in, pre_act, main_part, low_part)

        def forward_skipped(operand):
            return (
                jnp.zeros((full_rows, rank), jnp.bfloat16),
                jnp.zeros((full_rows, block_cols), jnp.float32),
                jnp.zeros((full_rows, width), jnp.float32),
                jnp.zeros((full_rows, rank), jnp.float32),
            )

        low_in, pre_act, main_part, low_part = lax.cond(
            valid, project, forward_skipped, normed_rows
        )
        main_sum, low_sum = (
            lax.psum(main_part.astype(jnp.bfloat16), "tp").astype(jnp.float32),
            lax.psum(low_part.astype(jnp.bfloat16), "tp").astype(jnp.float32),
        )
        low_out = low_sum.astype(jnp.bfloat16)
        branch = main_sum + jnp.dot(low_out, up_second[job_id], preferred_element_type=jnp.float32)
        result = (wide + mod_row[2] * branch * masks[slot]).astype(jnp.bfloat16)
        store_x = stored(store_x, resid, slot, valid)
        store_u = stored(store_u, normed_rows, slot, valid)
        store_pre = stored(store_pre, pre_act, slot, valid)
        store_low_in = stored(store_low_in, low_in, slot, valid)
        store_low_out = stored(store_low_out, low_out, slot, valid)
        carried = shifted(result, "segment", 1)
        return (carried, store_x, store_u, store_pre, store_low_in, store_low_out)

    start = (
        jnp.zeros((rows, width), jnp.bfloat16),
        jnp.zeros((micro, rows, width), jnp.bfloat16),
        jnp.zeros((micro, full_rows, width), jnp.bfloat16),
        jnp.zeros((micro, full_rows, block_cols), jnp.float32),
        jnp.zeros((micro, full_rows, rank), jnp.bfloat16),
        jnp.zeros((micro, rows, rank), jnp.bfloat16),
    )
    carried, store_x, store_u, store_pre, store_low_in, store_low_out = lax.fori_loop(
        0, ticks, forward_tick, start
    )

    def backward_tick(tick, carry):
        carried, acc_down_first, acc_up_first, acc_down_second, acc_up_second = carry
        micro_id = tick - (phase_count - 1 - phase_pos)
        valid = (micro_id >= 0) & (micro_id < micro)
        slot = jnp.clip(micro_id, 0, micro - 1)
        job_id = job_ids[slot]
        mod_row = mods[slot]
        upstream = jnp.where(phase_pos == phase_count - 1, entry_dy[slot], carried)
        up_wide = upstream.astype(jnp.float32) * masks[slot]
        wide, normed, inv_rms = rms_stats(store_x[slot])
        job_up_second = up_second[job_id]
        job_down_second = down_second[job_id]
        job_up_first = up_first[job_id]
        job_down_first = down_first[job_id]
        grad_branch = (mod_row[2] * up_wide).astype(jnp.bfloat16)
        grad_low_out = jnp.dot(
            grad_branch, job_up_second.T, preferred_element_type=jnp.float32
        ).astype(jnp.bfloat16)
        branch_full, low_full = (grad_branch, grad_low_out)
        normed_in = store_u[slot]
        pre_act = store_pre[slot]
        low_in = store_low_in[slot]
        low_out = store_low_out[slot]

        def backward_local(operands):
            branch_rows, low_out_rows, branch_all, low_all = operands
            up_second_term = jnp.dot(
                low_out_rows.T, branch_rows, preferred_element_type=jnp.float32
            )
            grad_activ = jnp.dot(
                branch_all, w_second.T, preferred_element_type=jnp.float32
            ) + jnp.dot(low_all, job_down_second, preferred_element_type=jnp.float32)
            activ = gelu_tanh(pre_act).astype(jnp.bfloat16)
            down_second_term = jnp.dot(low_all.T, activ, preferred_element_type=jnp.float32)
            grad_pre = (grad_activ * gelu_slope(pre_act)).astype(jnp.bfloat16)
            up_first_term = jnp.dot(low_in.T, grad_pre, preferred_element_type=jnp.float32)
            grad_low_in = jnp.dot(
                grad_pre, job_up_first.T, preferred_element_type=jnp.float32
            ).astype(jnp.bfloat16)
            down_first_term = jnp.dot(grad_low_in.T, normed_in, preferred_element_type=jnp.float32)
            normed_part = jnp.dot(
                grad_pre, w_first.T, preferred_element_type=jnp.float32
            ) + jnp.dot(grad_low_in, job_down_first, preferred_element_type=jnp.float32)
            return (normed_part, down_first_term, up_first_term, down_second_term, up_second_term)

        def backward_skipped(operands):
            return (
                jnp.zeros((full_rows, width), jnp.float32),
                jnp.zeros((rank, width), jnp.float32),
                jnp.zeros((rank, block_cols), jnp.float32),
                jnp.zeros((rank, block_cols), jnp.float32),
                jnp.zeros((rank, width), jnp.float32),
            )

        normed_part, down_first_term, up_first_term, down_second_term, up_second_term = lax.cond(
            valid, backward_local, backward_skipped, (grad_branch, low_out, branch_full, low_full)
        )
        grad_normed = lax.psum(normed_part.astype(jnp.bfloat16), "tp").astype(jnp.float32)
        scaled = grad_normed * (1.0 + mod_row[1])
        result = (
            up_wide
            + inv_rms * (scaled - normed * jnp.mean(scaled * normed, axis=-1, keepdims=True))
        ).astype(jnp.bfloat16)
        acc_down_first = added(acc_down_first, down_first_term, job_id)
        acc_up_first = added(acc_up_first, up_first_term, job_id)
        acc_down_second = added(acc_down_second, down_second_term, job_id)
        acc_up_second = added(acc_up_second, up_second_term, job_id)
        carried = shifted(result, "segment", -1)
        return (carried, acc_down_first, acc_up_first, acc_down_second, acc_up_second)

    start = (
        jnp.zeros((rows, width), jnp.bfloat16),
        jnp.zeros((jobs, rank, width), jnp.float32),
        jnp.zeros((jobs, rank, block_cols), jnp.float32),
        jnp.zeros((jobs, rank, block_cols), jnp.float32),
        jnp.zeros((jobs, rank, width), jnp.float32),
    )
    carried, acc_down_first, acc_up_first, acc_down_second, acc_up_second = lax.fori_loop(
        0, ticks, backward_tick, start
    )
    owned_down = lax.psum_scatter(
        acc_down_first.astype(jnp.bfloat16), "tp", scatter_dimension=0, tiled=True
    ).astype(jnp.float32)
    owned_up = lax.dynamic_slice_in_dim(acc_up_second, tp_pos * owned, owned, 0)
    return (owned_down[None], acc_up_first[None], acc_down_second[None], owned_up[None])


def solution(mesh):
    return jax.shard_map(
        shards,
        mesh=mesh,
        in_specs=(
            P(None, "tp", None),
            P(None, "tp", None),
            P(),
            P(),
            P("segment", None, None, None),
            P("segment", None, "tp"),
            P("segment", "tp", None),
            P("segment", None, None, None),
            P("segment", None, None, "tp"),
            P("segment", None, None, "tp"),
            P("segment", None, None, None),
        ),
        out_specs=(
            P("segment", "tp", None, None),
            P("segment", None, None, "tp"),
            P("segment", None, None, "tp"),
            P("segment", "tp", None, None),
        ),
        check_vma=False,
    )
```

profile of v0, /device:TPU:1, one launch (start us, length us, event | category | flops | bytes accessed | tf_op | source)
XLA Modules:
  0.0 2361.1 jit_solution(15847728185776825469)
XLA Ops:
  12.2 44.3 %all-gather.5.cloned.1.call-done = bf16[2,128,3072]{2,1,0:T(8,128)(2,1)} async-done(((bf16[2,8,3072]{2,1,0:T(8,128)(2,1)}), bf16[2,128,3072]{2,1,0:T(8,128)(2,1)}) %all-gather.5.cloned.1.call-update) | async-done | bytes 1572880 | tf_op jit(solution)/shard_map/all_gather | solution.py:78
  56.5 45.5 %all-gather.3.cloned.1.call-done = bf16[2,128,3072]{2,1,0:T(8,128)(2,1)} async-done(((bf16[2,8,3072]{2,1,0:T(8,128)(2,1)}), bf16[2,128,3072]{2,1,0:T(8,128)(2,1)}) %all-gather.3.cloned.1.call-update) | async-done | bytes 1572880 | tf_op jit(solution)/shard_map/all_gather | solution.py:79
  111.2 1069.4 %while.47 = (s32[]{:T(128)}, bf16[128,3072]{1,0:T(8,128)(2,1)}, bf16[2,128,3072]{2,1,0:T(8,128)(2,1)S(1)}, bf16[2,128,3072]{2,1,0:T(8,128)(2,1)}, f32[2,128,768]...) while((s32[]{:T(128)}, bf16[128,3072]{1,0:T(8,128)(2,1)}, ...), condition=%wide.region_6.7_spmd, body=%wide.region_0.6_spmd.sunk | while | flops 1248865408 | bytes 70453568 | solution.py:148
  122.7 31.1 %psum.40 = bf16[128,16]{0,1:T(8,128)(2,1)S(1)} all-reduce(bf16[128,16]{0,1:T(8,128)(2,1)S(1)} %get-tuple-element.1444), channel_id=1, replica_groups=mesh['segment'=8,'tp'=16] {'tp'}, use_global_device_ids=true, to_apply=%region_5.5 | all-reduce | flops 2048 | bytes 8192 | tf_op jit(solution)/shard_map/while/body/eval_jaxpr/psum | solution.py:127
  156.0 57.2 %all-reduce.4.cloned.1.call-done = bf16[128,3072]{1,0:T(8,128)(2,1)} async-done(((bf16[128,3072]{1,0:T(8,128)(2,1)}), bf16[128,3072]{1,0:T(8,128)(2,1)}) %all-reduce.4.cloned.1.call-update) | async-done | bytes 786448 | tf_op jit(solution)/shard_map/while/body/eval_jaxpr/psum | solution.py:126
  282.4 47.9 %all-reduce.4.cloned.1.call-done = bf16[128,3072]{1,0:T(8,128)(2,1)} async-done(((bf16[128,3072]{1,0:T(8,128)(2,1)}), bf16[128,3072]{1,0:T(8,128)(2,1)}) %all-reduce.4.cloned.1.call-update) | async-done | bytes 786448 | tf_op jit(solution)/shard_map/while/body/eval_jaxpr/psum | solution.py:126
  399.5 50.0 %all-reduce.4.cloned.1.call-done = bf16[128,3072]{1,0:T(8,128)(2,1)} async-done(((bf16[128,3072]{1,0:T(8,128)(2,1)}), bf16[128,3072]{1,0:T(8,128)(2,1)}) %all-reduce.4.cloned.1.call-update) | async-done | bytes 786448 | tf_op jit(solution)/shard_map/while/body/eval_jaxpr/psum | solution.py:126
  510.7 58.1 %all-reduce.4.cloned.1.call-done = bf16[128,3072]{1,0:T(8,128)(2,1)} async-done(((bf16[128,3072]{1,0:T(8,128)(2,1)}), bf16[128,3072]{1,0:T(8,128)(2,1)}) %all-reduce.4.cloned.1.call-update) | async-done | bytes 786448 | tf_op jit(solution)/shard_map/while/body/eval_jaxpr/psum | solution.py:126
  629.9 59.6 %all-reduce.4.cloned.1.call-done = bf16[128,3072]{1,0:T(8,128)(2,1)} async-done(((bf16[128,3072]{1,0:T(8,128)(2,1)}), bf16[128,3072]{1,0:T(8,128)(2,1)}) %all-reduce.4.cloned.1.call-update) | async-done | bytes 786448 | tf_op jit(solution)/shard_map/while/body/eval_jaxpr/psum | solution.py:126
  750.7 59.6 %all-reduce.4.cloned.1.call-done = bf16[128,3072]{1,0:T(8,128)(2,1)} async-done(((bf16[128,3072]{1,0:T(8,128)(2,1)}), bf16[128,3072]{1,0:T(8,128)(2,1)}) %all-reduce.4.cloned.1.call-update) | async-done | bytes 786448 | tf_op jit(solution)/shard_map/while/body/eval_jaxpr/psum | solution.py:126
  871.4 59.3 %all-reduce.4.cloned.1.call-done = bf16[128,3072]{1,0:T(8,128)(2,1)} async-done(((bf16[128,3072]{1,0:T(8,128)(2,1)}), bf16[128,3072]{1,0:T(8,128)(2,1)}) %all-reduce.4.cloned.1.call-update) | async-done | bytes 786448 | tf_op jit(solution)/shard_map/while/body/eval_jaxpr/psum | solution.py:126
  991.9 59.3 %all-reduce.4.cloned.1.call-done = bf16[128,3072]{1,0:T(8,128)(2,1)} async-done(((bf16[128,3072]{1,0:T(8,128)(2,1)}), bf16[128,3072]{1,0:T(8,128)(2,1)}) %all-reduce.4.cloned.1.call-update) | async-done | bytes 786448 | tf_op jit(solution)/shard_map/while/body/eval_jaxpr/psum | solution.py:126
  1112.5 51.5 %all-reduce.4.cloned.1.call-done = bf16[128,3072]{1,0:T(8,128)(2,1)} async-done(((bf16[128,3072]{1,0:T(8,128)(2,1)}), bf16[128,3072]{1,0:T(8,128)(2,1)}) %all-reduce.4.cloned.1.call-update) | async-done | bytes 786448 | tf_op jit(solution)/shard_map/while/body/eval_jaxpr/psum | solution.py:126
  1186.6 1091.5 %while.48 = (s32[]{:T(128)}, bf16[128,3072]{1,0:T(8,128)(2,1)S(1)}, f32[16,16,3072]{2,1,0:T(8,128)}, f32[16,16,768]{2,1,0:T(8,128)}, f32[16,16,768]{2,1,0:T(8,12...) while((s32[]{:T(128)}, bf16[128,3072]{1,0:T(8,128)(2,1)S(1)}, ...), condition=%wide.region_13.14_spmd, body=%wide.region_7.13_spmd.sunk | while | flops 1285258368 | bytes 68994952 | solution.py:229
  1202.8 81.4 %all-reduce.6.cloned.1.call-done = bf16[128,3072]{1,0:T(8,128)(2,1)} async-done(((bf16[128,3072]{1,0:T(8,128)(2,1)}), bf16[128,3072]{1,0:T(8,128)(2,1)}) %all-reduce.6.cloned.1.call-update) | async-done | bytes 786448 | tf_op jit(solution)/shard_map/while/body/eval_jaxpr/psum | solution.py:209
  1318.8 88.2 %all-reduce.6.cloned.1.call-done = bf16[128,3072]{1,0:T(8,128)(2,1)} async-done(((bf16[128,3072]{1,0:T(8,128)(2,1)}), bf16[128,3072]{1,0:T(8,128)(2,1)}) %all-reduce.6.cloned.1.call-update) | async-done | bytes 786448 | tf_op jit(solution)/shard_map/while/body/eval_jaxpr/psum | solution.py:209
  1441.6 89.6 %all-reduce.6.cloned.1.call-done = bf16[128,3072]{1,0:T(8,128)(2,1)} async-done(((bf16[128,3072]{1,0:T(8,128)(2,1)}), bf16[128,3072]{1,0:T(8,128)(2,1)}) %all-reduce.6.cloned.1.call-update) | async-done | bytes 786448 | tf_op jit(solution)/shard_map/while/body/eval_jaxpr/psum | solution.py:209
  1565.9 89.6 %all-reduce.6.cloned.1.call-done = bf16[128,3072]{1,0:T(8,128)(2,1)} async-done(((bf16[128,3072]{1,0:T(8,128)(2,1)}), bf16[128,3072]{1,0:T(8,128)(2,1)}) %all-reduce.6.cloned.1.call-update) | async-done | bytes 786448 | tf_op jit(solution)/shard_map/while/body/eval_jaxpr/psum | solution.py:209
  1690.1 88.5 %all-reduce.6.cloned.1.call-done = bf16[128,3072]{1,0:T(8,128)(2,1)} async-done(((bf16[128,3072]{1,0:T(8,128)(2,1)}), bf16[128,3072]{1,0:T(8,128)(2,1)}) %all-reduce.6.cloned.1.call-update) | async-done | bytes 786448 | tf_op jit(solution)/shard_map/while/body/eval_jaxpr/psum | solution.py:209
  1813.2 88.4 %all-reduce.6.cloned.1.call-done = bf16[128,3072]{1,0:T(8,128)(2,1)} async-done(((bf16[128,3072]{1,0:T(8,128)(2,1)}), bf16[128,3072]{1,0:T(8,128)(2,1)}) %all-reduce.6.cloned.1.call-update) | async-done | bytes 786448 | tf_op jit(solution)/shard_map/while/body/eval_jaxpr/psum | solution.py:209
  1947.5 76.1 %all-reduce.6.cloned.1.call-done = bf16[128,3072]{1,0:T(8,128)(2,1)} async-done(((bf16[128,3072]{1,0:T(8,128)(2,1)}), bf16[128,3072]{1,0:T(8,128)(2,1)}) %all-reduce.6.cloned.1.call-update) | async-done | bytes 786448 | tf_op jit(solution)/shard_map/while/body/eval_jaxpr/psum | solution.py:209
  2069.6 76.1 %all-reduce.6.cloned.1.call-done = bf16[128,3072]{1,0:T(8,128)(2,1)} async-done(((bf16[128,3072]{1,0:T(8,128)(2,1)}), bf16[128,3072]{1,0:T(8,128)(2,1)}) %all-reduce.6.cloned.1.call-update) | async-done | bytes 786448 | tf_op jit(solution)/shard_map/while/body/eval_jaxpr/psum | solution.py:209
  2180.4 79.3 %all-reduce.6.cloned.1.call-done = bf16[128,3072]{1,0:T(8,128)(2,1)} async-done(((bf16[128,3072]{1,0:T(8,128)(2,1)}), bf16[128,3072]{1,0:T(8,128)(2,1)}) %all-reduce.6.cloned.1.call-update) | async-done | bytes 786448 | tf_op jit(solution)/shard_map/while/body/eval_jaxpr/psum | solution.py:209
  2283.0 69.7 %reduce-scatter.4.cloned.1.call-done = bf16[1,16,3072]{2,1,0:T(8,128)(2,1)} async-done(((bf16[16,16,3072]{2,1,0:T(8,128)(2,1)}), bf16[1,16,3072]{2,1,0:T(8,128)(2,1)}) %reduce-scatter.4.cloned.1.call-update) | async-done | bytes 98320
  (741 shorter events, 935.1 us)
Async XLA Ops:
  7.2 49.4 %all-gather.5.cloned.1.call-start = ((), (), s32[]{:S(2)}) async-start(), calls=%async_computation.2 | async-start | bytes 1671168 | tf_op jit(solution)/shard_map/all_gather | solution.py:78
  7.9 94.1 %all-gather.3.cloned.1.call-start = ((), (), s32[]{:S(2)}) async-start(), calls=%async_computation.1 | async-start | bytes 1671168 | tf_op jit(solution)/shard_map/all_gather | solution.py:79
  111.2 102.0 %all-reduce.4.cloned.1.call-start = ((), (), s32[]{:S(2)}) async-start(), calls=%async_computation.4 | async-start | bytes 1572864 | tf_op jit(solution)/shard_map/while/body/eval_jaxpr/psum | solution.py:126
  229.8 100.5 %all-reduce.4.cloned.1.call-start = ((), (), s32[]{:S(2)}) async-start(), calls=%async_computation.4 | async-start | bytes 1572864 | tf_op jit(solution)/shard_map/while/body/eval_jaxpr/psum | solution.py:126
  346.9 102.7 %all-reduce.4.cloned.1.call-start = ((), (), s32[]{:S(2)}) async-start(), calls=%async_computation.4 | async-start | bytes 1572864 | tf_op jit(solution)/shard_map/while/body/eval_jaxpr/psum | solution.py:126
  466.1 102.6 %all-reduce.4.cloned.1.call-start = ((), (), s32[]{:S(2)}) async-start(), calls=%async_computation.4 | async-start | bytes 1572864 | tf_op jit(solution)/shard_map/while/body/eval_jaxpr/psum | solution.py:126
  585.3 104.2 %all-reduce.4.cloned.1.call-start = ((), (), s32[]{:S(2)}) async-start(), calls=%async_computation.4 | async-start | bytes 1572864 | tf_op jit(solution)/shard_map/while/body/eval_jaxpr/psum | solution.py:126
  706.1 104.2 %all-reduce.4.cloned.1.call-start = ((), (), s32[]{:S(2)}) async-start(), calls=%async_computation.4 | async-start | bytes 1572864 | tf_op jit(solution)/shard_map/while/body/eval_jaxpr/psum | solution.py:126
  826.8 103.9 %all-reduce.4.cloned.1.call-start = ((), (), s32[]{:S(2)}) async-start(), calls=%async_computation.4 | async-start | bytes 1572864 | tf_op jit(solution)/shard_map/while/body/eval_jaxpr/psum | solution.py:126
  947.4 103.9 %all-reduce.4.cloned.1.call-start = ((), (), s32[]{:S(2)}) async-start(), calls=%async_computation.4 | async-start | bytes 1572864 | tf_op jit(solution)/shard_map/while/body/eval_jaxpr/psum | solution.py:126
  1067.8 96.2 %all-reduce.4.cloned.1.call-start = ((), (), s32[]{:S(2)}) async-start(), calls=%async_computation.4 | async-start | bytes 1572864 | tf_op jit(solution)/shard_map/while/body/eval_jaxpr/psum | solution.py:126
  1186.6 97.6 %all-reduce.6.cloned.1.call-start = ((), (), s32[]{:S(2)}) async-start(), calls=%async_computation.5 | async-start | bytes 1572864 | tf_op jit(solution)/shard_map/while/body/eval_jaxpr/psum | solution.py:209
  1287.8 14.8 collective-permute-start.1
  1302.6 104.4 %all-reduce.6.cloned.1.call-start = ((), (), s32[]{:S(2)}) async-start(), calls=%async_computation.5 | async-start | bytes 1572864 | tf_op jit(solution)/shard_map/while/body/eval_jaxpr/psum | solution.py:209
  1410.6 14.8 collective-permute-start.1
  1425.4 105.8 %all-reduce.6.cloned.1.call-start = ((), (), s32[]{:S(2)}) async-start(), calls=%async_computation.5 | async-start | bytes 1572864 | tf_op jit(solution)/shard_map/while/body/eval_jaxpr/psum | solution.py:209
  1549.6 105.8 %all-reduce.6.cloned.1.call-start = ((), (), s32[]{:S(2)}) async-start(), calls=%async_computation.5 | async-start | bytes 1572864 | tf_op jit(solution)/shard_map/while/body/eval_jaxpr/psum | solution.py:209
  1673.8 104.7 %all-reduce.6.cloned.1.call-start = ((), (), s32[]{:S(2)}) async-start(), calls=%async_computation.5 | async-start | bytes 1572864 | tf_op jit(solution)/shard_map/while/body/eval_jaxpr/psum | solution.py:209
  1797.0 104.6 %all-reduce.6.cloned.1.call-start = ((), (), s32[]{:S(2)}) async-start(), calls=%async_computation.5 | async-start | bytes 1572864 | tf_op jit(solution)/shard_map/while/body/eval_jaxpr/psum | solution.py:209
  1905.2 14.8 collective-permute-start.1
  1920.0 103.7 %all-reduce.6.cloned.1.call-start = ((), (), s32[]{:S(2)}) async-start(), calls=%async_computation.5 | async-start | bytes 1572864 | tf_op jit(solution)/shard_map/while/body/eval_jaxpr/psum | solution.py:209
  2042.1 103.7 %all-reduce.6.cloned.1.call-start = ((), (), s32[]{:S(2)}) async-start(), calls=%async_computation.5 | async-start | bytes 1572864 | tf_op jit(solution)/shard_map/while/body/eval_jaxpr/psum | solution.py:209
  2164.2 95.5 %all-reduce.6.cloned.1.call-start = ((), (), s32[]{:S(2)}) async-start(), calls=%async_computation.5 | async-start | bytes 1572864 | tf_op jit(solution)/shard_map/while/body/eval_jaxpr/psum | solution.py:209
  2278.1 74.6 %reduce-scatter.4.cloned.1.call-start = ((), (), s32[]{:S(2)}) async-start(), calls=%async_computation.3 | async-start | bytes 1671168
  (142 other events, 1259.6 us)
Sparse Core Ops, SparseCore 0:
  10.1 46.3 all-gather.4
  58.7 43.3 all-gather.2
  122.8 90.3 all-reduce.3
  249.3 80.9 all-reduce.3
  366.3 83.1 all-reduce.3
  477.6 91.0 all-reduce.3
  596.8 92.6 all-reduce.3
  717.6 92.6 all-reduce.3
  838.3 92.3 all-reduce.3
  958.8 92.3 all-reduce.3
  1079.3 84.6 all-reduce.3
  1198.0 86.2 all-reduce.5
  1313.9 93.0 all-reduce.5
  1436.8 94.4 all-reduce.5
  1561.0 94.4 all-reduce.5
  1685.2 93.3 all-reduce.5
  1808.3 93.2 all-reduce.5
  1942.6 80.9 all-reduce.5
  2064.7 80.9 all-reduce.5
  2175.5 84.1 all-reduce.5
  2282.1 70.5 reduce-scatter.3
where the time goes:
time: 2370 us; the launch traced here: 2360 us
  waiting for transfers between devices  1550 us (65%)
  blocking collectives  279 us (12%)
  local copies, waits for them, and re-layouts  176 us (7%)
  other arithmetic  151 us (6%)
  starting transfers between devices  82 us (3%)
  matrix products  72.6 us (3%)
  loops' own time  37.7 us (2%)
    psum x9, waiting for transfers between devices, backward_tick(): lax.psum(normed_part.astype(jnp.bfloat16), 'tp').astype(jnp.float32)  757 us
    psum x9, waiting for transfers between devices, forward_tick(): lax.psum(main_part.astype(jnp.bfloat16), 'tp').astype(jnp.float32)  503 us
    psum x9, blocking collectives, forward_tick(): lax.psum(low_part.astype(jnp.bfloat16), 'tp').astype(jnp.float32)  279 us
    ppermute x18, waiting for transfers between devices, shifted(): return lax.ppermute(value, axis, pairs)  128 us
    ppermute x18, starting transfers between devices, shifted(): return lax.ppermute(value, axis, pairs)  81.9 us
    unnamed x4, waiting for transfers between devices  71.1 us
  transfers between devices with their start and end apart: 39, of which 39 were waited for; matrix products, arithmetic and copies ran while one was open for 5% of the time, Pallas kernels for 0%

commit v1 on v0

v1 whole, which is shorter than its diff:
```python
import math

import jax
import jax.numpy as jnp
from jax import lax
from jax.sharding import PartitionSpec as P

EPS = 1e-06
ROOT_TWO_PI = math.sqrt(2.0 / math.pi)
F32 = jnp.float32
BF16 = jnp.bfloat16
PAD = 128


def gelu_and_slope(values):
    inner = ROOT_TWO_PI * (values + 0.044715 * values * values * values)
    tangent = jnp.tanh(inner)
    activ = 0.5 * values * (1.0 + tangent)
    slope = 0.5 * (1.0 + tangent) + 0.5 * values * (1.0 - tangent * tangent) * ROOT_TWO_PI * (
        1.0 + 3.0 * 0.044715 * values * values
    )
    return activ, slope


def rms_stats(resid):
    wide = resid.astype(F32)
    inv_rms = lax.rsqrt(jnp.mean(wide * wide, axis=-1, keepdims=True) + EPS)
    return wide, wide * inv_rms, inv_rms


def dot(a, b, a_dim, b_dim):
    return lax.dot_general(a, b, (((a_dim,), (b_dim,)), ((), ())), preferred_element_type=F32)


def gathered(rows, tp):
    spread = jnp.broadcast_to(rows[None], (tp,) + rows.shape)
    got = lax.all_to_all(spread, "tp", 0, 0)
    return got.reshape(tp * rows.shape[0], rows.shape[1])


def scattered(parts, tp):
    cut = parts.reshape(tp, parts.shape[0] // tp, parts.shape[1])
    return lax.all_to_all(cut, "tp", 0, 0).astype(F32).sum(0)


def shards(
    latents,
    cotangent,
    token_counts,
    job_ids,
    modulation,
    w_in,
    w_out,
    down_in,
    up_in,
    down_out,
    up_out,
):
    tp = lax.axis_size("tp")
    segments = lax.axis_size("segment")
    planes = segments // 2
    seg = lax.axis_index("segment")
    plane, core = seg // 2, seg % 2
    tp_pos = lax.axis_index("tp")
    micro, own_rows, width = latents.shape
    cols = w_in.shape[2]
    jobs, rank = down_in.shape[1], down_in.shape[2]
    rows = own_rows * tp
    swap = [(s, s ^ 1) for s in range(segments)]
    onward = [(s, (s + 2) % segments) for s in range(segments)]
    back = [(d, s) for s, d in onward]

    job = job_ids[core]
    other_job = job_ids[1 - core]
    adapters = [a[0] for a in (down_in, up_in, down_out, up_out)]

    def packed(which):
        return jnp.concatenate([a[which] for a in adapters], axis=1)

    def ordered(own, other):
        return (jnp.where(core == 0, own, other), jnp.where(core == 0, other, own))

    w_first = ordered(w_in[0], lax.ppermute(w_in[0], "segment", swap))
    w_second = ordered(w_out[0], lax.ppermute(w_out[0], "segment", swap))
    low_own, low_other = packed(job), lax.ppermute(packed(other_job), "segment", swap)
    mods = ordered(
        modulation[0, core], lax.ppermute(modulation[0, 1 - core], "segment", swap)
    )
    cuts = (width, width + cols, width + 2 * cols)
    lows = [jnp.split(pack, cuts, axis=1) for pack in ordered(low_own, low_other)]

    row_index = tp_pos * own_rows + lax.iota(jnp.int32, own_rows)
    mask = (row_index < token_counts[core]).astype(F32)[:, None]
    x = (latents[core].astype(F32) * mask).astype(BF16)
    e_last = (cotangent[core].astype(F32) * mask).astype(BF16)

    def gate_rows(e, i):
        return (mods[i][2:3] * e.astype(F32)).astype(BF16)

    def forward(x, i, last):
        low_d_in, low_u_in, low_d_out, low_u_out = lows[i]
        wide, normed, inv_rms = rms_stats(x)
        u = gathered((normed * (1.0 + mods[i][1:2]) + mods[i][0:1]).astype(BF16), tp)
        low_in = dot(u, low_d_in, 1, 1).astype(BF16)
        pre = dot(u, w_first[i], 1, 0) + dot(low_in, low_u_in, 1, 0)
        activ = gelu_and_slope(pre)[0].astype(BF16)
        low_part = dot(activ, low_d_out, 1, 1).astype(BF16)
        saved = (x, u, pre, low_in, low_part)
        if last:
            return x, saved
        main_part = dot(activ, w_second[i], 1, 0).astype(BF16)
        sent = jnp.concatenate([main_part, jnp.pad(low_part, ((0, 0), (0, PAD - rank)))], axis=1)
        sums = scattered(sent, tp)
        low_out = sums[:, width : width + rank].astype(BF16)
        branch = sums[:, :width] + dot(low_out, low_u_out, 1, 0)
        return (wide + mods[i][2:3] * branch * mask).astype(BF16), saved

    def backward(e, i, saved, g_branch, first):
        low_d_in, low_u_in, low_d_out, low_u_out = lows[i]
        x, u, pre, low_in, low_part = saved
        if g_branch is None:
            g_branch = gathered(gate_rows(e, i), tp)
        g_low_out = dot(g_branch, low_u_out, 1, 1).astype(BF16)
        g_act = dot(g_branch, w_second[i], 1, 1) + dot(g_low_out, low_d_out, 1, 0)
        activ, slope = gelu_and_slope(pre)
        grad_down_out = dot(g_low_out, activ.astype(BF16), 0, 0)
        g_pre = (g_act * slope).astype(BF16)
        grad_up_in = dot(low_in, g_pre, 0, 0)
        g_low_in = dot(g_pre, low_u_in, 1, 1).astype(BF16)
        kept = (g_branch, g_low_in, grad_up_in, grad_down_out)
        if first:
            return e, kept
        part = dot(g_pre, w_first[i], 1, 1) + dot(g_low_in, low_d_in, 1, 0)
        g_u = scattered(part.astype(BF16), tp)
        wide, normed, inv_rms = rms_stats(x)
        q = g_u * (1.0 + mods[i][1:2])
        mean = jnp.mean(q * normed, axis=-1, keepdims=True)
        return (e.astype(F32) + inv_rms * (q - normed * mean)).astype(BF16), kept

    def zeros(*shape, dtype=BF16):
        return jnp.zeros(shape, dtype)

    def no_saved():
        return (
            zeros(own_rows, width),
            zeros(rows, width),
            zeros(rows, cols, dtype=F32),
            zeros(rows, rank),
            zeros(rows, rank),
        )

    def no_kept():
        return (
            zeros(rows, width),
            zeros(rows, rank),
            zeros(rank, cols, dtype=F32),
            zeros(rank, cols, dtype=F32),
        )

    def forward_plane(x, p):
        x, saved0 = forward(x, 0, False)
        x, saved1 = forward(x, 1, p == planes - 1)
        return x, (saved0, saved1)

    def backward_plane(e, saved, p, g_branch=None):
        e, kept1 = backward(e, 1, saved[1], g_branch, False)
        e, kept0 = backward(e, 0, saved[0], None, p == 0)
        return e, (kept0, kept1)

    g_last = lax.cond(
        plane == planes - 1,
        lambda e: gathered(gate_rows(e, 1), tp),
        lambda e: zeros(rows, width),
        e_last,
    )
    saved = (no_saved(), no_saved())
    kept = (no_kept(), no_kept())
    for p in range(planes - 1):
        x, saved = lax.cond(
            plane == p,
            lambda x, saved: forward_plane(x, p),
            lambda x, saved: (x, saved),
            x,
            saved,
        )
        x = lax.ppermute(x, "segment", onward)

    def turn(x, saved, kept):
        x, saved = forward_plane(x, planes - 1)
        e, kept = backward_plane(e_last, saved, planes - 1, g_last)
        return e, saved, kept

    e, saved, kept = lax.cond(
        plane == planes - 1, turn, lambda x, saved, kept: (x, saved, kept), x, saved, kept
    )
    for p in range(planes - 2, -1, -1):
        e = lax.ppermute(e, "segment", back)
        e, kept = lax.cond(
            plane == p,
            lambda e, saved, kept: backward_plane(e, saved, p),
            lambda e, saved, kept: (e, kept),
            e,
            saved,
            kept,
        )

    narrow = jnp.stack([saved[0][4].T, saved[1][4].T, kept[0][1].T, kept[1][1].T])
    got = lax.all_to_all(jnp.broadcast_to(narrow[None], (tp,) + narrow.shape), "tp", 0, 0)
    narrow_sum = got.astype(F32).sum(0)
    grads = []
    for i in range(2):
        low_out = narrow_sum[i].astype(BF16)
        grad_up_out = dot(low_out, kept[i][0], 1, 0)
        g_low = narrow_sum[2 + i]
        high = g_low.astype(BF16)
        rest = (g_low - high.astype(F32)).astype(BF16)
        grad_down_in = dot(high, saved[i][1], 1, 0) + dot(rest, saved[i][1], 1, 0)
        grads.append(jnp.concatenate([grad_down_in, kept[i][2], kept[i][3], grad_up_out], axis=1))
    mine = jnp.where(core == 0, grads[0], grads[1])
    theirs = lax.ppermute(jnp.where(core == 0, grads[1], grads[0]), "segment", swap)

    def by_job(own, other):
        index = lax.iota(jnp.int32, jobs)[:, None, None]
        return jnp.where(index == job, own[None], 0.0) + jnp.where(
            index == other_job, other[None], 0.0
        )

    def owned(own, other):
        owners = jobs // tp
        index = tp_pos * owners + lax.iota(jnp.int32, owners)[:, None, None]
        return jnp.where(index == job, own[None], 0.0) + jnp.where(
            index == other_job, other[None], 0.0
        )

    own_d_in, own_u_in, own_d_out, own_u_out = jnp.split(mine, cuts, axis=1)
    oth_d_in, oth_u_in, oth_d_out, oth_u_out = jnp.split(theirs, cuts, axis=1)
    return (
        owned(own_d_in, oth_d_in)[None],
        by_job(own_u_in, oth_u_in)[None],
        by_job(own_d_out, oth_d_out)[None],
        owned(own_u_out, oth_u_out)[None],
    )


def solution(mesh):
    return jax.shard_map(
        shards,
        mesh=mesh,
        in_specs=(
            P(None, "tp", None),
            P(None, "tp", None),
            P(),
            P(),
            P("segment", None, None, None),
            P("segment", None, "tp"),
            P("segment", "tp", None),
            P("segment", None, None, None),
            P("segment", None, None, "tp"),
            P("segment", None, None, "tp"),
            P("segment", None, None, None),
        ),
        out_specs=(
            P("segment", "tp", None, None),
            P("segment", None, None, "tp"),
            P("segment", None, None, "tp"),
            P("segment", "tp", None, None),
        ),
        check_vma=False,
    )
```

time: 2370 us -> 749 us (0.32)
  waiting for transfers between devices: 1550 us -> 119 us
  starting transfers between devices: 82 us -> 420 us
  blocking collectives: 279 us -> 76.3 us
  local copies, waits for them, and re-layouts: 176 us -> 15.8 us
  other arithmetic: 151 us -> 31.1 us
  matrix products: 72.6 us -> 46.7 us
    psum x18 -> x0, waiting for transfers between devices: 1260 us -> none  [the longest x9 757 us: backward_tick(): lax.psum(normed_part.astype(jnp.bfloat16), 'tp').astype(jnp.float32)]
    ppermute x18 -> x11, starting transfers between devices: 81.9 us -> 409 us  [the longest x3 290 us: shards(): e = lax.ppermute(e, 'segment', back)]
    psum x9 -> x0, blocking collectives: 279 us -> none  [forward_tick(): lax.psum(low_part.astype(jnp.bfloat16), 'tp').astype(jnp.float32)]
    all_gather x2 -> x0, waiting for transfers between devices: 89.8 us -> none  [the longest x1 45.5 us: shards(): lax.all_gather(cotangent, 'tp', axis=1, tiled=True)]
    dynamic_slice x81 -> x3, local copies, waits for them, and re-layouts: 81.5 us -> 3.61 us  [the longest x1 1.35 us: shards(): job = job_ids[core]]
    all_to_all x0 -> x5, blocking collectives: none -> 76.3 us  [the longest x3 51.6 us: gathered(): got = lax.all_to_all(spread, 'tp', 0, 0)]
    dynamic_update_slice x63 -> x0, other arithmetic: 71.5 us -> none  [the longest x45 41.9 us: stored(): lax.dynamic_update_index_in_dim(store, jnp.where(valid, value, previous),...]
    unnamed x4 -> x0, waiting for transfers between devices: 71.1 us -> none
  transfers between devices with their start and end apart: 39 -> 14, of which waited for: 39 -> 11; matrix products, arithmetic and copies ran while one was open for 5% -> 3% of each run, Pallas kernels for 0% -> 0%
where the time goes in v1:
time: 749 us; the launch traced here: 738 us
  starting transfers between devices  420 us (56%)
  waiting for transfers between devices  119 us (16%)
  blocking collectives  76.3 us (10%)
  matrix products  46.7 us (6%)
  other arithmetic  31.1 us (4%)
  loops' own time  23.1 us (3%)
  local copies, waits for them, and re-layouts  15.8 us (2%)
    ppermute x3, starting transfers between devices, shards(): e = lax.ppermute(e, 'segment', back)  290 us
    ppermute x3, waiting for transfers between devices, shards(): e = lax.ppermute(e, 'segment', back)  82 us
    ppermute x3, starting transfers between devices, shards(): x = lax.ppermute(x, 'segment', onward)  75.9 us
    all_to_all x3, blocking collectives, gathered(): got = lax.all_to_all(spread, 'tp', 0, 0)  51.6 us
    dot_general x32, matrix products, dot(): lax.dot_general(a, b, (((a_dim,), (b_dim,)), ((), ())), preferred_element...  46.7 us
    ppermute x1, starting transfers between devices, shards(): lax.ppermute(jnp.where(core == 0, grads[1], grads[0]), 'segment', swap)  40.7 us
    all_to_all x2, waiting for transfers between devices, scattered(): return lax.all_to_all(cut, 'tp', 0, 0).astype(F32).sum(0)  21.6 us
    select_n x4, other arithmetic, ordered(): return (jnp.where(core == 0, own, other), jnp.where(core == 0, other, own))  15.9 us
  transfers between devices with their start and end apart: 14, of which 11 were waited for; matrix products, arithmetic and copies ran while one was open for 3% of the time, Pallas kernels for 0%

profile of v1, /device:TPU:1, one launch (start us, length us, event | category | flops | bytes accessed | tf_op | source)
XLA Modules:
  0.0 738.3 jit_solution(12656219153197314940)
XLA Ops:
  18.5 6.6 broadcast_select_fusion
  25.3 8.6 %broadcast_select_fusion.2 = (bf16[3072,768]{1,0:T(8,128)(2,1)}, bf16[3072,768]{1,0:T(8,128)(2,1)}) fusion(bf16[3072,768]{1,0:T(8,128)(2,1)} %collective-permute-done.1, pred[]{:T(512)S(6)} %eq.65, bf16[1,3072,768]{2,1,0:T(8,128)(2,1)S(1)} %bitcast.433), kind=kLoop, calls=%fused_computation.470 | loop fusion | flops 4718592 | bytes 18874368 | tf_op jit(solution)/shard_map/jit(_where)/select_n | solution.py:81
  33.9 94.0 %conditional.8 = (bf16[8,3072]{1,0:T(8,128)(2,1)S(1)}, bf16[8,3072]{1,0:T(8,128)(2,1)S(1)}, bf16[128,3072]{1,0:T(8,128)(2,1)}, f32[128,768]{1,0:T(8,128)}, bf16[...) conditional(s32[]{:T(128)} %convert_element_type.509, ...), branch_computations={%region_0.1_spmd, %region_1.6_spmd} | conditional | flops 2466967552 | bytes 63939216 | solution.py:179
  35.2 21.5 %all_to_all.125 = bf16[16,8,3072]{2,1,0:T(8,128)(2,1)S(1)} all-to-all(bf16[16,8,3072]{2,1,0:T(8,128)(2,1)S(1)} %broadcast_in_dim.139), channel_id=1, replica_groups=mesh['segment'=8,'tp'=16] {'tp'}, dimensions={0} | all-to-all | bytes 1572864 | tf_op jit(solution)/shard_map/cond/branch_1_fun/all_to_all | solution.py:37
  70.2 13.0 %all-to-all-done.2 = bf16[16,8,3200]{2,1,0:T(8,128)(2,1)S(1)} async-done(((bf16[16,8,3200]{2,1,0:T(8,128)(2,1)}), bf16[16,8,3200]{2,1,0:T(8,128)(2,1)S(1)}, u32[]{:S(2)}, u32[]{:S(2)}) %all-to-all-start.2) | async-done | bytes 819232 | tf_op jit(solution)/shard_map/cond/branch_1_fun/all_to_all | solution.py:43
  85.2 16.8 %all_to_all.126 = bf16[16,8,3072]{2,1,0:T(8,128)(2,1)S(1)} all-to-all(bf16[16,8,3072]{2,1,0:T(8,128)(2,1)S(1)} %broadcast_in_dim.140), channel_id=1, replica_groups=mesh['segment'=8,'tp'=16] {'tp'}, dimensions={0} | all-to-all | bytes 1572864 | tf_op jit(solution)/shard_map/cond/branch_1_fun/all_to_all | solution.py:37
  112.6 14.3 %all_to_all.136 = bf16[16,8,3200]{2,1,0:T(8,128)(2,1)S(1)} all-to-all(bf16[16,8,3200]{2,1,0:T(8,128)(2,1)S(1)} %fusion.13), channel_id=1, replica_groups=mesh['segment'=8,'tp'=16] {'tp'}, dimensions={0} | all-to-all | bytes 1638400 | tf_op jit(solution)/shard_map/cond/branch_1_fun/all_to_all | solution.py:43
  128.0 4.1 collective-permute-done.4
  132.2 7.7 %conditional.9 = ((bf16[8,3072]{1,0:T(8,128)(2,1)S(1)}, bf16[8,3072]{1,0:T(8,128)(2,1)S(1)}, bf16[128,3072]{1,0:T(8,128)(2,1)}, f32[128,768]{1,0:T(8,128)}, bf16...) conditional(s32[]{:T(128)} %convert_element_type.508, ...), branch_computations={%region_6.7_spmd, %region_7.12_spmd} | conditional | flops 2466967552 | bytes 79012584 | solution.py:179
  139.9 73.8 %collective-permute-start.5 = (bf16[8,3072]{1,0:T(8,128)(2,1)S(1)}, bf16[8,3072]{1,0:T(8,128)(2,1)S(1)}, u32[]{:S(2)}, u32[]{:S(2)}) collective-permute-start(bf16[8,3072]{1,0:T(8,128)(2,1)S(1)} %get-tuple-element.610), channel_id=1, source_target_pairs={{0,32},{16,48},{32,64},{48,80},{64,96},{80,112},{96,0},{112,16},{1... | collective-permute-start | bytes 147464 | tf_op jit(solution)/shard_map/ppermute | solution.py:186
  219.0 14.7 %conditional.12 = (bf16[8,3072]{1,0:T(8,128)(2,1)S(1)}, bf16[8,3072]{1,0:T(8,128)(2,1)S(1)}, bf16[128,3072]{1,0:T(8,128)(2,1)}, f32[128,768]{1,0:T(8,128)}, bf16...) conditional(s32[]{:T(128)} %convert_element_type.506, ...), branch_computations={%region_20.21_spmd, %region_21.29_spmd} | conditional | flops 4355855360 | bytes 119821968 | solution.py:193
  233.7 197.7 %collective-permute-start.7 = (bf16[8,3072]{1,0:T(8,128)(2,1)S(1)}, bf16[8,3072]{1,0:T(8,128)(2,1)S(1)}, u32[]{:S(2)}, u32[]{:S(2)}) collective-permute-start(bf16[8,3072]{1,0:T(8,128)(2,1)S(1)} %get-tuple-element.634), channel_id=1, source_target_pairs={{32,0},{48,16},{64,32},{80,48},{96,64},{112,80},{0,96},{16,112},{3... | collective-permute-start | bytes 147464 | tf_op jit(solution)/shard_map/ppermute | solution.py:197
  436.8 6.4 conditional.14
  443.2 89.4 %collective-permute-start.9 = (bf16[8,3072]{1,0:T(8,128)(2,1)S(1)}, bf16[8,3072]{1,0:T(8,128)(2,1)S(1)}, u32[]{:S(2)}, u32[]{:S(2)}) collective-permute-start(bf16[8,3072]{1,0:T(8,128)(2,1)S(1)} %get-tuple-element.666), channel_id=1, source_target_pairs={{32,0},{48,16},{64,32},{80,48},{96,64},{112,80},{0,96},{16,112},{3... | collective-permute-start | bytes 147464 | tf_op jit(solution)/shard_map/ppermute | solution.py:197
  532.6 79.7 %collective-permute-done.9 = bf16[8,3072]{1,0:T(8,128)(2,1)S(1)} collective-permute-done((bf16[8,3072]{1,0:T(8,128)(2,1)S(1)}, bf16[8,3072]{1,0:T(8,128)(2,1)S(1)}, u32[]{:S(2)}, u32[]{:S(2)}) %collective-permute-start.9) | collective-permute-done | bytes 49184 | tf_op jit(solution)/shard_map/ppermute | solution.py:197
  612.3 65.7 %conditional.15 = ((bf16[128,3072]{1,0:T(8,128)(2,1)}, bf16[128,16]{0,1:T(8,128)(2,1)}, f32[16,768]{1,0:T(8,128)}, f32[16,768]{1,0:T(8,128)}, bf16[128,3072]{1,0...) conditional(s32[]{:T(128)} %convert_element_type.509, ...), branch_computations={%region_45.46_spmd, %region_46.50_spmd} | conditional | flops 1882680320 | bytes 54596224 | solution.py:198
  612.4 13.3 %all_to_all.134 = bf16[16,8,3072]{2,1,0:T(8,128)(2,1)S(1)} all-to-all(bf16[16,8,3072]{2,1,0:T(8,128)(2,1)S(1)} %broadcast_in_dim.175), channel_id=1, replica_groups=mesh['segment'=8,'tp'=16] {'tp'}, dimensions={0} | all-to-all | bytes 1572864 | tf_op jit(solution)/shard_map/cond/branch_1_fun/all_to_all | solution.py:37
  626.1 4.5 fusion.311
  640.5 8.6 %all-to-all-done.28 = bf16[16,8,3072]{2,1,0:T(8,128)(2,1)S(1)} async-done(((bf16[16,8,3072]{2,1,0:T(8,128)(2,1)}), bf16[16,8,3072]{2,1,0:T(8,128)(2,1)S(1)}, u32[]{:S(2)}, u32[]{:S(2)}) %all-to-all-start.28) | async-done | bytes 786464 | tf_op jit(solution)/shard_map/cond/branch_1_fun/all_to_all | solution.py:43
  652.1 4.3 all-to-all-start.29
  660.0 6.8 all-to-all-done.29
  666.8 4.3 fusion.313
  678.8 10.4 %all_to_all.135 = bf16[16,4,16,128]{3,2,1,0:T(8,128)(2,1)S(1)} all-to-all(bf16[16,4,16,128]{3,2,1,0:T(8,128)(2,1)S(1)} %broadcast_in_dim.205), channel_id=1, replica_groups=mesh['segment'=8,'tp'=16] {'tp'}, dimensions={0} | all-to-all | bytes 524288 | tf_op jit(solution)/shard_map/all_to_all | solution.py:208
  692.7 40.7 %collective-permute-start.10 = (f32[16,7680]{1,0:T(8,128)S(1)}, f32[16,7680]{1,0:T(8,128)S(1)}, u32[]{:S(2)}, u32[]{:S(2)}) collective-permute-start(f32[16,7680]{1,0:T(8,128)S(1)} %get-tuple-element.805), channel_id=1, source_target_pairs={{0,16},{16,0},{32,48},{48,32},{64,80},{80,64},{96,112},{112,96},{1... | collective-permute-start | bytes 1474568 | tf_op jit(solution)/shard_map/ppermute | solution.py:220
  (165 shorter events, 91.0 us)
Async XLA Ops:
  7.5 8.0 %collective-permute-start.2 = (bf16[16,7680]{1,0:T(8,128)(2,1)S(1)}, bf16[16,7680]{1,0:T(8,128)(2,1)S(1)}, u32[]{:S(2)}, u32[]{:S(2)}) collective-permute-start(bf16[16,7680]{1,0:T(8,128)(2,1)S(1)} %pad_maximum_fusion.3), channel_id=1, source_target_pairs={{0,16},{16,0},{32,48},{48,32},{64,80},{80,64},{96,112},{112,96},{1... | collective-permute-start | bytes 737288 | tf_op jit(solution)/shard_map/ppermute | solution.py:85
  10.1 4.8 collective-permute-start
  10.2 8.4 %collective-permute-start.3 = (bf16[768,3072]{1,0:T(8,128)(2,1)}, bf16[768,3072]{1,0:T(8,128)(2,1)}, u32[]{:S(2)}, u32[]{:S(2)}) collective-permute-start(bf16[768,3072]{1,0:T(8,128)(2,1)} %bitcast.430), channel_id=1, source_target_pairs={{0,16},{16,0},{32,48},{48,32},{64,80},{80,64},{96,112},{112,96},{1... | collective-permute-start | bytes 14155784 | tf_op jit(solution)/shard_map/ppermute | solution.py:84
  10.7 14.6 %collective-permute-start.1 = (bf16[3072,768]{1,0:T(8,128)(2,1)}, bf16[3072,768]{1,0:T(8,128)(2,1)}, u32[]{:S(2)}, u32[]{:S(2)}) collective-permute-start(bf16[3072,768]{1,0:T(8,128)(2,1)} %bitcast.431), channel_id=1, source_target_pairs={{0,16},{16,0},{32,48},{48,32},{64,80},{80,64},{96,112},{112,96},{1... | collective-permute-start | bytes 14155784 | tf_op jit(solution)/shard_map/ppermute | solution.py:83
  35.2 27.2 %copy-start.45 = (bf16[16,768]{1,0:T(8,128)(2,1)S(1)}, bf16[16,768]{1,0:T(8,128)(2,1)}, u32[]{:S(2)}) copy-start(bf16[16,768]{1,0:T(8,128)(2,1)} %get-tuple-element.384) | copy-start | bytes 73732 | tf_op jit(solution)/shard_map/cond
  63.7 19.6 %copy-start.27 = (bf16[128,16]{1,0:T(8,128)(2,1)}, bf16[128,16]{1,0:T(8,128)(2,1)S(1)}, u32[]{:S(2)}) copy-start(bf16[128,16]{1,0:T(8,128)(2,1)S(1)} %convolution_convert_fusion.3) | copy-start | bytes 12292 | tf_op jit(solution)/shard_map/cond
  63.7 19.6 %copy-start.17 = (bf16[16,3072]{1,0:T(8,128)(2,1)S(1)}, bf16[16,3072]{1,0:T(8,128)(2,1)}, u32[]{:S(2)}) copy-start(bf16[16,3072]{1,0:T(8,128)(2,1)} %get-tuple-element.385) | copy-start | bytes 294916 | tf_op jit(solution)/shard_map/cond
  66.5 16.7 %all-to-all-start.2 = ((bf16[16,8,3200]{2,1,0:T(8,128)(2,1)}), bf16[16,8,3200]{2,1,0:T(8,128)(2,1)S(1)}, u32[]{:S(2)}, u32[]{:S(2)}) async-start(bf16[16,8,3200]{2,1,0:T(8,128)(2,1)} %fusion.11), calls=%async_computation.2 | async-start | bytes 1638400 | tf_op jit(solution)/shard_map/cond/branch_1_fun/all_to_all | solution.py:43
  85.2 22.9 %slice-start.12 = ((s8[4718592]{0:T(1024)(128)(4,1)}), s8[4194304]{0:T(1024)(128)(4,1)S(1)}, s32[]{:S(2)}) async-start(s8[4718592]{0:T(1024)(128)(4,1)} %bitcast.390), calls=%async_computation.43 | async-start | bytes 8388608 | tf_op jit(solution)/shard_map/cond
  128.0 4.2 collective-permute-start.4
  139.9 75.0 %collective-permute-start.5 = (bf16[8,3072]{1,0:T(8,128)(2,1)S(1)}, bf16[8,3072]{1,0:T(8,128)(2,1)S(1)}, u32[]{:S(2)}, u32[]{:S(2)}) collective-permute-start(bf16[8,3072]{1,0:T(8,128)(2,1)S(1)} %get-tuple-element.610), channel_id=1, source_target_pairs={{0,32},{16,48},{32,64},{48,80},{64,96},{80,112},{96,0},{112,16},{1... | collective-permute-start | bytes 147464 | tf_op jit(solution)/shard_map/ppermute | solution.py:186
  214.9 4.2 collective-permute-start.6
  233.7 198.9 %copy-start.12 = (bf16[128,3072]{1,0:T(8,128)(2,1)}, bf16[128,3072]{1,0:T(8,128)(2,1)S(1)}, u32[]{:S(2)}) copy-start(bf16[128,3072]{1,0:T(8,128)(2,1)S(1)} %get-tuple-element.639) | copy-start | bytes 2359300
  233.7 198.9 %collective-permute-start.7 = (bf16[8,3072]{1,0:T(8,128)(2,1)S(1)}, bf16[8,3072]{1,0:T(8,128)(2,1)S(1)}, u32[]{:S(2)}, u32[]{:S(2)}) collective-permute-start(bf16[8,3072]{1,0:T(8,128)(2,1)S(1)} %get-tuple-element.634), channel_id=1, source_target_pairs={{32,0},{48,16},{64,32},{80,48},{96,64},{112,80},{0,96},{16,112},{3... | collective-permute-start | bytes 147464 | tf_op jit(solution)/shard_map/ppermute | solution.py:197
  432.6 4.2 collective-permute-start.8
  436.8 95.8 %copy-start.31 = (bf16[128,16]{1,0:T(8,128)(2,1)S(1)}, bf16[128,16]{1,0:T(8,128)(2,1)}, u32[]{:S(2)}) copy-start(bf16[128,16]{1,0:T(8,128)(2,1)} %get-tuple-element.632) | copy-start | bytes 12292
  443.2 169.1 %collective-permute-start.9 = (bf16[8,3072]{1,0:T(8,128)(2,1)S(1)}, bf16[8,3072]{1,0:T(8,128)(2,1)S(1)}, u32[]{:S(2)}, u32[]{:S(2)}) collective-permute-start(bf16[8,3072]{1,0:T(8,128)(2,1)S(1)} %get-tuple-element.666), channel_id=1, source_target_pairs={{32,0},{48,16},{64,32},{80,48},{96,64},{112,80},{0,96},{16,112},{3... | collective-permute-start | bytes 147464 | tf_op jit(solution)/shard_map/ppermute | solution.py:197
  612.3 77.0 %copy-start.6 = (bf16[128,3072]{1,0:T(8,128)(2,1)S(1)}, bf16[128,3072]{1,0:T(8,128)(2,1)}, u32[]{:S(2)}) copy-start(bf16[128,3072]{1,0:T(8,128)(2,1)} %get-tuple-element.669) | copy-start | bytes 2359300
  612.3 77.4 %copy-start.11 = (bf16[128,3072]{1,0:T(8,128)(2,1)S(1)}, bf16[128,3072]{1,0:T(8,128)(2,1)}, u32[]{:S(2)}) copy-start(bf16[128,3072]{1,0:T(8,128)(2,1)} %get-tuple-element.673) | copy-start | bytes 2359300
  625.8 45.3 %copy-start.15 = (bf16[16,8,3072]{2,1,0:T(8,128)(2,1)}, bf16[16,8,3072]{2,1,0:T(8,128)(2,1)S(1)}, u32[]{:S(2)}) copy-start(bf16[16,8,3072]{2,1,0:T(8,128)(2,1)S(1)} %all_to_all.134) | copy-start | bytes 2359300 | tf_op jit(solution)/shard_map/cond
  635.1 14.0 %all-to-all-start.28 = ((bf16[16,8,3072]{2,1,0:T(8,128)(2,1)}), bf16[16,8,3072]{2,1,0:T(8,128)(2,1)S(1)}, u32[]{:S(2)}, u32[]{:S(2)}) async-start(bf16[16,8,3072]{2,1,0:T(8,128)(2,1)} %fusion.244), calls=%async_computation.28 | async-start | bytes 1572864 | tf_op jit(solution)/shard_map/cond/branch_1_fun/all_to_all | solution.py:43
  651.1 20.0 %copy-start.23 = (bf16[16,3072]{1,0:T(8,128)(2,1)S(1)}, bf16[16,3072]{1,0:T(8,128)(2,1)}, u32[]{:S(2)}) copy-start(bf16[16,3072]{1,0:T(8,128)(2,1)} %get-tuple-element.511) | copy-start | bytes 294916 | tf_op jit(solution)/shard_map/cond
  652.1 14.7 %all-to-all-start.29 = ((bf16[16,8,3072]{2,1,0:T(8,128)(2,1)}), bf16[16,8,3072]{2,1,0:T(8,128)(2,1)}, u32[]{:S(2)}, u32[]{:S(2)}) async-start(bf16[16,8,3072]{2,1,0:T(8,128)(2,1)} %broadcast_in_dim.176), calls=%async_computation.29 | async-start | bytes 1572864 | tf_op jit(solution)/shard_map/cond/branch_1_fun/all_to_all | solution.py:37
  692.7 43.2 %collective-permute-start.10 = (f32[16,7680]{1,0:T(8,128)S(1)}, f32[16,7680]{1,0:T(8,128)S(1)}, u32[]{:S(2)}, u32[]{:S(2)}) collective-permute-start(f32[16,7680]{1,0:T(8,128)S(1)} %get-tuple-element.805), channel_id=1, source_target_pairs={{0,16},{16,0},{32,48},{48,32},{64,80},{80,64},{96,112},{112,96},{1... | collective-permute-start | bytes 1474568 | tf_op jit(solution)/shard_map/ppermute | solution.py:220
  (15 other events, 121.6 us)

commit v2 on v1

v2 whole, which is shorter than its diff:
```python
import functools
import math

import jax
import jax.numpy as jnp
from jax import lax
from jax.experimental import pallas as pl
from jax.experimental.pallas import tpu as pltpu
from jax.sharding import PartitionSpec as P

EPS = 1e-06
ROOT_TWO_PI = math.sqrt(2.0 / math.pi)
F32 = jnp.float32
BF16 = jnp.bfloat16
PAD = 128
CUTS = 2
PAIR = 16
VMEM = pl.BlockSpec(memory_space=pltpu.VMEM)
HBM = pl.BlockSpec(memory_space=pltpu.HBM)
SMEM = pl.BlockSpec(memory_space=pltpu.SMEM)
PARAMS = pltpu.CompilerParams(vmem_limit_bytes=40 * 1024 * 1024)


def shape_of(*shape, dtype=BF16):
    return jax.ShapeDtypeStruct(shape, dtype)


def gelu_and_slope(values):
    inner = ROOT_TWO_PI * (values + 0.044715 * values * values * values)
    tangent = jnp.tanh(inner)
    half = 0.5 * (1.0 + tangent)
    slope = half + 0.5 * values * (1.0 - tangent * tangent) * ROOT_TWO_PI * (
        1.0 + 3.0 * 0.044715 * values * values
    )
    return values * half, slope


def rms_stats(wide):
    inv_rms = lax.rsqrt(jnp.mean(wide * wide, axis=-1, keepdims=True) + EPS)
    return wide * inv_rms, inv_rms


def dot(a, b, a_dim, b_dim):
    return lax.dot_general(a, b, (((a_dim,), (b_dim,)), ((), ())), preferred_element_type=F32)


def fetch(own, ours, theirs, buf, sem, at):
    @pl.when(own == 1)
    def _():
        pltpu.make_async_copy(ours.at[at], buf.at[at], sem).start()

    @pl.when(own != 1)
    def _():
        pltpu.make_async_copy(theirs.at[at], buf.at[at], sem).start()


def arrived(ours, buf, sem, at):
    pltpu.make_async_copy(ours.at[at], buf.at[at], sem).wait()


def cut(c, size):
    return pl.ds(c * (size // CUTS), size // CUTS)


def forward_kernel(
    own_ref,
    u_ref,
    wi_own,
    wi_other,
    wo_own,
    wo_other,
    di_ref,
    ui_ref,
    do_ref,
    act_ref,
    slope_ref,
    low_in_ref,
    low_ref,
    *rest,
    last,
):
    sent_ref, (wi_buf, wo_buf, sems) = (None, rest) if last else (rest[0], rest[1:])
    own = own_ref[0]
    width, rank = u_ref.shape[1], di_ref.shape[0]
    for c in range(CUTS):
        fetch(own, wi_own, wi_other, wi_buf, sems.at[c], (cut(c, width),))
    if not last:
        for c in range(CUTS):
            at = (slice(None), cut(c, width))
            fetch(own, wo_own, wo_other, wo_buf, sems.at[CUTS + c], at)
    low_in = dot(u_ref[...], di_ref[...], 1, 1).astype(BF16)
    low_in_ref[...] = low_in
    pre = dot(low_in, ui_ref[...], 1, 0)
    for c in range(CUTS):
        at = cut(c, width)
        arrived(wi_own, wi_buf, sems.at[c], (at,))
        pre = pre + dot(u_ref[:, at], wi_buf[at], 1, 0)
    act, slope = gelu_and_slope(pre)
    act = act.astype(BF16)
    act_ref[...] = act
    slope_ref[...] = slope
    low = dot(act, do_ref[...], 1, 1).astype(BF16)
    low_ref[...] = low
    if last:
        return
    sent_ref[:, width:] = jnp.zeros((sent_ref.shape[0], PAD), BF16)
    sent_ref[:, width : width + rank] = low
    for c in range(CUTS):
        at = (slice(None), cut(c, width))
        arrived(wo_own, wo_buf, sems.at[CUTS + c], at)
        sent_ref[at] = dot(act, wo_buf[at], 1, 0).astype(BF16)


def backward_kernel(
    own_ref,
    g_ref,
    slope_ref,
    act_ref,
    low_in_ref,
    wi_own,
    wi_other,
    wo_own,
    wo_other,
    di_ref,
    ui_ref,
    do_ref,
    uo_ref,
    g_low_in_ref,
    grad_ui_ref,
    grad_do_ref,
    *rest,
    first,
):
    part_ref, (wi_buf, wo_buf, sems) = (None, rest) if first else (rest[0], rest[1:])
    own = own_ref[0]
    width = g_ref.shape[1]
    for c in range(CUTS):
        at = (slice(None), cut(c, width))
        fetch(own, wo_own, wo_other, wo_buf, sems.at[c], at)
    if not first:
        for c in range(CUTS):
            fetch(own, wi_own, wi_other, wi_buf, sems.at[CUTS + c], (cut(c, width),))
    g_low_out = dot(g_ref[...], uo_ref[...], 1, 1).astype(BF16)
    grad_do_ref[...] = dot(g_low_out, act_ref[...], 0, 0)
    g_act = dot(g_low_out, do_ref[...], 1, 0)
    for c in range(CUTS):
        at = (slice(None), cut(c, width))
        arrived(wo_own, wo_buf, sems.at[c], at)
        g_act = g_act + dot(g_ref[at], wo_buf[at], 1, 1)
    g_pre = (g_act * slope_ref[...]).astype(BF16)
    g_low_in = dot(g_pre, ui_ref[...], 1, 1).astype(BF16)
    g_low_in_ref[...] = g_low_in
    grad_ui_ref[...] = dot(low_in_ref[...], g_pre, 0, 0)
    if first:
        return
    for c in range(CUTS):
        at = cut(c, width)
        arrived(wi_own, wi_buf, sems.at[CUTS + c], (at,))
        part = dot(g_pre, wi_buf[at], 1, 1) + dot(g_low_in, di_ref[:, at], 1, 0)
        part_ref[:, at] = part.astype(BF16)


def block_scratch(width, cols, without):
    return [
        pltpu.VMEM((PAIR, PAD) if without == "in" else (width, cols), BF16),
        pltpu.VMEM((PAIR, PAD) if without == "out" else (cols, width), BF16),
        pltpu.SemaphoreType.DMA((2 * CUTS,)),
    ]


def block_cost(rows, width, cols, matmuls):
    return pl.CostEstimate(
        flops=2 * matmuls * rows * width * cols,
        bytes_accessed=2 * matmuls * width * cols,
        transcendentals=rows * cols,
    )


def block_forward(own, u, w_first, w_second, low, last):
    rows, width = u.shape
    cols, rank = w_first[0].shape[1], low[0].shape[0]
    out = [
        shape_of(rows, cols),
        shape_of(rows, cols, dtype=F32),
        shape_of(rows, rank),
        shape_of(rows, rank),
    ]
    out += [] if last else [shape_of(rows, width + PAD)]
    return pl.pallas_call(
        functools.partial(forward_kernel, last=last),
        out_shape=out,
        in_specs=[SMEM, VMEM, HBM, HBM, HBM, HBM, VMEM, VMEM, VMEM],
        out_specs=[VMEM] * len(out),
        scratch_shapes=block_scratch(width, cols, "out" if last else None),
        compiler_params=PARAMS,
        cost_estimate=block_cost(rows, width, cols, 1 if last else 2),
        name="block_forward",
    )(own, u, *w_first, *w_second, *low[:3])


def block_backward(own, g, saved, w_first, w_second, low, first):
    rows, width = g.shape
    cols, rank = w_first[0].shape[1], low[0].shape[0]
    out = [
        shape_of(rows, rank),
        shape_of(rank, cols, dtype=F32),
        shape_of(rank, cols, dtype=F32),
    ]
    out += [] if first else [shape_of(rows, width)]
    act, slope, low_in = saved
    return pl.pallas_call(
        functools.partial(backward_kernel, first=first),
        out_shape=out,
        in_specs=[SMEM] + [VMEM] * 4 + [HBM] * 4 + [VMEM] * 4,
        out_specs=[VMEM] * len(out),
        scratch_shapes=block_scratch(width, cols, "in" if first else None),
        compiler_params=PARAMS,
        cost_estimate=block_cost(rows, width, cols, 1 if first else 2),
        name="block_backward",
    )(own, g, slope, act, low_in, *w_first, *w_second, *low)


def summed(got_ref, own_rows, at):
    total = None
    for k in range(0, got_ref.shape[0], PAIR):
        part = got_ref[k : k + PAIR, at].astype(F32)
        part = part.reshape(PAIR // own_rows, own_rows, part.shape[1]).sum(0)
        total = part if total is None else total + part
    return total


def spread(out_ref, rows):
    pair = jnp.concatenate([rows] * (PAIR // rows.shape[0]), axis=0).astype(BF16)
    for k in range(0, out_ref.shape[0], PAIR):
        out_ref[k : k + PAIR] = pair


def modulated(wide, mod_ref):
    return rms_stats(wide)[0] * (1.0 + mod_ref[1:2]) + mod_ref[0:1]


def first_rows_kernel(pick_ref, x_ref, e_ref, mod_ref, gate_ref, out_ref):
    u = modulated(x_ref[...].astype(F32), mod_ref)
    g = gate_ref[2:3] * e_ref[...].astype(F32)
    spread(out_ref, jnp.where(pick_ref[0] == 1, u, g))


def rows_in_kernel(x_ref, mod_ref, out_ref):
    spread(out_ref, modulated(x_ref[...].astype(F32), mod_ref))


def gate_rows_kernel(e_ref, mod_ref, out_ref):
    spread(out_ref, mod_ref[2:3] * e_ref[...].astype(F32))


def forward_rows_kernel(got_ref, x_ref, mask_ref, mod_ref, uo_ref, next_ref, x_out, *spread_out):
    own_rows, width = x_ref.shape
    rank = uo_ref.shape[0]
    low = summed(got_ref, own_rows, pl.ds(width, PAD)).astype(BF16)[:, :rank]
    branch = summed(got_ref, own_rows, pl.ds(0, width)) + dot(low, uo_ref[...], 1, 0)
    x = x_ref[...].astype(F32) + mod_ref[2:3] * branch * mask_ref[...]
    x = x.astype(BF16)
    x_out[...] = x
    for out_ref in spread_out:
        spread(out_ref, modulated(x.astype(F32), next_ref))


def backward_rows_kernel(got_ref, e_ref, x_ref, mod_ref, next_ref, e_out, *spread_out):
    own_rows, width = x_ref.shape
    normed, inv_rms = rms_stats(x_ref[...].astype(F32))
    q = summed(got_ref, own_rows, pl.ds(0, width)) * (1.0 + mod_ref[1:2])
    mean = jnp.mean(q * normed, axis=-1, keepdims=True)
    e = (e_ref[...].astype(F32) + inv_rms * (q - normed * mean)).astype(BF16)
    e_out[...] = e
    for out_ref in spread_out:
        spread(out_ref, next_ref[2:3] * e.astype(F32))


def rows_call(kernel, out, *operands, scalars=0):
    return pl.pallas_call(
        kernel,
        out_shape=out,
        in_specs=[SMEM] * scalars + [VMEM] * (len(operands) - scalars),
        out_specs=jax.tree.map(lambda _: VMEM, out),
        compiler_params=PARAMS,
        name=kernel.__name__,
    )(*operands)


def exchanged(parts, tp):
    rows, width = parts.shape
    got = lax.all_to_all(parts.reshape(tp, rows // tp, width), "tp", 0, 0)
    return got.reshape(rows, width)


def shards(
    latents,
    cotangent,
    token_counts,
    job_ids,
    modulation,
    w_in,
    w_out,
    down_in,
    up_in,
    down_out,
    up_out,
):
    tp = lax.axis_size("tp")
    segments = lax.axis_size("segment")
    planes = segments // 2
    seg = lax.axis_index("segment")
    plane, core = seg // 2, seg % 2
    tp_pos = lax.axis_index("tp")
    micro, own_rows, width = latents.shape
    cols = w_in.shape[2]
    jobs, rank = down_in.shape[1], down_in.shape[2]
    rows = own_rows * tp
    swap = [(s, s ^ 1) for s in range(segments)]
    onward = [(s, (s + 2) % segments) for s in range(segments)]
    back = [(d, s) for s, d in onward]
    last_plane = planes - 1

    job = job_ids[core]
    other_job = job_ids[1 - core]
    adapters = [a[0] for a in (down_in, up_in, down_out, up_out)]

    def packed(which):
        return jnp.concatenate([a[which] for a in adapters], axis=1)

    def ordered(own, other):
        return (jnp.where(core == 0, own, other), jnp.where(core == 0, other, own))

    mods = ordered(
        modulation[0, core], lax.ppermute(modulation[0, 1 - core], "segment", swap)
    )
    w_first = (w_in[0], lax.ppermute(w_in[0], "segment", swap))
    w_second = (w_out[0], lax.ppermute(w_out[0], "segment", swap))
    low_own, low_other = packed(job), lax.ppermute(packed(other_job), "segment", swap)
    cuts = (width, width + cols, width + 2 * cols)
    lows = [jnp.split(pack, cuts, axis=1) for pack in ordered(low_own, low_other)]
    owns = [(core == i).astype(jnp.int32).reshape(1) for i in range(2)]

    row_index = tp_pos * own_rows + lax.iota(jnp.int32, own_rows)
    mask = (row_index < token_counts[core]).astype(F32)[:, None]
    x = (latents[core].astype(F32) * mask).astype(BF16)
    e_last = (cotangent[core].astype(F32) * mask).astype(BF16)

    full = shape_of(rows, width)
    some = shape_of(own_rows, width)
    ends = exchanged(
        rows_call(
            first_rows_kernel,
            full,
            (plane == 0).astype(jnp.int32).reshape(1),
            x,
            e_last,
            mods[0],
            mods[1],
            scalars=1,
        ),
        tp,
    )

    def forward_plane(x, p):
        saved = []
        for i in range(2):
            if i:
                u = exchanged(sent, tp)
            else:
                u = ends if p == 0 else exchanged(rows_call(rows_in_kernel, full, x, mods[0]), tp)
            last = p == last_plane and i == 1
            act, slope, low_in, low_part, *part = block_forward(
                owns[i], u, w_first, w_second, lows[i], last
            )
            saved.append((x, u, (act, slope, low_in), low_part))
            if last:
                break
            got = exchanged(part[0], tp)
            out = [some] if i else [some, full]
            x, *sent = rows_call(
                forward_rows_kernel, out, got, x, mask, mods[i], lows[i][3], mods[1]
            )
            sent = sent[0] if sent else None
        return x, tuple(saved)

    def backward_plane(e, saved, p):
        kept = [None, None]
        for i in (1, 0):
            if i == 0:
                g = exchanged(sent, tp)
            elif p == last_plane:
                g = ends
            else:
                g = exchanged(rows_call(gate_rows_kernel, full, e, mods[1]), tp)
            x, u, acts, low_part = saved[i]
            first = p == 0 and i == 0
            g_low_in, grad_ui, grad_do, *part = block_backward(
                owns[i], g, acts, w_first, w_second, lows[i], first
            )
            kept[i] = (g, g_low_in, grad_ui, grad_do)
            if first:
                break
            got = exchanged(part[0], tp)
            out = [some, full] if i else [some]
            e, *sent = rows_call(backward_rows_kernel, out, got, e, x, mods[i], mods[0])
            sent = sent[0] if sent else None
        return e, tuple(kept)

    def zeros(*shape, dtype=BF16):
        return jnp.zeros(shape, dtype)

    def no_saved():
        acts = (zeros(rows, cols), zeros(rows, cols, dtype=F32), zeros(rows, rank))
        return (zeros(own_rows, width), zeros(rows, width), acts, zeros(rows, rank))

    def no_kept():
        return (
            zeros(rows, width),
            zeros(rows, rank),
            zeros(rank, cols, dtype=F32),
            zeros(rank, cols, dtype=F32),
        )

    saved = (no_saved(), no_saved())
    kept = (no_kept(), no_kept())
    for p in range(last_plane):
        x, saved = lax.cond(
            plane == p,
            lambda x, saved: forward_plane(x, p),
            lambda x, saved: (x, saved),
            x,
            saved,
        )
        x = lax.ppermute(x, "segment", onward)

    def turn(x, saved, kept):
        x, saved = forward_plane(x, last_plane)
        e, kept = backward_plane(e_last, saved, last_plane)
        return e, saved, kept

    e, saved, kept = lax.cond(
        plane == last_plane, turn, lambda x, saved, kept: (x, saved, kept), x, saved, kept
    )
    for p in range(last_plane - 1, -1, -1):
        e = lax.ppermute(e, "segment", back)
        e, kept = lax.cond(
            plane == p,
            lambda e, saved, kept: backward_plane(e, saved, p),
            lambda e, saved, kept: (e, kept),
            e,
            saved,
            kept,
        )

    narrow = jnp.stack([saved[0][3].T, saved[1][3].T, kept[0][1].T, kept[1][1].T])
    got = lax.all_to_all(jnp.broadcast_to(narrow[None], (tp,) + narrow.shape), "tp", 0, 0)
    narrow_sum = got.astype(F32).sum(0)
    grads = []
    for i in range(2):
        low_out = narrow_sum[i].astype(BF16)
        grad_up_out = dot(low_out, kept[i][0], 1, 0)
        g_low = narrow_sum[2 + i]
        high = g_low.astype(BF16)
        rest = (g_low - high.astype(F32)).astype(BF16)
        grad_down_in = dot(high, saved[i][1], 1, 0) + dot(rest, saved[i][1], 1, 0)
        grads.append(jnp.concatenate([grad_down_in, kept[i][2], kept[i][3], grad_up_out], axis=1))
    mine = jnp.where(core == 0, grads[0], grads[1])
    theirs = lax.ppermute(jnp.where(core == 0, grads[1], grads[0]), "segment", swap)

    def by_job(own, other):
        index = lax.iota(jnp.int32, jobs)[:, None, None]
        return jnp.where(index == job, own[None], 0.0) + jnp.where(
            index == other_job, other[None], 0.0
        )

    def owned(own, other):
        owners = jobs // tp
        index = tp_pos * owners + lax.iota(jnp.int32, owners)[:, None, None]
        return jnp.where(index == job, own[None], 0.0) + jnp.where(
            index == other_job, other[None], 0.0
        )

    own_d_in, own_u_in, own_d_out, own_u_out = jnp.split(mine, cuts, axis=1)
    oth_d_in, oth_u_in, oth_d_out, oth_u_out = jnp.split(theirs, cuts, axis=1)
    return (
        owned(own_d_in, oth_d_in)[None],
        by_job(own_u_in, oth_u_in)[None],
        by_job(own_d_out, oth_d_out)[None],
        owned(own_u_out, oth_u_out)[None],
    )


def solution(mesh):
    return jax.shard_map(
        shards,
        mesh=mesh,
        in_specs=(
            P(None, "tp", None),
            P(None, "tp", None),
            P(),
            P(),
            P("segment", None, None, None),
            P("segment", None, "tp"),
            P("segment", "tp", None),
            P("segment", None, None, None),
            P("segment", None, None, "tp"),
            P("segment", None, None, "tp"),
            P("segment", None, None, None),
        ),
        out_specs=(
            P("segment", "tp", None, None),
            P("segment", None, None, "tp"),
            P("segment", None, None, "tp"),
            P("segment", "tp", None, None),
        ),
        check_vma=False,
    )
```

time: 749 us -> 654 us (0.87)
  matrix products: 46.7 us -> 4.72 us
  starting transfers between devices: 420 us -> 380 us
  Pallas kernels: 0 us -> 29.9 us
  other arithmetic: 31.1 us -> 6.85 us
  waiting for transfers between devices: 119 us -> 106 us
  loops' own time: 23.1 us -> 14.5 us
    dot_general x32 -> x6, matrix products: 46.7 us -> 4.72 us  [dot(): lax.dot_general(a, b, (((a_dim,), (b_dim,)), ((), ())), preferred_element...]
    ppermute x3, starting transfers between devices: 290 us -> 250 us  [shards(): e = lax.ppermute(e, 'segment', back)]
    pallas_call x0 -> x9, Pallas kernels: none -> 29.9 us  [the longest x2 14.7 us: block_backward(): pl.pallas_call(functools.partial(backward_kernel, first=first), out_shape...]
    select_n x4 -> x2, other arithmetic: 15.9 us -> 0.11 us  [ordered(): return (jnp.where(core == 0, own, other), jnp.where(core == 0, other, own))]
    ppermute x3, waiting for transfers between devices: 82 us -> 74 us  [shards(): e = lax.ppermute(e, 'segment', back)]
    ppermute x3, starting transfers between devices: 75.9 us -> 68.2 us  [shards(): x = lax.ppermute(x, 'segment', onward)]
    all_to_all x4 -> x5, blocking collectives: 65.9 us -> 73.4 us  [exchanged(): got = lax.all_to_all(parts.reshape(tp, rows // tp, width), 'tp', 0, 0)]
    all_to_all x3 -> x2, waiting for transfers between devices: 28.5 us -> 24.4 us  [exchanged(): got = lax.all_to_all(parts.reshape(tp, rows // tp, width), 'tp', 0, 0)]
  transfers between devices with their start and end apart: 14 -> 13, of which waited for: 11 -> 8; matrix products, arithmetic and copies ran while one was open for 3% -> 1% of each run, Pallas kernels for 0% -> 0%
where the time goes in v2:
time: 654 us; the launch traced here: 644 us
  starting transfers between devices  380 us (58%)
  waiting for transfers between devices  106 us (16%)
  blocking collectives  83.6 us (13%)
  Pallas kernels  29.9 us (5%)
  loops' own time  14.5 us (2%)
  local copies, waits for them, and re-layouts  12.1 us (2%)
  other arithmetic  6.85 us (1%)
  between operations  6.75 us (1%)
    ppermute x3, starting transfers between devices, shards(): e = lax.ppermute(e, 'segment', back)  250 us
    ppermute x3, waiting for transfers between devices, shards(): e = lax.ppermute(e, 'segment', back)  74 us
    all_to_all x5, blocking collectives, exchanged(): got = lax.all_to_all(parts.reshape(tp, rows // tp, width), 'tp', 0, 0)  73.4 us
    ppermute x3, starting transfers between devices, shards(): x = lax.ppermute(x, 'segment', onward)  68.2 us
    ppermute x1, starting transfers between devices, shards(): lax.ppermute(jnp.where(core == 0, grads[1], grads[0]), 'segment', swap)  47.4 us
    all_to_all x2, waiting for transfers between devices, exchanged(): got = lax.all_to_all(parts.reshape(tp, rows // tp, width), 'tp', 0, 0)  24.4 us
    pallas_call x2, Pallas kernels, block_backward(): pl.pallas_call(functools.partial(backward_kernel, first=first), out_shape...  14.7 us
  transfers between devices with their start and end apart: 13, of which 8 were waited for; matrix products, arithmetic and copies ran while one was open for 1% of the time, Pallas kernels for 0%

profile of v2, /device:TPU:1, one launch (start us, length us, event | category | flops | bytes accessed | tf_op | source)
XLA Modules:
  0.0 643.9 jit_solution(4119278030089519749)
XLA Ops:
  15.8 7.9 %all-to-all-start.28 = ((bf16[16,8,3072]{2,1,0:T(8,128)(2,1)}), bf16[16,8,3072]{2,1,0:T(8,128)(2,1)S(1)}, u32[]{:S(2)}, u32[]{:S(2)}) async-start(bf16[16,8,3072]{2,1,0:T(8,128)(2,1)} %bitcast.64), calls=%async_computation.28 | async-start | bytes 1572864 | tf_op jit(solution)/shard_map/all_to_all | solution.py:292
  23.8 13.3 %all-to-all-done.28 = bf16[16,8,3072]{2,1,0:T(8,128)(2,1)S(1)} async-done(((bf16[16,8,3072]{2,1,0:T(8,128)(2,1)}), bf16[16,8,3072]{2,1,0:T(8,128)(2,1)S(1)}, u32[]{:S(2)}, u32[]{:S(2)}) %all-to-all-start.28) | async-done | bytes 786464 | tf_op jit(solution)/shard_map/all_to_all | solution.py:292
  37.1 60.1 %conditional.7 = (bf16[8,3072]{1,0:T(8,128)(2,1)S(1)}, bf16[8,3072]{1,0:T(8,128)(2,1)S(1)}, bf16[128,3072]{1,0:T(8,128)(2,1)S(1)}, bf16[128,768]{1,0:T(8,128)(2,...) conditional(s32[]{:T(128)} %convert_element_type.84, ...), branch_computations={%region_0.1_spmd, %region_1.2_spmd} | conditional | flops 2415919104 | bytes 54427880 | solution.py:428
  37.1 4.8 block_forward.8
  41.9 17.4 %all_to_all.122 = bf16[16,8,3200]{2,1,0:T(8,128)(2,1)S(1)} all-to-all(bf16[16,8,3200]{2,1,0:T(8,128)(2,1)S(1)} %bitcast.172), channel_id=1, replica_groups=mesh['segment'=8,'tp'=16] {'tp'}, dimensions={0} | all-to-all | bytes 1638400 | tf_op jit(solution)/shard_map/cond/branch_1_fun/all_to_all | solution.py:292
  60.1 15.5 %all_to_all.123 = bf16[16,8,3072]{2,1,0:T(8,128)(2,1)} all-to-all(bf16[16,8,3072]{2,1,0:T(8,128)(2,1)S(1)} %bitcast.185), channel_id=1, replica_groups=mesh['segment'=8,'tp'=16] {'tp'}, dimensions={0} | all-to-all | bytes 1572864 | tf_op jit(solution)/shard_map/cond/branch_1_fun/all_to_all | solution.py:292
  75.6 5.8 block_forward.9
  81.5 3.6 all-to-all-start.2
  85.2 11.1 %all-to-all-done.2 = bf16[16,8,3200]{2,1,0:T(8,128)(2,1)S(1)} async-done(((bf16[16,8,3200]{2,1,0:T(8,128)(2,1)}), bf16[16,8,3200]{2,1,0:T(8,128)(2,1)S(1)}, u32[]{:S(2)}, u32[]{:S(2)}) %all-to-all-start.2) | async-done | bytes 819232 | tf_op jit(solution)/shard_map/cond/branch_1_fun/all_to_all | solution.py:292
  97.3 4.1 collective-permute-done.4
  101.9 66.1 %collective-permute-start.5 = (bf16[8,3072]{1,0:T(8,128)(2,1)S(1)}, bf16[8,3072]{1,0:T(8,128)(2,1)S(1)}, u32[]{:S(2)}, u32[]{:S(2)}) collective-permute-start(bf16[8,3072]{1,0:T(8,128)(2,1)S(1)} %get-tuple-element.779), channel_id=1, source_target_pairs={{0,32},{16,48},{32,64},{48,80},{64,96},{80,112},{96,0},{112,16},{1... | collective-permute-start | bytes 147464 | tf_op jit(solution)/shard_map/ppermute | solution.py:435
  173.4 11.1 %conditional.10 = (bf16[8,3072]{1,0:T(8,128)(2,1)S(1)}, bf16[8,3072]{1,0:T(8,128)(2,1)S(1)}, bf16[128,3072]{1,0:T(8,128)(2,1)}, bf16[128,768]{1,0:T(8,128)(2,1)}...) conditional(s32[]{:T(128)} %convert_element_type.81, ...), branch_computations={%region_6.7_spmd, %region_7.8_spmd} | conditional | flops 4227858432 | bytes 78053824 | solution.py:442
  184.5 176.3 %collective-permute-start.7 = (bf16[8,3072]{1,0:T(8,128)(2,1)S(1)}, bf16[8,3072]{1,0:T(8,128)(2,1)S(1)}, u32[]{:S(2)}, u32[]{:S(2)}) collective-permute-start(bf16[8,3072]{1,0:T(8,128)(2,1)S(1)} %get-tuple-element.807), channel_id=1, source_target_pairs={{32,0},{48,16},{64,32},{80,48},{96,64},{112,80},{0,96},{16,112},{3... | collective-permute-start | bytes 147464 | tf_op jit(solution)/shard_map/ppermute | solution.py:446
  366.1 5.8 conditional.12
  371.9 71.1 %collective-permute-start.9 = (bf16[8,3072]{1,0:T(8,128)(2,1)S(1)}, bf16[8,3072]{1,0:T(8,128)(2,1)S(1)}, u32[]{:S(2)}, u32[]{:S(2)}) collective-permute-start(bf16[8,3072]{1,0:T(8,128)(2,1)S(1)} %get-tuple-element.841), channel_id=1, source_target_pairs={{32,0},{48,16},{64,32},{80,48},{96,64},{112,80},{0,96},{16,112},{3... | collective-permute-start | bytes 147464 | tf_op jit(solution)/shard_map/ppermute | solution.py:446
  444.6 71.7 %collective-permute-done.9 = bf16[8,3072]{1,0:T(8,128)(2,1)S(1)} collective-permute-done((bf16[8,3072]{1,0:T(8,128)(2,1)S(1)}, bf16[8,3072]{1,0:T(8,128)(2,1)S(1)}, u32[]{:S(2)}, u32[]{:S(2)}) %collective-permute-start.9) | collective-permute-done | bytes 49184 | tf_op jit(solution)/shard_map/ppermute | solution.py:446
  516.3 57.1 %conditional.13 = ((bf16[128,3072]{1,0:T(8,128)(2,1)}, bf16[128,16]{1,0:T(8,128)(2,1)}, f32[16,768]{1,0:T(8,128)S(1)}, f32[16,768]{1,0:T(8,128)S(1)}, bf16[128,3...) conditional(s32[]{:T(128)} %convert_element_type.84, ...), branch_computations={%region_12.13_spmd, %region_13.14_spmd} | conditional | flops 1811939328 | bytes 50331844 | solution.py:447
  516.4 13.7 %all_to_all.143 = bf16[16,8,3072]{2,1,0:T(8,128)(2,1)S(1)} all-to-all(bf16[16,8,3072]{2,1,0:T(8,128)(2,1)S(1)} %bitcast.164), channel_id=1, replica_groups=mesh['segment'=8,'tp'=16] {'tp'}, dimensions={0} | all-to-all | bytes 1572864 | tf_op jit(solution)/shard_map/cond/branch_1_fun/all_to_all | solution.py:292
  530.1 9.1 %block_backward.14 = (bf16[128,16]{1,0:T(8,128)(2,1)}, f32[16,768]{1,0:T(8,128)S(1)}, f32[16,768]{1,0:T(8,128)}, bf16[128,3072]{1,0:T(8,128)(2,1)S(1)}) custom-call(s32[1]{0:T(128)} %get-tuple-element.644.own_ref, bf16[128,3072]{1,0:T(8,128)(2,1)S(1)} %bitcast.241, f32[128,768]{1,0:T(8,128)} %get-tuple-element.647.slope_ref, ...), custom_call_target="tpu_custom_call" | custom-call | flops 1207959552 | bytes 9437184 | tf_op jit(solution)/shard_map/cond/branch_1_fun/block_backward/pallas_call | solution.py:211
  539.1 13.0 %all_to_all.144 = bf16[16,8,3072]{2,1,0:T(8,128)(2,1)S(1)} all-to-all(bf16[16,8,3072]{2,1,0:T(8,128)(2,1)S(1)} %bitcast.177), channel_id=1, replica_groups=mesh['segment'=8,'tp'=16] {'tp'}, dimensions={0} | all-to-all | bytes 1572864 | tf_op jit(solution)/shard_map/cond/branch_1_fun/all_to_all | solution.py:292
  553.8 13.8 %all_to_all.145 = bf16[16,8,3072]{2,1,0:T(8,128)(2,1)} all-to-all(bf16[16,8,3072]{2,1,0:T(8,128)(2,1)S(1)} %bitcast.184), channel_id=1, replica_groups=mesh['segment'=8,'tp'=16] {'tp'}, dimensions={0} | all-to-all | bytes 1572864 | tf_op jit(solution)/shard_map/cond/branch_1_fun/all_to_all | solution.py:292
  567.7 5.6 block_backward.15
  575.2 10.2 %all_to_all.146 = bf16[16,4,16,128]{3,2,1,0:T(8,128)(2,1)S(1)} all-to-all(bf16[16,4,16,128]{3,2,1,0:T(8,128)(2,1)S(1)} %broadcast_in_dim.106), channel_id=1, replica_groups=mesh['segment'=8,'tp'=16] {'tp'}, dimensions={0} | all-to-all | bytes 524288 | tf_op jit(solution)/shard_map/all_to_all | solution.py:457
  591.0 47.4 %collective-permute-start.10 = (f32[16,7680]{1,0:T(8,128)S(1)}, f32[16,7680]{1,0:T(8,128)S(1)}, u32[]{:S(2)}, u32[]{:S(2)}) collective-permute-start(f32[16,7680]{1,0:T(8,128)S(1)} %get-tuple-element.859), channel_id=1, source_target_pairs={{0,16},{16,0},{32,48},{48,32},{64,80},{80,64},{96,112},{112,96},{1... | collective-permute-start | bytes 1474568 | tf_op jit(solution)/shard_map/ppermute | solution.py:469
  (100 shorter events, 41.6 us)
Async XLA Ops:
  7.9 15.7 %collective-permute-start.3 = (bf16[16,7680]{1,0:T(8,128)(2,1)S(1)}, bf16[16,7680]{1,0:T(8,128)(2,1)S(1)}, u32[]{:S(2)}, u32[]{:S(2)}) collective-permute-start(bf16[16,7680]{1,0:T(8,128)(2,1)S(1)} %pad_maximum_fusion.3), channel_id=1, source_target_pairs={{0,16},{16,0},{32,48},{48,32},{64,80},{80,64},{96,112},{112,96},{1... | collective-permute-start | bytes 737288 | tf_op jit(solution)/shard_map/ppermute | solution.py:339
  10.5 4.2 collective-permute-start
  10.6 26.5 %collective-permute-start.1 = (bf16[3072,768]{1,0:T(8,128)(2,1)}, bf16[3072,768]{1,0:T(8,128)(2,1)}, u32[]{:S(2)}, u32[]{:S(2)}) collective-permute-start(bf16[3072,768]{1,0:T(8,128)(2,1)} %bitcast.187), channel_id=1, source_target_pairs={{0,16},{16,0},{32,48},{48,32},{64,80},{80,64},{96,112},{112,96},{1... | collective-permute-start | bytes 14155784 | tf_op jit(solution)/shard_map/ppermute | solution.py:337
  11.1 26.0 %collective-permute-start.2 = (bf16[768,3072]{1,0:T(8,128)(2,1)}, bf16[768,3072]{1,0:T(8,128)(2,1)}, u32[]{:S(2)}, u32[]{:S(2)}) collective-permute-start(bf16[768,3072]{1,0:T(8,128)(2,1)} %bitcast.209), channel_id=1, source_target_pairs={{0,16},{16,0},{32,48},{48,32},{64,80},{80,64},{96,112},{112,96},{1... | collective-permute-start | bytes 14155784 | tf_op jit(solution)/shard_map/ppermute | solution.py:338
  15.8 21.3 %all-to-all-start.28 = ((bf16[16,8,3072]{2,1,0:T(8,128)(2,1)}), bf16[16,8,3072]{2,1,0:T(8,128)(2,1)S(1)}, u32[]{:S(2)}, u32[]{:S(2)}) async-start(bf16[16,8,3072]{2,1,0:T(8,128)(2,1)} %bitcast.64), calls=%async_computation.28 | async-start | bytes 1572864 | tf_op jit(solution)/shard_map/all_to_all | solution.py:292
  37.1 38.5 %slice-start = ((s8[4718592]{0:T(1024)(128)(4,1)}), s8[4194304]{0:T(1024)(128)(4,1)S(1)}, s32[]{:S(2)}) async-start(s8[4718592]{0:T(1024)(128)(4,1)} %bitcast.195), calls=%async_computation.30 | async-start | bytes 8388608 | tf_op jit(solution)/shard_map/cond
  37.1 38.5 %slice-start.14 = ((s8[4718592]{0:T(1024)(128)(4,1)}), s8[4194304]{0:T(1024)(128)(4,1)S(1)}, s32[]{:S(2)}) async-start(s8[4718592]{0:T(1024)(128)(4,1)} %bitcast.217), calls=%async_computation.44 | async-start | bytes 8388608 | tf_op jit(solution)/shard_map/cond
  37.1 38.5 %slice-start.1 = ((s8[4718592]{0:T(1024)(128)(4,1)}), s8[524288]{0:T(1024)(128)(4,1)S(1)}, s32[]{:S(2)}) async-start(s8[4718592]{0:T(1024)(128)(4,1)} %bitcast.195), calls=%async_computation.31 | async-start | bytes 1048576 | tf_op jit(solution)/shard_map/cond
  37.1 38.5 %slice-start.15 = ((s8[4718592]{0:T(1024)(128)(4,1)}), s8[524288]{0:T(1024)(128)(4,1)S(1)}, s32[]{:S(2)}) async-start(s8[4718592]{0:T(1024)(128)(4,1)} %bitcast.217), calls=%async_computation.45 | async-start | bytes 1048576 | tf_op jit(solution)/shard_map/cond
  81.5 14.8 %all-to-all-start.2 = ((bf16[16,8,3200]{2,1,0:T(8,128)(2,1)}), bf16[16,8,3200]{2,1,0:T(8,128)(2,1)S(1)}, u32[]{:S(2)}, u32[]{:S(2)}) async-start(bf16[16,8,3200]{2,1,0:T(8,128)(2,1)} %bitcast.4), calls=%async_computation.2 | async-start | bytes 1638400 | tf_op jit(solution)/shard_map/cond/branch_1_fun/all_to_all | solution.py:292
  97.2 4.2 collective-permute-start.4
  101.9 67.3 %collective-permute-start.5 = (bf16[8,3072]{1,0:T(8,128)(2,1)S(1)}, bf16[8,3072]{1,0:T(8,128)(2,1)S(1)}, u32[]{:S(2)}, u32[]{:S(2)}) collective-permute-start(bf16[8,3072]{1,0:T(8,128)(2,1)S(1)} %get-tuple-element.779), channel_id=1, source_target_pairs={{0,32},{16,48},{32,64},{48,80},{64,96},{80,112},{96,0},{112,16},{1... | collective-permute-start | bytes 147464 | tf_op jit(solution)/shard_map/ppermute | solution.py:435
  169.2 4.2 collective-permute-start.6
  184.5 177.5 %copy-start.5 = (bf16[128,3072]{1,0:T(8,128)(2,1)}, bf16[128,3072]{1,0:T(8,128)(2,1)S(1)}, u32[]{:S(2)}) copy-start(bf16[128,3072]{1,0:T(8,128)(2,1)S(1)} %get-tuple-element.812) | copy-start | bytes 2359300
  184.5 177.5 %collective-permute-start.7 = (bf16[8,3072]{1,0:T(8,128)(2,1)S(1)}, bf16[8,3072]{1,0:T(8,128)(2,1)S(1)}, u32[]{:S(2)}, u32[]{:S(2)}) collective-permute-start(bf16[8,3072]{1,0:T(8,128)(2,1)S(1)} %get-tuple-element.807), channel_id=1, source_target_pairs={{32,0},{48,16},{64,32},{80,48},{96,64},{112,80},{0,96},{16,112},{3... | collective-permute-start | bytes 147464 | tf_op jit(solution)/shard_map/ppermute | solution.py:446
  362.0 4.2 collective-permute-start.8
  371.9 144.4 %collective-permute-start.9 = (bf16[8,3072]{1,0:T(8,128)(2,1)S(1)}, bf16[8,3072]{1,0:T(8,128)(2,1)S(1)}, u32[]{:S(2)}, u32[]{:S(2)}) collective-permute-start(bf16[8,3072]{1,0:T(8,128)(2,1)S(1)} %get-tuple-element.841), channel_id=1, source_target_pairs={{32,0},{48,16},{64,32},{80,48},{96,64},{112,80},{0,96},{16,112},{3... | collective-permute-start | bytes 147464 | tf_op jit(solution)/shard_map/ppermute | solution.py:446
  516.3 69.2 %copy-start.4 = (bf16[128,3072]{1,0:T(8,128)(2,1)S(1)}, bf16[128,3072]{1,0:T(8,128)(2,1)}, u32[]{:S(2)}) copy-start(bf16[128,3072]{1,0:T(8,128)(2,1)} %get-tuple-element.844) | copy-start | bytes 2359300
  530.0 43.3 %copy-start.8 = (bf16[16,8,3072]{2,1,0:T(8,128)(2,1)}, bf16[16,8,3072]{2,1,0:T(8,128)(2,1)S(1)}, u32[]{:S(2)}) copy-start(bf16[16,8,3072]{2,1,0:T(8,128)(2,1)S(1)} %all_to_all.143) | copy-start | bytes 2359300 | tf_op jit(solution)/shard_map/cond
  530.0 37.6 %slice-start.12 = ((s8[4718592]{0:T(1024)(128)(4,1)}), s8[4194304]{0:T(1024)(128)(4,1)S(1)}, s32[]{:S(2)}) async-start(s8[4718592]{0:T(1024)(128)(4,1)} %bitcast.207), calls=%async_computation.42 | async-start | bytes 8388608 | tf_op jit(solution)/shard_map/cond
  530.0 37.6 %slice-start.26 = ((s8[4718592]{0:T(1024)(128)(4,1)}), s8[4194304]{0:T(1024)(128)(4,1)S(1)}, s32[]{:S(2)}) async-start(s8[4718592]{0:T(1024)(128)(4,1)} %bitcast.229), calls=%async_computation.56 | async-start | bytes 8388608 | tf_op jit(solution)/shard_map/cond
  530.1 37.6 %slice-start.13 = ((s8[4718592]{0:T(1024)(128)(4,1)}), s8[524288]{0:T(1024)(128)(4,1)S(1)}, s32[]{:S(2)}) async-start(s8[4718592]{0:T(1024)(128)(4,1)} %bitcast.207), calls=%async_computation.43 | async-start | bytes 1048576 | tf_op jit(solution)/shard_map/cond
  530.1 37.6 %slice-start.27 = ((s8[4718592]{0:T(1024)(128)(4,1)}), s8[524288]{0:T(1024)(128)(4,1)S(1)}, s32[]{:S(2)}) async-start(s8[4718592]{0:T(1024)(128)(4,1)} %bitcast.229), calls=%async_computation.57 | async-start | bytes 1048576 | tf_op jit(solution)/shard_map/cond
  591.0 50.0 %collective-permute-start.10 = (f32[16,7680]{1,0:T(8,128)S(1)}, f32[16,7680]{1,0:T(8,128)S(1)}, u32[]{:S(2)}, u32[]{:S(2)}) collective-permute-start(f32[16,7680]{1,0:T(8,128)S(1)} %get-tuple-element.859), channel_id=1, source_target_pairs={{0,16},{16,0},{32,48},{48,32},{64,80},{80,64},{96,112},{112,96},{1... | collective-permute-start | bytes 1474568 | tf_op jit(solution)/shard_map/ppermute | solution.py:469
  (2 other events, 20.8 us)

commit v3 on v2

v3 whole, which is shorter than its diff:
```python
import functools
import math

import jax
import jax.numpy as jnp
from jax import lax
from jax.experimental import pallas as pl
from jax.experimental.pallas import tpu as pltpu
from jax.sharding import PartitionSpec as P

EPS = 1e-06
ROOT_TWO_PI = math.sqrt(2.0 / math.pi)
F32 = jnp.float32
BF16 = jnp.bfloat16
PAD = 128
CUTS = 2
PAIR = 16
VMEM = pl.BlockSpec(memory_space=pltpu.VMEM)
HBM = pl.BlockSpec(memory_space=pltpu.HBM)
SMEM = pl.BlockSpec(memory_space=pltpu.SMEM)
PARAMS = pltpu.CompilerParams(vmem_limit_bytes=16 * 1024 * 1024)


def shape_of(*shape, dtype=BF16):
    return jax.ShapeDtypeStruct(shape, dtype)


def gelu_and_slope(values):
    inner = ROOT_TWO_PI * (values + 0.044715 * values * values * values)
    tangent = jnp.tanh(inner)
    half = 0.5 * (1.0 + tangent)
    slope = half + 0.5 * values * (1.0 - tangent * tangent) * ROOT_TWO_PI * (
        1.0 + 3.0 * 0.044715 * values * values
    )
    return values * half, slope


def rms_stats(wide):
    inv_rms = lax.rsqrt(jnp.mean(wide * wide, axis=-1, keepdims=True) + EPS)
    return wide * inv_rms, inv_rms


def dot(a, b, a_dim, b_dim):
    return lax.dot_general(a, b, (((a_dim,), (b_dim,)), ((), ())), preferred_element_type=F32)


def fetch(own, ours, theirs, buf, sem):
    @pl.when(own)
    def _():
        pltpu.make_async_copy(ours, buf, sem).start()

    @pl.when(jnp.logical_not(own))
    def _():
        pltpu.make_async_copy(theirs, buf, sem).start()


def cut(c, size):
    return pl.ds(c * (size // CUTS), size // CUTS)


def keep(buf, out, sem):
    copy = pltpu.make_async_copy(buf, out, sem)
    copy.start()
    return copy


def in_hbm(*arrays):
    return [pltpu.with_memory_space_constraint(a, pltpu.HBM) for a in arrays]


def order_kernel(flag_ref, wi_own, wi_other, wo_own, wo_other, *refs):
    outs, (wi_buf, wo_buf, in_sems, out_sems) = refs[:2], refs[2:]
    sources = ((wi_own, wi_other, wi_buf), (wo_own, wo_other, wo_buf))

    @pl.when(flag_ref[0] == 1)
    def _():
        for k, (ours, theirs, buf) in enumerate(sources):
            fetch(flag_ref[1] == 1, ours, theirs, buf, in_sems.at[k])
        for k, (ours, theirs, buf) in enumerate(sources):
            pltpu.make_async_copy(ours, buf, in_sems.at[k]).wait()
            pltpu.make_async_copy(buf, outs[k], out_sems.at[k]).start()
        for k, (ours, theirs, buf) in enumerate(sources):
            pltpu.make_async_copy(buf, outs[k], out_sems.at[k]).wait()


def second_weights(flag, weights):
    out = [shape_of(*weights[0].shape), shape_of(*weights[2].shape)]
    return pl.pallas_call(
        order_kernel,
        out_shape=out,
        in_specs=[SMEM] + [HBM] * 4,
        out_specs=[HBM] * 2,
        scratch_shapes=[
            pltpu.VMEM(out[0].shape, BF16),
            pltpu.VMEM(out[1].shape, BF16),
            pltpu.SemaphoreType.DMA((2,)),
            pltpu.SemaphoreType.DMA((2,)),
        ],
        compiler_params=PARAMS,
        name="second_weights",
    )(flag, *in_hbm(*weights))


def forward_kernel(*refs, last, streamed):
    if streamed:
        own_ref, u_ref, wi_own, wi_other, wo_own, wo_other, *refs = refs
        wi_ref, wo_ref, w_sems = refs[-3:]
        refs = refs[:-3]
        width = u_ref.shape[1]
        for c in range(CUTS):
            at = (cut(c, width),)
            fetch(own_ref[0] == 1, wi_own.at[at], wi_other.at[at], wi_ref.at[at], w_sems.at[c])
        for c in range(CUTS):
            at = (slice(None), cut(c, width))
            fetch(
                own_ref[0] == 1, wo_own.at[at], wo_other.at[at], wo_ref.at[at], w_sems.at[CUTS + c]
            )
    else:
        u_ref, wi_ref, *refs = refs
        wo_ref, refs = (None, refs) if last else (refs[0], refs[1:])

    def arrived(source, held, n, at):
        if streamed:
            pltpu.make_async_copy(source.at[at], held.at[at], w_sems.at[n]).wait()

    wi_own, wo_own = (wi_own, wo_own) if streamed else (None, None)
    di_ref, ui_ref, do_ref, act_out, slope_out, low_in_out, low_out, u_out, *rest = refs
    sent_ref, rest = (None, rest) if last else (rest[0], rest[1:])
    act_ref, slope_ref, low_in_ref, low_ref, out_sems = rest
    width, rank = u_ref.shape[1], di_ref.shape[0]
    low_in = dot(u_ref[...], di_ref[...], 1, 1).astype(BF16)
    low_in_ref[...] = low_in
    copies = [keep(u_ref, u_out, out_sems.at[4]), keep(low_in_ref, low_in_out, out_sems.at[0])]
    pre = dot(low_in, ui_ref[...], 1, 0)
    for c in range(CUTS if streamed else 1):
        at = cut(c, width) if streamed else slice(None)
        arrived(wi_own, wi_ref, c, (at,))
        pre = pre + dot(u_ref[:, at], wi_ref[at], 1, 0)
    act, slope = gelu_and_slope(pre)
    act = act.astype(BF16)
    act_ref[...] = act
    slope_ref[...] = slope
    copies.append(keep(act_ref, act_out, out_sems.at[1]))
    copies.append(keep(slope_ref, slope_out, out_sems.at[2]))
    low_ref[...] = dot(do_ref[...], act, 1, 1).astype(BF16)
    copies.append(keep(low_ref, low_out, out_sems.at[3]))
    if not last:
        sent_ref[:, width:] = jnp.zeros((sent_ref.shape[0], PAD), BF16)
        sent_ref[:, width : width + rank] = dot(act, do_ref[...], 1, 1).astype(BF16)
        for c in range(CUTS):
            at = cut(c, width)
            arrived(wo_own, wo_ref, CUTS + c, (slice(None), at))
            sent_ref[:, at] = dot(act, wo_ref[:, at], 1, 0).astype(BF16)
    for copy in copies:
        copy.wait()


def backward_kernel(*refs, first, streamed):
    if streamed:
        wi_ref, wo_ref, w_sems = refs[-3:]
        g_ref, slope_in, act_in, low_in_in, wo_hbm, wi_hbm, *refs = refs[:-3]
        width = g_ref.shape[1]
        for c in range(CUTS):
            at = (cut(c, width),)
            pltpu.make_async_copy(wo_hbm.at[at], wo_ref.at[at], w_sems.at[c]).start()
        for c in range(CUTS):
            at = (slice(None), cut(c, width))
            pltpu.make_async_copy(wi_hbm.at[at], wi_ref.at[at], w_sems.at[CUTS + c]).start()
    else:
        wi_hbm = wo_hbm = None
        g_ref, slope_in, act_in, low_in_in, wo_ref, *refs = refs
        wi_ref, refs = (None, refs) if first else (refs[0], refs[1:])

    def arrived(source, held, n, at):
        if streamed:
            pltpu.make_async_copy(source.at[at], held.at[at], w_sems.at[n]).wait()

    di_ref, ui_ref, do_ref, uo_ref, g_low_out_ref, grad_ui_out, grad_do_out, g_out, *rest = refs
    part_ref, rest = (None, rest) if first else (rest[0], rest[1:])
    act_ref, slope_ref, low_in_ref, g_low_ref, grad_ui, grad_do, io_sems = rest
    width = g_ref.shape[1]
    slope_copy = keep(slope_in, slope_ref, io_sems.at[1])
    low_in_copy = keep(low_in_in, low_in_ref, io_sems.at[2])
    act_copy = keep(act_in, act_ref, io_sems.at[0])
    g_low_out = dot(g_ref[...], uo_ref[...], 1, 1).astype(BF16)
    g_act = dot(g_low_out, do_ref[...], 1, 0)
    for c in range(CUTS if streamed else 1):
        at = cut(c, width) if streamed else slice(None)
        arrived(wo_hbm, wo_ref, c, (at,))
        g_act = g_act + dot(g_ref[:, at], wo_ref[at], 1, 0)
    slope_copy.wait()
    g_pre = (g_act * slope_ref[...]).astype(BF16)
    g_low_ref[...] = dot(ui_ref[...], g_pre, 1, 1).astype(BF16)
    copies = [keep(g_ref, g_out, io_sems.at[6]), keep(g_low_ref, g_low_out_ref, io_sems.at[3])]
    low_in_copy.wait()
    grad_ui[...] = dot(low_in_ref[...], g_pre, 0, 0)
    copies.append(keep(grad_ui, grad_ui_out, io_sems.at[4]))
    act_copy.wait()
    grad_do[...] = dot(g_low_out, act_ref[...], 0, 0)
    copies.append(keep(grad_do, grad_do_out, io_sems.at[5]))
    if not first:
        g_low_in = dot(g_pre, ui_ref[...], 1, 1).astype(BF16)
        for c in range(CUTS):
            at = (slice(None), cut(c, width))
            arrived(wi_hbm, wi_ref, CUTS + c, at)
            part = dot(g_pre, wi_ref[at], 1, 0) + dot(g_low_in, di_ref[at], 1, 0)
            part_ref[at] = part.astype(BF16)
    for copy in copies:
        copy.wait()


def block_cost(rows, width, cols, matmuls):
    return pl.CostEstimate(
        flops=2 * matmuls * rows * width * cols,
        bytes_accessed=2 * matmuls * width * cols,
        transcendentals=rows * cols,
    )


def in_vmem(*arrays):
    return [pltpu.with_memory_space_constraint(a, pltpu.VMEM) for a in arrays]


def block_forward(u, weights, low, own=None):
    rows, width = u.shape
    streamed, last = own is not None, len(weights) == 1
    rank, cols = low[1].shape
    kept = [((rows, cols), BF16), ((rows, cols), F32), ((rows, rank), BF16), ((rank, rows), BF16)]
    out = [shape_of(*s, dtype=t) for s, t in kept] + [shape_of(rows, width)]
    out += [] if last else [shape_of(rows, width + PAD)]
    stream_scratch = [
        pltpu.VMEM((width, cols), BF16),
        pltpu.VMEM((cols, width), BF16),
        pltpu.SemaphoreType.DMA((2 * CUTS,)),
    ]
    first_specs = [SMEM, VMEM] + [HBM] * 4 if streamed else [VMEM] * (1 + len(weights))
    return pl.pallas_call(
        functools.partial(forward_kernel, last=last, streamed=streamed),
        out_shape=out,
        in_specs=first_specs + [VMEM] * 3,
        out_specs=[HBM] * (len(kept) + 1) + ([] if last else [VMEM]),
        scratch_shapes=[
            *(pltpu.VMEM(s, t) for s, t in kept),
            pltpu.SemaphoreType.DMA((len(kept) + 1,)),
            *(stream_scratch if streamed else []),
        ],
        compiler_params=PARAMS,
        cost_estimate=block_cost(rows, width, cols, 1 if last else 2),
        name="block_forward",
    )(*((own, u, *in_hbm(*weights)) if streamed else (u, *in_vmem(*weights))), *low[:3])


def block_backward(g, acts, weights, low, streamed):
    rows, width = g.shape
    first = len(weights) == 1
    rank, cols = low[1].shape
    kept = [((rank, rows), BF16), ((rank, cols), F32), ((rank, cols), F32)]
    out = [shape_of(*s, dtype=t) for s, t in kept] + [shape_of(rows, width)]
    out += [] if first else [shape_of(rows, width)]
    act, slope, low_in = acts
    stream_scratch = [
        pltpu.VMEM((cols, width), BF16),
        pltpu.VMEM((width, cols), BF16),
        pltpu.SemaphoreType.DMA((2 * CUTS,)),
    ]
    return pl.pallas_call(
        functools.partial(backward_kernel, first=first, streamed=streamed),
        out_shape=out,
        in_specs=[VMEM] + [HBM] * 3 + [HBM if streamed else VMEM] * len(weights) + [VMEM] * 4,
        out_specs=[HBM] * (len(kept) + 1) + ([] if first else [VMEM]),
        scratch_shapes=[
            pltpu.VMEM((rows, cols), BF16),
            pltpu.VMEM((rows, cols), F32),
            pltpu.VMEM((rows, rank), BF16),
            *(pltpu.VMEM(s, t) for s, t in kept),
            pltpu.SemaphoreType.DMA((7,)),
            *(stream_scratch if streamed else []),
        ],
        compiler_params=PARAMS,
        cost_estimate=block_cost(rows, width, cols, len(weights)),
        name="block_backward",
    )(g, slope, act, low_in, *(in_hbm if streamed else in_vmem)(*weights), *low)


def turn_kernel(flag_ref, *refs):
    narrow_buf, wide_buf, in_sems, out_sems = refs[-4:]
    outs, sources = refs[-8:-4], refs[:4]
    step = narrow_buf.shape[1]

    def turn(own, ours, theirs, target, in_buf, out_buf, by_rows):
        count = ours.shape[0 if by_rows else 1] // step

        def cut_of(ref, c, rows):
            at = pl.ds(pl.multiple_of(c * step, step), step)
            return ref.at[at] if rows else ref.at[:, at]

        def come(c):
            slot = lax.rem(c, 2)
            source, other = (cut_of(ref, c, by_rows) for ref in (ours, theirs))
            fetch(own, source, other, in_buf.at[slot], in_sems.at[slot])

        def going(c, slot):
            target_cut = cut_of(target, c, not by_rows)
            return pltpu.make_async_copy(out_buf.at[slot], target_cut, out_sems.at[slot])

        come(0)

        def body(c, carry):
            slot = lax.rem(c, 2)

            @pl.when(c + 1 < count)
            def _():
                come(c + 1)

            source = cut_of(ours, c, by_rows)
            pltpu.make_async_copy(source, in_buf.at[slot], in_sems.at[slot]).wait()

            @pl.when(c >= 2)
            def _():
                going(c - 2, slot).wait()

            out_buf[slot] = in_buf[slot].T
            going(c, slot).start()
            return carry

        lax.fori_loop(0, count, body, 0)
        going(count - 2, count % 2).wait()
        going(count - 1, 1 - count % 2).wait()

    @pl.when(flag_ref[0] == 1)
    def _():
        for i in range(2):
            own = flag_ref[1] == i
            turn(own, *sources[:2], outs[2 * i], narrow_buf, wide_buf, True)
            turn(own, *sources[2:], outs[2 * i + 1], wide_buf, narrow_buf, False)


def turned_weights(flag, weights, held):
    width, cols = weights[0].shape
    step = 384
    out = pl.pallas_call(
        turn_kernel,
        out_shape=[shape_of(cols, width), shape_of(width, cols)] * 2,
        in_specs=[SMEM] + [HBM] * (4 + len(held)),
        out_specs=[HBM] * 4,
        scratch_shapes=[
            pltpu.VMEM((2, step, cols), BF16),
            pltpu.VMEM((2, cols, step), BF16),
            pltpu.SemaphoreType.DMA((2,)),
            pltpu.SemaphoreType.DMA((2,)),
        ],
        input_output_aliases={5 + k: k for k in range(len(held))},
        compiler_params=PARAMS,
        name="turned_weights",
    )(flag, *in_hbm(*weights), *held)
    return tuple(out)


def summed(got_ref, own_rows, at):
    total = None
    for k in range(0, got_ref.shape[0], PAIR):
        part = got_ref[k : k + PAIR, at].astype(F32)
        part = part.reshape(PAIR // own_rows, own_rows, part.shape[1]).sum(0)
        total = part if total is None else total + part
    return total


def spread(out_ref, rows):
    pair = jnp.concatenate([rows] * (PAIR // rows.shape[0]), axis=0).astype(BF16)
    for k in range(0, out_ref.shape[0], PAIR):
        out_ref[k : k + PAIR] = pair


def modulated(wide, mod_ref):
    return rms_stats(wide)[0] * (1.0 + mod_ref[1:2]) + mod_ref[0:1]


def first_rows_kernel(
    ids_ref,
    counts_ref,
    x_ref,
    e_ref,
    mod_own,
    mod_other,
    out_ref,
    x_out,
    e_out,
    mask_out,
    mod_0,
    mod_1,
    x_in,
    e_in,
    mod_in,
    sems,
):
    copies = [
        keep(source, held, sems.at[k])
        for k, (source, held) in enumerate(((x_ref, x_in), (e_ref, e_in), (mod_own, mod_in)))
    ]
    for copy in copies:
        copy.wait()
    at_start, core, tp_pos = ids_ref[0], ids_ref[1], ids_ref[2]
    own_rows = x_ref.shape[1]
    row = tp_pos * own_rows + lax.broadcasted_iota(jnp.int32, (own_rows, 1), 0)
    mask = (row < counts_ref[core]).astype(F32)
    mask_out[...] = mask
    ours, theirs = mod_in[core], mod_other[core]
    mod_0[...] = jnp.where(core == 0, ours, theirs)
    mod_1[...] = jnp.where(core == 0, theirs, ours)
    x = (x_in[core].astype(F32) * mask).astype(BF16)
    e = (e_in[core].astype(F32) * mask).astype(BF16)
    x_out[...] = x
    e_out[...] = e
    u = modulated(x.astype(F32), mod_0)
    g = mod_1[2:3] * e.astype(F32)
    spread(out_ref, jnp.where(at_start == 1, u, g))


def pack_kernel(ids_ref, jobs_ref, *refs):
    sources, ours, theirs, sems = refs[:-3], refs[-3], refs[-2], refs[-1]
    core = ids_ref[1]
    copies = []
    for n, (job, out) in enumerate(((jobs_ref[core], ours), (jobs_ref[1 - core], theirs))):
        start = 0
        for k, source in enumerate(sources):
            at = pl.ds(start, source.shape[2])
            copies.append(keep(source.at[job], out.at[:, at], sems.at[n * len(sources) + k]))
            start += source.shape[2]
    for copy in copies:
        copy.wait()


def rows_in_kernel(x_ref, mod_ref, out_ref):
    spread(out_ref, modulated(x_ref[...].astype(F32), mod_ref))


def gate_rows_kernel(e_ref, mod_ref, out_ref):
    spread(out_ref, mod_ref[2:3] * e_ref[...].astype(F32))


def forward_rows_kernel(got_ref, x_ref, mask_ref, mod_ref, uo_ref, next_ref, x_out, *outs):
    own_rows, width = x_ref.shape
    rank = uo_ref.shape[0]
    low = summed(got_ref, own_rows, pl.ds(width, PAD)).astype(BF16)[:, :rank]
    branch = summed(got_ref, own_rows, pl.ds(0, width)) + dot(low, uo_ref[...], 1, 0)
    x = x_ref[...].astype(F32) + mod_ref[2:3] * branch * mask_ref[...]
    x = x.astype(BF16)
    x_out[...] = x
    if outs:
        x_saved, spread_out = outs
        x_saved[...] = x_ref[...]
        spread(spread_out, modulated(x.astype(F32), next_ref))


def backward_rows_kernel(got_ref, e_ref, x_ref, mod_ref, next_ref, e_out, *spread_out):
    own_rows, width = x_ref.shape
    normed, inv_rms = rms_stats(x_ref[...].astype(F32))
    q = summed(got_ref, own_rows, pl.ds(0, width)) * (1.0 + mod_ref[1:2])
    mean = jnp.mean(q * normed, axis=-1, keepdims=True)
    e = (e_ref[...].astype(F32) + inv_rms * (q - normed * mean)).astype(BF16)
    e_out[...] = e
    for out_ref in spread_out:
        spread(out_ref, next_ref[2:3] * e.astype(F32))


def narrow_kernel(*refs):
    parts, out_ref = refs[:-1], refs[-1]
    rows = jnp.concatenate([part[...].astype(F32) for part in parts], axis=0).astype(BF16)
    for k in range(0, out_ref.shape[0], rows.shape[0]):
        out_ref[k : k + rows.shape[0]] = rows


def gradients_kernel(ids_ref, got_ref, *refs):
    per_block, (ours, theirs) = refs[:8], refs[8:]
    rank, cols = per_block[2].shape
    width = per_block[0].shape[1]
    deep = 4 * rank
    total = None
    for k in range(0, got_ref.shape[0], deep):
        part = got_ref[k : k + deep].astype(F32)
        total = part if total is None else total + part
    for i in range(2):
        g_ref, u_ref, ui_ref, do_ref = per_block[4 * i : 4 * i + 4]
        low_out = total[i * rank : (i + 1) * rank].astype(BF16)
        g_low = total[(2 + i) * rank : (3 + i) * rank]
        high = g_low.astype(BF16)
        rest = (g_low - high.astype(F32)).astype(BF16)
        grads = (
            dot(high, u_ref[...], 1, 0) + dot(rest, u_ref[...], 1, 0),
            ui_ref[...],
            do_ref[...],
            dot(low_out, g_ref[...], 1, 0),
        )

        def put(out, grads=grads):
            start = 0
            for grad in grads:
                out[:, start : start + grad.shape[1]] = grad
                start += grad.shape[1]

        pl.when(ids_ref[1] == i)(functools.partial(put, ours))
        pl.when(ids_ref[1] != i)(functools.partial(put, theirs))


def by_job_kernel(ids_ref, jobs_ref, ours, theirs, di_ref, ui_ref, do_ref, uo_ref):
    core, tp_pos = ids_ref[1], ids_ref[2]
    owners, _, width = di_ref.shape
    cols = ui_ref.shape[2]
    for out in (di_ref, ui_ref, do_ref, uo_ref):
        out[...] = jnp.zeros(out.shape, F32)
    for job, grads in ((jobs_ref[core], ours), (jobs_ref[1 - core], theirs)):
        ui_ref[job] += grads[:, width : width + cols]
        do_ref[job] += grads[:, width + cols : width + 2 * cols]
        place = job - tp_pos * owners

        def owned(place=place, grads=grads):
            di_ref[place] += grads[:, :width]
            uo_ref[place] += grads[:, width + 2 * cols :]

        pl.when((place >= 0) & (place < owners))(owned)


def rows_call(kernel, out, *operands, scalars=0):
    return pl.pallas_call(
        kernel,
        out_shape=out,
        in_specs=[SMEM] * scalars + [VMEM] * (len(operands) - scalars),
        out_specs=jax.tree.map(lambda _: VMEM, out),
        compiler_params=PARAMS,
        name=kernel.__name__,
    )(*operands)


def exchanged(parts, tp):
    rows, width = parts.shape
    got = lax.all_to_all(parts.reshape(tp, rows // tp, width), "tp", 0, 0)
    return got.reshape(rows, width)


def shards(
    latents,
    cotangent,
    token_counts,
    job_ids,
    modulation,
    w_in,
    w_out,
    down_in,
    up_in,
    down_out,
    up_out,
):
    tp = lax.axis_size("tp")
    segments = lax.axis_size("segment")
    planes = segments // 2
    seg = lax.axis_index("segment")
    plane, core = seg // 2, seg % 2
    tp_pos = lax.axis_index("tp")
    micro, own_rows, width = latents.shape
    cols = w_in.shape[2]
    jobs, rank = down_in.shape[1], down_in.shape[2]
    rows = own_rows * tp
    swap = [(s, s ^ 1) for s in range(segments)]
    onward = [(s, (s + 2) % segments) for s in range(segments)]
    back = [(d, s) for s, d in onward]
    last_plane = planes - 1

    ids = jnp.stack([(plane == 0).astype(jnp.int32), core, tp_pos]).astype(jnp.int32)
    full = shape_of(rows, width)
    some = shape_of(own_rows, width)
    mod = modulation[0]
    mod_other = lax.ppermute(mod, "segment", swap)
    w_first = (w_in[0], lax.ppermute(w_in[0], "segment", swap))
    w_second = (w_out[0], lax.ppermute(w_out[0], "segment", swap))

    mod_shape = shape_of(*mod.shape[1:], dtype=F32)
    sources = (latents, cotangent, mod)
    ends, x, e_last, mask, *mods = pl.pallas_call(
        first_rows_kernel,
        out_shape=[full, some, some, shape_of(own_rows, 1, dtype=F32), mod_shape, mod_shape],
        in_specs=[SMEM, SMEM, HBM, HBM, HBM, VMEM],
        out_specs=[VMEM] * 6,
        scratch_shapes=[pltpu.VMEM(a.shape, a.dtype) for a in sources]
        + [pltpu.SemaphoreType.DMA((len(sources),))],
        compiler_params=PARAMS,
        name="first_rows_kernel",
    )(
        ids,
        token_counts,
        *in_hbm(*sources),
        mod_other,
    )

    adapters = [a[0] for a in (down_in, up_in, down_out, up_out)]
    packed = shape_of(rank, sum(a.shape[2] for a in adapters))
    low_own, low_sent = pl.pallas_call(
        pack_kernel,
        out_shape=[packed, packed],
        in_specs=[SMEM, SMEM] + [HBM] * len(adapters),
        out_specs=[VMEM, VMEM],
        scratch_shapes=[pltpu.SemaphoreType.DMA((2 * len(adapters),))],
        compiler_params=PARAMS,
        cost_estimate=pl.CostEstimate(
            flops=0, bytes_accessed=4 * math.prod(packed.shape), transcendentals=0
        ),
        name="pack_kernel",
    )(ids, job_ids, *in_hbm(*adapters))
    low_other = lax.ppermute(low_sent, "segment", swap)
    cuts = (width, width + cols, width + 2 * cols)
    lows = [
        jnp.split(jnp.where(core == i, low_own, low_other), cuts, axis=1) for i in range(2)
    ]

    ends = exchanged(ends, tp)

    def turn_weights(which, held, x):
        flag = jnp.stack([which.astype(jnp.int32), core])
        turned = turned_weights(flag, (*w_first, *w_second), held)
        return lax.optimization_barrier((turned, x))

    owns = [(core == i).astype(jnp.int32).reshape(1) for i in range(2)]
    flag = jnp.stack([(plane > 0).astype(jnp.int32), core])
    turn_flag = (plane >= planes // 2).astype(jnp.int32)
    ends, flag, turn_flag = lax.optimization_barrier((ends, flag, turn_flag))
    second, x = lax.optimization_barrier((second_weights(flag, (*w_first, *w_second)), x))
    turned, x = turn_weights(turn_flag, (), x)

    def forward_plane(x, second, p):
        saved = []
        for i in range(2):
            if i:
                u = exchanged(sent, tp)
            else:
                u = ends if p == 0 else exchanged(rows_call(rows_in_kernel, full, x, mods[0]), tp)
            last = p == last_plane and i == 1
            if i == 0 or p == 0:
                done = block_forward(u, (*w_first, *w_second), lows[i], owns[i])
            else:
                done = block_forward(u, second[:1] if last else second, lows[i])
            act, slope, low_in, low_part, u, *part = done
            kept = (u, (act, slope, low_in), low_part)
            if last:
                saved.append((x, *kept))
                break
            got = exchanged(part[0], tp)
            if i == 0:
                x_next, x, sent = rows_call(
                    forward_rows_kernel,
                    [some, some, full],
                    got,
                    x,
                    mask,
                    mods[0],
                    lows[0][3],
                    mods[1],
                )
            else:
                (x_next,) = rows_call(
                    forward_rows_kernel, [some], got, x, mask, mods[1], lows[1][3], mods[1]
                )
            saved.append((x, *kept))
            x = x_next
        return x, tuple(saved)

    def backward_plane(e, saved, turned, p):
        kept = [None, None]
        for i in (1, 0):
            if i == 0:
                g = exchanged(sent, tp)
            elif p == last_plane:
                g = ends
            else:
                g = exchanged(rows_call(gate_rows_kernel, full, e, mods[1]), tp)
            x, u, acts, low_part = saved[i]
            first = p == 0 and i == 0
            w_in_t, w_out_t = turned[2 * i : 2 * i + 2]
            g_low_in, grad_ui, grad_do, g, *part = block_backward(
                g, acts, [w_out_t] if first else [w_out_t, w_in_t], lows[i], i == 1
            )
            kept[i] = (g, g_low_in, grad_ui, grad_do)
            if first:
                break
            got = exchanged(part[0], tp)
            out = [some, full] if i else [some]
            e, *sent = rows_call(backward_rows_kernel, out, got, e, x, mods[i], mods[0])
            sent = sent[0] if sent else None
        return e, tuple(kept)

    def zeros(*shape, dtype=BF16):
        return jnp.zeros(shape, dtype)

    def no_saved():
        acts = (zeros(rows, cols), zeros(rows, cols, dtype=F32), zeros(rows, rank))
        return (zeros(own_rows, width), zeros(rows, width), acts, zeros(rank, rows))

    def no_kept():
        return (
            zeros(rows, width),
            zeros(rank, rows),
            zeros(rank, cols, dtype=F32),
            zeros(rank, cols, dtype=F32),
        )

    saved = (no_saved(), no_saved())
    kept = (no_kept(), no_kept())
    for p in range(last_plane):
        x, saved = lax.cond(
            plane == p,
            lambda x, saved: forward_plane(x, second, p),
            lambda x, saved: (x, saved),
            x,
            saved,
        )
        x = lax.ppermute(x, "segment", onward)
        if p == planes // 2 - 1:
            turned, x = turn_weights(plane < planes // 2, turned, x)

    def turn(x, saved, kept):
        x, saved = forward_plane(x, second, last_plane)
        e, kept = backward_plane(e_last, saved, turned, last_plane)
        return e, saved, kept

    e, saved, kept = lax.cond(
        plane == last_plane, turn, lambda x, saved, kept: (x, saved, kept), x, saved, kept
    )
    for p in range(last_plane - 1, -1, -1):
        e = lax.ppermute(e, "segment", back)
        e, kept = lax.cond(
            plane == p,
            lambda e, saved, kept: backward_plane(e, saved, turned, p),
            lambda e, saved, kept: (e, kept),
            e,
            saved,
            kept,
        )

    narrow = (saved[0][3], saved[1][3], kept[0][1], kept[1][1])
    got = exchanged(rows_call(narrow_kernel, shape_of(tp * 4 * rank, rows), *narrow), tp)
    wide = [shape_of(*packed.shape, dtype=F32)] * 2
    per_block = [(kept[i][0], saved[i][1], kept[i][2], kept[i][3]) for i in range(2)]
    mine, sent = rows_call(
        gradients_kernel, wide, ids, got, *per_block[0], *per_block[1], scalars=1
    )
    theirs = lax.ppermute(sent, "segment", swap)
    owned = shape_of(jobs // tp, rank, width, dtype=F32)
    split = shape_of(jobs, rank, cols, dtype=F32)
    grads = rows_call(
        by_job_kernel, [owned, split, split, owned], ids, job_ids, mine, theirs, scalars=2
    )
    return tuple(grad[None] for grad in grads)


def solution(mesh):
    return jax.shard_map(
        shards,
        mesh=mesh,
        in_specs=(
            P(None, "tp", None),
            P(None, "tp", None),
            P(),
            P(),
            P("segment", None, None, None),
            P("segment", None, "tp"),
            P("segment", "tp", None),
            P("segment", None, None, None),
            P("segment", None, None, "tp"),
            P("segment", None, None, "tp"),
            P("segment", None, None, None),
        ),
        out_specs=(
            P("segment", "tp", None, None),
            P("segment", None, None, "tp"),
            P("segment", None, None, "tp"),
            P("segment", "tp", None, None),
        ),
        check_vma=False,
    )
```

time: 654 us -> 604 us (0.924)
  starting transfers between devices: 380 us -> 315 us
  Pallas kernels: 29.9 us -> 62 us
  blocking collectives: 83.6 us -> 95.3 us
  waiting for transfers between devices: 106 us -> 96.2 us
  local copies, waits for them, and re-layouts: 12.1 us -> 4.25 us
  other arithmetic: 6.85 us -> 0.27 us
    ppermute x3, starting transfers between devices: 250 us -> 205 us  [shards(): e = lax.ppermute(e, 'segment', back)]
    pallas_call x4 -> x9, Pallas kernels: 25.3 us -> 53.9 us  [the longest x2 30.8 us: turned_weights(): pl.pallas_call(turn_kernel, out_shape=[shape_of(cols, width), shape_of(wi...]
    all_to_all x5 -> x7, blocking collectives: 73.4 us -> 95.3 us  [exchanged(): got = lax.all_to_all(parts.reshape(tp, rows // tp, width), 'tp', 0, 0)]
    ppermute x3, starting transfers between devices: 68.2 us -> 55.5 us  [shards(): x = lax.ppermute(x, 'segment', onward)]
    all_to_all x2 -> x1, waiting for transfers between devices: 24.4 us -> 13.4 us  [exchanged(): got = lax.all_to_all(parts.reshape(tp, rows // tp, width), 'tp', 0, 0)]
    all_to_all x1 -> x0, blocking collectives: 10.2 us -> none  [shards(): lax.all_to_all(jnp.broadcast_to(narrow[None], (tp,) + narrow.shape), 'tp'...]
    another operation x6, loops' own time: 6.36 us -> 12.9 us  [the longest x3 7.79 us: shards(): lax.cond(plane == p, lambda x, saved: forward_plane(x, second, p), lambda...]
  transfers between devices with their start and end apart: 13 -> 12, of which waited for: 8 -> 8; matrix products, arithmetic and copies ran while one was open for 1% -> 0% of each run, Pallas kernels for 0% -> 6%
where the time goes in v3:
time: 604 us; the launch traced here: 595 us
  starting transfers between devices  315 us (52%)
  waiting for transfers between devices  96.2 us (16%)
  blocking collectives  95.3 us (16%)
  Pallas kernels  62 us (10%)
  loops' own time  20.4 us (3%)
    ppermute x3, starting transfers between devices, shards(): e = lax.ppermute(e, 'segment', back)  205 us
    all_to_all x7, blocking collectives, exchanged(): got = lax.all_to_all(parts.reshape(tp, rows // tp, width), 'tp', 0, 0)  95.3 us
    ppermute x3, waiting for transfers between devices, shards(): e = lax.ppermute(e, 'segment', back)  68.8 us
    ppermute x3, starting transfers between devices, shards(): x = lax.ppermute(x, 'segment', onward)  55.5 us
    ppermute x1, starting transfers between devices, shards(): theirs = lax.ppermute(sent, 'segment', swap)  44.8 us
    pallas_call x2, Pallas kernels, turned_weights(): pl.pallas_call(turn_kernel, out_shape=[shape_of(cols, width), shape_of(wi...  30.8 us
    all_to_all x1, waiting for transfers between devices, exchanged(): got = lax.all_to_all(parts.reshape(tp, rows // tp, width), 'tp', 0, 0)  13.4 us
  transfers between devices with their start and end apart: 12, of which 8 were waited for; matrix products, arithmetic and copies ran while one was open for 0% of the time, Pallas kernels for 6%

profile of v3, /device:TPU:1, one launch (start us, length us, event | category | flops | bytes accessed | tf_op | source)
XLA Modules:
  0.0 595.0 jit_solution(8854157292600496270)
XLA Ops:
  6.4 4.3 collective-permute-done.2.mod_other
  14.0 7.9 %all-to-all-start.28 = ((bf16[16,8,3072]{2,1,0:T(8,128)(2,1)}), bf16[16,8,3072]{2,1,0:T(8,128)(2,1)S(1)}, u32[]{:S(2)}, u32[]{:S(2)}) async-start(bf16[16,8,3072]{2,1,0:T(8,128)(2,1)} %bitcast.64), calls=%async_computation.28 | async-start | bytes 1572864 | tf_op jit(solution)/shard_map/all_to_all | solution.py:536
  21.9 13.4 %all-to-all-done.28 = bf16[16,8,3072]{2,1,0:T(8,128)(2,1)S(1)} async-done(((bf16[16,8,3072]{2,1,0:T(8,128)(2,1)}), bf16[16,8,3072]{2,1,0:T(8,128)(2,1)S(1)}, u32[]{:S(2)}, u32[]{:S(2)}) %all-to-all-start.28) | async-done | bytes 786464 | tf_op jit(solution)/shard_map/all_to_all | solution.py:536
  36.6 57.4 %conditional.7 = (bf16[8,3072]{1,0:T(8,128)(2,1)S(1)}, bf16[8,3072]{1,0:T(8,128)(2,1)}, bf16[128,3072]{1,0:T(8,128)(2,1)S(1)}, bf16[128,768]{1,0:T(8,128)(2,1)},...) conditional(s32[]{:T(128)} %convert_element_type.12, ...), branch_computations={%region_0.1_spmd, %region_1.2_spmd} | conditional | flops 2415919104 | bytes 23724136 | solution.py:707
  36.6 4.5 block_forward.8
  41.1 17.1 %all_to_all.122 = bf16[16,8,3200]{2,1,0:T(8,128)(2,1)S(1)} all-to-all(bf16[16,8,3200]{2,1,0:T(8,128)(2,1)S(1)} %bitcast.147), channel_id=1, replica_groups=mesh['segment'=8,'tp'=16] {'tp'}, dimensions={0} | all-to-all | bytes 1638400 | tf_op jit(solution)/shard_map/cond/branch_1_fun/all_to_all | solution.py:536
  59.1 14.8 %all_to_all.123 = bf16[16,8,3072]{2,1,0:T(8,128)(2,1)S(1)} all-to-all(bf16[16,8,3072]{2,1,0:T(8,128)(2,1)S(1)} %bitcast.158), channel_id=1, replica_groups=mesh['segment'=8,'tp'=16] {'tp'}, dimensions={0} | all-to-all | bytes 1572864 | tf_op jit(solution)/shard_map/cond/branch_1_fun/all_to_all | solution.py:536
  73.9 5.3 block_forward.9
  79.1 13.9 %all_to_all.124 = bf16[16,8,3200]{2,1,0:T(8,128)(2,1)S(1)} all-to-all(bf16[16,8,3200]{2,1,0:T(8,128)(2,1)S(1)} %bitcast.146), channel_id=1, replica_groups=mesh['segment'=8,'tp'=16] {'tp'}, dimensions={0} | all-to-all | bytes 1638400 | tf_op jit(solution)/shard_map/cond/branch_1_fun/all_to_all | solution.py:536
  98.2 7.7 %conditional.8 = ((bf16[8,3072]{1,0:T(8,128)(2,1)S(1)}, bf16[8,3072]{1,0:T(8,128)(2,1)}, bf16[128,3072]{1,0:T(8,128)(2,1)S(1)}, bf16[128,768]{1,0:T(8,128)(2,1)}...) conditional(s32[]{:T(128)} %convert_element_type.29, ...), branch_computations={%region_2.3_spmd, %region_3.4_spmd} | conditional | flops 2415919104 | bytes 53608656 | solution.py:707
  106.0 55.4 %collective-permute-start.5 = (bf16[8,3072]{1,0:T(8,128)(2,1)S(1)}, bf16[8,3072]{1,0:T(8,128)(2,1)S(1)}, u32[]{:S(2)}, u32[]{:S(2)}) collective-permute-start(bf16[8,3072]{1,0:T(8,128)(2,1)S(1)} %get-tuple-element.865), channel_id=1, source_target_pairs={{0,32},{16,48},{32,64},{48,80},{64,96},{80,112},{96,0},{112,16},{1... | collective-permute-start | bytes 147464 | tf_op jit(solution)/shard_map/ppermute | solution.py:714
  161.4 30.2 %turned_weights.3 = (bf16[768,3072]{1,0:T(8,128)(2,1)}, bf16[3072,768]{1,0:T(8,128)(2,1)}, bf16[768,3072]{1,0:T(8,128)(2,1)}, bf16[3072,768]{1,0:T(8,128)(2,1)}) custom-call(s32[2]{0:T(128)S(1)} %get-tuple-element.960.flag_ref, bf16[3072,768]{1,0:T(8,128)(2,1)} %bitcast.168, ...), custom_call_target="tpu_custom_call", output_to_operand_aliasing={{0}: (5, {}), {1}: (6, {}), {2}: (7, {}), {3}: (8, {})} | custom-call | tf_op jit(solution)/shard_map/turned_weights/pallas_call | solution.py:341
  195.8 9.4 %conditional.10 = (bf16[8,3072]{1,0:T(8,128)(2,1)S(1)}, bf16[8,3072]{1,0:T(8,128)(2,1)}, bf16[128,3072]{1,0:T(8,128)(2,1)S(1)}, bf16[128,768]{1,0:T(8,128)(2,1)}...) conditional(s32[]{:T(128)} %convert_element_type.26, ...), branch_computations={%region_6.7_spmd, %region_7.8_spmd} | conditional | flops 4227858432 | bytes 89752048 | solution.py:723
  205.2 136.8 %collective-permute-start.7 = (bf16[8,3072]{1,0:T(8,128)(2,1)S(1)}, bf16[8,3072]{1,0:T(8,128)(2,1)S(1)}, u32[]{:S(2)}, u32[]{:S(2)}) collective-permute-start(bf16[8,3072]{1,0:T(8,128)(2,1)S(1)} %get-tuple-element.899), channel_id=1, source_target_pairs={{32,0},{48,16},{64,32},{80,48},{96,64},{112,80},{0,96},{16,112},{3... | collective-permute-start | bytes 147464 | tf_op jit(solution)/shard_map/ppermute | solution.py:727
  347.7 5.1 conditional.12
  352.8 64.7 %collective-permute-start.9 = (bf16[8,3072]{1,0:T(8,128)(2,1)S(1)}, bf16[8,3072]{1,0:T(8,128)(2,1)S(1)}, u32[]{:S(2)}, u32[]{:S(2)}) collective-permute-start(bf16[8,3072]{1,0:T(8,128)(2,1)S(1)} %get-tuple-element.933), channel_id=1, source_target_pairs={{32,0},{48,16},{64,32},{80,48},{96,64},{112,80},{0,96},{16,112},{3... | collective-permute-start | bytes 147464 | tf_op jit(solution)/shard_map/ppermute | solution.py:727
  417.5 66.4 %collective-permute-done.9 = bf16[8,3072]{1,0:T(8,128)(2,1)S(1)} collective-permute-done((bf16[8,3072]{1,0:T(8,128)(2,1)S(1)}, bf16[8,3072]{1,0:T(8,128)(2,1)S(1)}, u32[]{:S(2)}, u32[]{:S(2)}) %collective-permute-start.9) | collective-permute-done | bytes 49184 | tf_op jit(solution)/shard_map/ppermute | solution.py:727
  483.9 49.6 %conditional.13 = ((bf16[128,3072]{1,0:T(8,128)(2,1)}, bf16[16,128]{1,0:T(8,128)(2,1)S(1)}, f32[16,768]{1,0:T(8,128)S(1)}, f32[16,768]{1,0:T(8,128)S(1)}, bf16[1...) conditional(s32[]{:T(128)} %convert_element_type.12, ...), branch_computations={%region_12.13_spmd, %region_13.14_spmd} | conditional | flops 1811939328 | bytes 33030264 | solution.py:728
  484.0 13.2 %all_to_all.147 = bf16[16,8,3072]{2,1,0:T(8,128)(2,1)S(1)} all-to-all(bf16[16,8,3072]{2,1,0:T(8,128)(2,1)S(1)} %bitcast.127), channel_id=1, replica_groups=mesh['segment'=8,'tp'=16] {'tp'}, dimensions={0} | all-to-all | bytes 1572864 | tf_op jit(solution)/shard_map/cond/branch_1_fun/all_to_all | solution.py:536
  497.2 5.7 block_backward.14
  502.9 13.0 %all_to_all.148 = bf16[16,8,3072]{2,1,0:T(8,128)(2,1)S(1)} all-to-all(bf16[16,8,3072]{2,1,0:T(8,128)(2,1)S(1)} %bitcast.152), channel_id=1, replica_groups=mesh['segment'=8,'tp'=16] {'tp'}, dimensions={0} | all-to-all | bytes 1572864 | tf_op jit(solution)/shard_map/cond/branch_1_fun/all_to_all | solution.py:536
  517.6 13.1 %all_to_all.149 = bf16[16,8,3072]{2,1,0:T(8,128)(2,1)S(1)} all-to-all(bf16[16,8,3072]{2,1,0:T(8,128)(2,1)S(1)} %bitcast.162), channel_id=1, replica_groups=mesh['segment'=8,'tp'=16] {'tp'}, dimensions={0} | all-to-all | bytes 1572864 | tf_op jit(solution)/shard_map/cond/branch_1_fun/all_to_all | solution.py:536
  533.5 10.1 %all_to_all.150 = bf16[16,64,128]{2,1,0:T(8,128)(2,1)S(1)} all-to-all(bf16[16,64,128]{2,1,0:T(8,128)(2,1)S(1)} %bitcast.139), channel_id=1, replica_groups=mesh['segment'=8,'tp'=16] {'tp'}, dimensions={0} | all-to-all | bytes 524288 | tf_op jit(solution)/shard_map/all_to_all | solution.py:536
  546.2 44.8 %collective-permute-start.10 = (f32[16,7680]{1,0:T(8,128)S(1)}, f32[16,7680]{1,0:T(8,128)S(1)}, u32[]{:S(2)}, u32[]{:S(2)}) collective-permute-start(f32[16,7680]{1,0:T(8,128)S(1)} %get-tuple-element.945), channel_id=1, source_target_pairs={{0,16},{16,0},{32,48},{48,32},{64,80},{80,64},{96,112},{112,96},{1... | collective-permute-start | bytes 1474568 | tf_op jit(solution)/shard_map/ppermute | solution.py:744
  (58 shorter events, 38.7 us)
Async XLA Ops:
  0.6 34.8 %collective-permute-start = (bf16[3072,768]{1,0:T(8,128)(2,1)}, bf16[3072,768]{1,0:T(8,128)(2,1)}, u32[]{:S(2)}, u32[]{:S(2)}) collective-permute-start(bf16[3072,768]{1,0:T(8,128)(2,1)} %bitcast.163), channel_id=1, source_target_pairs={{0,16},{16,0},{32,48},{48,32},{64,80},{80,64},{96,112},{112,96},{1... | collective-permute-start | bytes 14155784 | tf_op jit(solution)/shard_map/ppermute | solution.py:573
  2.1 33.3 %collective-permute-start.1 = (bf16[768,3072]{1,0:T(8,128)(2,1)}, bf16[768,3072]{1,0:T(8,128)(2,1)}, u32[]{:S(2)}, u32[]{:S(2)}) collective-permute-start(bf16[768,3072]{1,0:T(8,128)(2,1)} %bitcast.171), channel_id=1, source_target_pairs={{0,16},{16,0},{32,48},{48,32},{64,80},{80,64},{96,112},{112,96},{1... | collective-permute-start | bytes 14155784 | tf_op jit(solution)/shard_map/ppermute | solution.py:574
  2.3 0.7 copy-start
  4.7 17.1 %collective-permute-start.3 = (bf16[16,7680]{1,0:T(8,128)(2,1)S(1)}, bf16[16,7680]{1,0:T(8,128)(2,1)S(1)}, u32[]{:S(2)}, u32[]{:S(2)}) collective-permute-start(bf16[16,7680]{1,0:T(8,128)(2,1)S(1)} %get-tuple-element.846), channel_id=1, source_target_pairs={{0,16},{16,0},{32,48},{48,32},{64,80},{80,64},{96,112},{112,96},{1... | collective-permute-start | bytes 737288 | tf_op jit(solution)/shard_map/ppermute | solution.py:608
  6.1 4.5 copy-start.9
  6.1 4.5 collective-permute-start.2
  10.7 0.7 copy-start.2
  14.0 21.4 %all-to-all-start.28 = ((bf16[16,8,3072]{2,1,0:T(8,128)(2,1)}), bf16[16,8,3072]{2,1,0:T(8,128)(2,1)S(1)}, u32[]{:S(2)}, u32[]{:S(2)}) async-start(bf16[16,8,3072]{2,1,0:T(8,128)(2,1)} %bitcast.64), calls=%async_computation.28 | async-start | bytes 1572864 | tf_op jit(solution)/shard_map/all_to_all | solution.py:536
  94.0 4.2 collective-permute-start.4
  106.0 85.6 %collective-permute-start.5 = (bf16[8,3072]{1,0:T(8,128)(2,1)S(1)}, bf16[8,3072]{1,0:T(8,128)(2,1)S(1)}, u32[]{:S(2)}, u32[]{:S(2)}) collective-permute-start(bf16[8,3072]{1,0:T(8,128)(2,1)S(1)} %get-tuple-element.865), channel_id=1, source_target_pairs={{0,32},{16,48},{32,64},{48,80},{64,96},{80,112},{96,0},{112,16},{1... | collective-permute-start | bytes 147464 | tf_op jit(solution)/shard_map/ppermute | solution.py:714
  191.6 4.2 collective-permute-start.6
  205.2 138.0 %collective-permute-start.7 = (bf16[8,3072]{1,0:T(8,128)(2,1)S(1)}, bf16[8,3072]{1,0:T(8,128)(2,1)S(1)}, u32[]{:S(2)}, u32[]{:S(2)}) collective-permute-start(bf16[8,3072]{1,0:T(8,128)(2,1)S(1)} %get-tuple-element.899), channel_id=1, source_target_pairs={{32,0},{48,16},{64,32},{80,48},{96,64},{112,80},{0,96},{16,112},{3... | collective-permute-start | bytes 147464 | tf_op jit(solution)/shard_map/ppermute | solution.py:727
  343.2 4.4 collective-permute-start.8
  352.8 131.1 %collective-permute-start.9 = (bf16[8,3072]{1,0:T(8,128)(2,1)S(1)}, bf16[8,3072]{1,0:T(8,128)(2,1)S(1)}, u32[]{:S(2)}, u32[]{:S(2)}) collective-permute-start(bf16[8,3072]{1,0:T(8,128)(2,1)S(1)} %get-tuple-element.933), channel_id=1, source_target_pairs={{32,0},{48,16},{64,32},{80,48},{96,64},{112,80},{0,96},{16,112},{3... | collective-permute-start | bytes 147464 | tf_op jit(solution)/shard_map/ppermute | solution.py:727
  483.9 108.6 %copy-start.1 = (s32[2]{0:T(128)S(1)}, s32[2]{0:T(128)}, u32[]{:S(2)}) copy-start(s32[2]{0:T(128)} %jobs_ref.3) | copy-start | bytes 28
  497.2 33.5 %slice-start.6 = ((s8[4718592]{0:T(1024)(128)(4,1)}), s8[4194304]{0:T(1024)(128)(4,1)S(1)}, s32[]{:S(2)}) async-start(s8[4718592]{0:T(1024)(128)(4,1)} %bitcast.87), calls=%async_computation.36 | async-start | bytes 8388608 | tf_op jit(solution)/shard_map/cond
  497.2 33.5 %slice-start.7 = ((s8[4718592]{0:T(1024)(128)(4,1)}), s8[524288]{0:T(1024)(128)(4,1)S(1)}, s32[]{:S(2)}) async-start(s8[4718592]{0:T(1024)(128)(4,1)} %bitcast.87), calls=%async_computation.37 | async-start | bytes 1048576 | tf_op jit(solution)/shard_map/cond
  546.2 46.3 %collective-permute-start.10 = (f32[16,7680]{1,0:T(8,128)S(1)}, f32[16,7680]{1,0:T(8,128)S(1)}, u32[]{:S(2)}, u32[]{:S(2)}) collective-permute-start(f32[16,7680]{1,0:T(8,128)S(1)} %get-tuple-element.945), channel_id=1, source_target_pairs={{0,16},{16,0},{32,48},{48,32},{64,80},{80,64},{96,112},{112,96},{1... | collective-permute-start | bytes 1474568 | tf_op jit(solution)/shard_map/ppermute | solution.py:744

commit v4 on v3

--- a/solution.py
+++ b/solution.py
@@ -66,39 +66,6 @@
 
 def in_hbm(*arrays):
     return [pltpu.with_memory_space_constraint(a, pltpu.HBM) for a in arrays]
-
-
-def order_kernel(flag_ref, wi_own, wi_other, wo_own, wo_other, *refs):
-    outs, (wi_buf, wo_buf, in_sems, out_sems) = refs[:2], refs[2:]
-    sources = ((wi_own, wi_other, wi_buf), (wo_own, wo_other, wo_buf))
-
-    @pl.when(flag_ref[0] == 1)
-    def _():
-        for k, (ours, theirs, buf) in enumerate(sources):
-            fetch(flag_ref[1] == 1, ours, theirs, buf, in_sems.at[k])
-        for k, (ours, theirs, buf) in enumerate(sources):
-            pltpu.make_async_copy(ours, buf, in_sems.at[k]).wait()
-            pltpu.make_async_copy(buf, outs[k], out_sems.at[k]).start()
-        for k, (ours, theirs, buf) in enumerate(sources):
-            pltpu.make_async_copy(buf, outs[k], out_sems.at[k]).wait()
-
-
-def second_weights(flag, weights):
-    out = [shape_of(*weights[0].shape), shape_of(*weights[2].shape)]
-    return pl.pallas_call(
-        order_kernel,
-        out_shape=out,
-        in_specs=[SMEM] + [HBM] * 4,
-        out_specs=[HBM] * 2,
-        scratch_shapes=[
-            pltpu.VMEM(out[0].shape, BF16),
-            pltpu.VMEM(out[1].shape, BF16),
-            pltpu.SemaphoreType.DMA((2,)),
-            pltpu.SemaphoreType.DMA((2,)),
-        ],
-        compiler_params=PARAMS,
-        name="second_weights",
-    )(flag, *in_hbm(*weights))
 
 
 def forward_kernel(*refs, last, streamed):
@@ -282,7 +249,33 @@
     )(g, slope, act, low_in, *(in_hbm if streamed else in_vmem)(*weights), *low)
 
 
-def turn_kernel(flag_ref, *refs):
+def ready_kernel(flag_ref, *refs, order):
+    if order:
+        ordered, wi_buf, wo_buf, buf_sems = refs[8:12], *refs[-3:]
+        refs = refs[:8] + refs[12:-3]
+
+        @pl.when(flag_ref[2] == 1)
+        def _():
+            order_weights(flag_ref, refs[:4], ordered, (wi_buf, wo_buf), buf_sems)
+
+    turn_weights(flag_ref, *refs)
+
+
+def order_weights(flag_ref, refs, outs, bufs, sems):
+    sources = ((refs[0], refs[1], bufs[0]), (refs[2], refs[3], bufs[1]))
+    for i in range(2):
+        for k, (ours, theirs, buf) in enumerate(sources):
+            if i:
+                pltpu.make_async_copy(buf, outs[k], sems.at[2 + k]).wait()
+            fetch(flag_ref[1] == i, ours, theirs, buf, sems.at[k])
+        for k, (ours, theirs, buf) in enumerate(sources):
+            pltpu.make_async_copy(ours, buf, sems.at[k]).wait()
+            pltpu.make_async_copy(buf, outs[2 * i + k], sems.at[2 + k]).start()
+    for k, (ours, theirs, buf) in enumerate(sources):
+        pltpu.make_async_copy(buf, outs[2 + k], sems.at[2 + k]).wait()
+
+
+def turn_weights(flag_ref, *refs):
     narrow_buf, wide_buf, in_sems, out_sems = refs[-4:]
     outs, sources = refs[-8:-4], refs[:4]
     step = narrow_buf.shape[1]
@@ -335,25 +328,33 @@
             turn(own, *sources[2:], outs[2 * i + 1], wide_buf, narrow_buf, False)
 
 
-def turned_weights(flag, weights, held):
+def ready_weights(flag, weights, held):
     width, cols = weights[0].shape
     step = 384
+    turned = [shape_of(cols, width), shape_of(width, cols)] * 2
+    ordered = [] if held else [shape_of(width, cols), shape_of(cols, width)] * 2
+    buffers = [
+        pltpu.VMEM((width, cols), BF16),
+        pltpu.VMEM((cols, width), BF16),
+        pltpu.SemaphoreType.DMA((4,)),
+    ]
     out = pl.pallas_call(
-        turn_kernel,
-        out_shape=[shape_of(cols, width), shape_of(width, cols)] * 2,
+        functools.partial(ready_kernel, order=not held),
+        out_shape=turned + ordered,
         in_specs=[SMEM] + [HBM] * (4 + len(held)),
-        out_specs=[HBM] * 4,
+        out_specs=[HBM] * (4 + len(ordered)),
         scratch_shapes=[
             pltpu.VMEM((2, step, cols), BF16),
             pltpu.VMEM((2, cols, step), BF16),
             pltpu.SemaphoreType.DMA((2,)),
             pltpu.SemaphoreType.DMA((2,)),
+            *([] if held else buffers),
         ],
         input_output_aliases={5 + k: k for k in range(len(held))},
         compiler_params=PARAMS,
-        name="turned_weights",
+        name="ready_weights",
     )(flag, *in_hbm(*weights), *held)
-    return tuple(out)
+    return tuple(out[:4]), tuple(out[4:])
 
 
 def summed(got_ref, own_rows, at):
@@ -375,45 +376,25 @@
     return rms_stats(wide)[0] * (1.0 + mod_ref[1:2]) + mod_ref[0:1]
 
 
-def first_rows_kernel(
-    ids_ref,
-    counts_ref,
-    x_ref,
-    e_ref,
-    mod_own,
-    mod_other,
-    out_ref,
-    x_out,
-    e_out,
-    mask_out,
-    mod_0,
-    mod_1,
-    x_in,
-    e_in,
-    mod_in,
-    sems,
-):
-    copies = [
-        keep(source, held, sems.at[k])
-        for k, (source, held) in enumerate(((x_ref, x_in), (e_ref, e_in), (mod_own, mod_in)))
-    ]
-    for copy in copies:
-        copy.wait()
+def first_rows_kernel(ids_ref, counts_ref, x_ref, e_ref, out_ref, x_out, e_out, mask_out):
     at_start, core, tp_pos = ids_ref[0], ids_ref[1], ids_ref[2]
     own_rows = x_ref.shape[1]
     row = tp_pos * own_rows + lax.broadcasted_iota(jnp.int32, (own_rows, 1), 0)
     mask = (row < counts_ref[core]).astype(F32)
     mask_out[...] = mask
-    ours, theirs = mod_in[core], mod_other[core]
-    mod_0[...] = jnp.where(core == 0, ours, theirs)
-    mod_1[...] = jnp.where(core == 0, theirs, ours)
-    x = (x_in[core].astype(F32) * mask).astype(BF16)
-    e = (e_in[core].astype(F32) * mask).astype(BF16)
-    x_out[...] = x
-    e_out[...] = e
-    u = modulated(x.astype(F32), mod_0)
-    g = mod_1[2:3] * e.astype(F32)
-    spread(out_ref, jnp.where(at_start == 1, u, g))
+    x = x_ref[core].astype(F32) * mask
+    e = e_ref[core].astype(F32) * mask
+    x_out[...] = x.astype(BF16)
+    e_out[...] = e.astype(BF16)
+    spread(out_ref, jnp.where(at_start == 1, x, e))
+
+
+def modulate_kernel(x_ref, mod_ref, out_ref):
+    out_ref[...] = modulated(x_ref[...].astype(F32), mod_ref).astype(BF16)
+
+
+def gate_kernel(e_ref, mod_ref, out_ref):
+    out_ref[...] = (mod_ref[2:3] * e_ref[...].astype(F32)).astype(BF16)
 
 
 def pack_kernel(ids_ref, jobs_ref, *refs):
@@ -520,13 +501,14 @@
         pl.when((place >= 0) & (place < owners))(owned)
 
 
-def rows_call(kernel, out, *operands, scalars=0):
+def rows_call(kernel, out, *operands, scalars=0, cost=None):
     return pl.pallas_call(
         kernel,
         out_shape=out,
         in_specs=[SMEM] * scalars + [VMEM] * (len(operands) - scalars),
         out_specs=jax.tree.map(lambda _: VMEM, out),
         compiler_params=PARAMS,
+        cost_estimate=cost,
         name=kernel.__name__,
     )(*operands)
 
@@ -568,28 +550,21 @@
     ids = jnp.stack([(plane == 0).astype(jnp.int32), core, tp_pos]).astype(jnp.int32)
     full = shape_of(rows, width)
     some = shape_of(own_rows, width)
-    mod = modulation[0]
-    mod_other = lax.ppermute(mod, "segment", swap)
     w_first = (w_in[0], lax.ppermute(w_in[0], "segment", swap))
     w_second = (w_out[0], lax.ppermute(w_out[0], "segment", swap))
 
-    mod_shape = shape_of(*mod.shape[1:], dtype=F32)
-    sources = (latents, cotangent, mod)
-    ends, x, e_last, mask, *mods = pl.pallas_call(
+    ends, x, e_last, mask = rows_call(
         first_rows_kernel,
-        out_shape=[full, some, some, shape_of(own_rows, 1, dtype=F32), mod_shape, mod_shape],
-        in_specs=[SMEM, SMEM, HBM, HBM, HBM, VMEM],
-        out_specs=[VMEM] * 6,
-        scratch_shapes=[pltpu.VMEM(a.shape, a.dtype) for a in sources]
-        + [pltpu.SemaphoreType.DMA((len(sources),))],
-        compiler_params=PARAMS,
-        name="first_rows_kernel",
-    )(
+        [full, some, some, shape_of(own_rows, 1, dtype=F32)],
         ids,
         token_counts,
-        *in_hbm(*sources),
-        mod_other,
-    )
+        latents,
+        cotangent,
+        scalars=2,
+    )
+    ends, ids, mod = lax.optimization_barrier((ends, ids, modulation[0]))
+    mod_other = lax.ppermute(mod, "segment", swap)
+    mods = [jnp.where(core == i, mod, mod_other)[core] for i in range(2)]
 
     adapters = [a[0] for a in (down_in, up_in, down_out, up_out)]
     packed = shape_of(rank, sum(a.shape[2] for a in adapters))
@@ -612,31 +587,31 @@
     ]
 
     ends = exchanged(ends, tp)
-
-    def turn_weights(which, held, x):
-        flag = jnp.stack([which.astype(jnp.int32), core])
-        turned = turned_weights(flag, (*w_first, *w_second), held)
-        return lax.optimization_barrier((turned, x))
-
+    ahead = pl.CostEstimate(
+        flops=16 * rows * width * cols, bytes_accessed=16 * width * cols, transcendentals=rows * width
+    )
     owns = [(core == i).astype(jnp.int32).reshape(1) for i in range(2)]
-    flag = jnp.stack([(plane > 0).astype(jnp.int32), core])
-    turn_flag = (plane >= planes // 2).astype(jnp.int32)
-    ends, flag, turn_flag = lax.optimization_barrier((ends, flag, turn_flag))
-    second, x = lax.optimization_barrier((second_weights(flag, (*w_first, *w_second)), x))
-    turned, x = turn_weights(turn_flag, (), x)
-
-    def forward_plane(x, second, p):
+    flag = jnp.stack([plane >= planes // 2, core, plane > 0]).astype(jnp.int32)
+    ends, flag = lax.optimization_barrier((ends, flag))
+    (turned, ordered), x = lax.optimization_barrier(
+        (ready_weights(flag, (*w_first, *w_second), ()), x)
+    )
+
+    def forward_plane(x, ordered, p):
         saved = []
         for i in range(2):
             if i:
                 u = exchanged(sent, tp)
+            elif p == 0:
+                u = rows_call(modulate_kernel, full, ends, mods[0])
             else:
-                u = ends if p == 0 else exchanged(rows_call(rows_in_kernel, full, x, mods[0]), tp)
+                u = exchanged(rows_call(rows_in_kernel, full, x, mods[0], cost=ahead), tp)
             last = p == last_plane and i == 1
-            if i == 0 or p == 0:
+            if p == 0:
                 done = block_forward(u, (*w_first, *w_second), lows[i], owns[i])
             else:
-                done = block_forward(u, second[:1] if last else second, lows[i])
+                pair = ordered[2 * i : 2 * i + 2]
+                done = block_forward(u, pair[:1] if last else pair, lows[i])
             act, slope, low_in, low_part, u, *part = done
             kept = (u, (act, slope, low_in), low_part)
             if last:
@@ -668,14 +643,14 @@
             if i == 0:
                 g = exchanged(sent, tp)
             elif p == last_plane:
-                g = ends
+                g = rows_call(gate_kernel, full, ends, mods[1])
             else:
-                g = exchanged(rows_call(gate_rows_kernel, full, e, mods[1]), tp)
+                g = exchanged(rows_call(gate_rows_kernel, full, e, mods[1], cost=ahead), tp)
             x, u, acts, low_part = saved[i]
             first = p == 0 and i == 0
             w_in_t, w_out_t = turned[2 * i : 2 * i + 2]
             g_low_in, grad_ui, grad_do, g, *part = block_backward(
-                g, acts, [w_out_t] if first else [w_out_t, w_in_t], lows[i], i == 1
+                g, acts, [w_out_t] if first else [w_out_t, w_in_t], lows[i], False
             )
             kept[i] = (g, g_low_in, grad_ui, grad_do)
             if first:
@@ -706,17 +681,20 @@
     for p in range(last_plane):
         x, saved = lax.cond(
             plane == p,
-            lambda x, saved: forward_plane(x, second, p),
+            lambda x, saved: forward_plane(x, ordered, p),
             lambda x, saved: (x, saved),
             x,
             saved,
         )
         x = lax.ppermute(x, "segment", onward)
         if p == planes // 2 - 1:
-            turned, x = turn_weights(plane < planes // 2, turned, x)
+            flag = jnp.stack([plane < planes // 2, core]).astype(jnp.int32)
+            (turned, _), x = lax.optimization_barrier(
+                (ready_weights(flag, (*w_first, *w_second), turned), x)
+            )
 
     def turn(x, saved, kept):
-        x, saved = forward_plane(x, second, last_plane)
+        x, saved = forward_plane(x, ordered, last_plane)
         e, kept = backward_plane(e_last, saved, turned, last_plane)
         return e, saved, kept
 
@@ -735,9 +713,10 @@
         )
 
     narrow = (saved[0][3], saved[1][3], kept[0][1], kept[1][1])
-    got = exchanged(rows_call(narrow_kernel, shape_of(tp * 4 * rank, rows), *narrow), tp)
+    narrow_out = shape_of(tp * 4 * rank, rows)
+    got = exchanged(rows_call(narrow_kernel, narrow_out, *narrow, cost=ahead), tp)
     wide = [shape_of(*packed.shape, dtype=F32)] * 2
-    per_block = [(kept[i][0], saved[i][1], kept[i][2], kept[i][3]) for i in range(2)]
+    per_block = [(*in_vmem(kept[i][0], saved[i][1]), kept[i][2], kept[i][3]) for i in range(2)]
     mine, sent = rows_call(
         gradients_kernel, wide, ids, got, *per_block[0], *per_block[1], scalars=1
     )

time: 604 us -> 591 us (0.978)
  starting transfers between devices: 315 us -> 308 us
    pallas_call x4 -> x2, Pallas kernels: 34 us -> 30.8 us  [ready_weights(): pl.pallas_call(functools.partial(ready_kernel, order=not held), out_shape...]
where the time goes in v4:
time: 591 us; the launch traced here: 581 us
  starting transfers between devices  308 us (52%)
  blocking collectives  95.6 us (16%)
  waiting for transfers between devices  90.5 us (15%)
  Pallas kernels  59.1 us (10%)
  loops' own time  16.7 us (3%)
  local copies, waits for them, and re-layouts  8.93 us (2%)
    ppermute x3, starting transfers between devices, shards(): e = lax.ppermute(e, 'segment', back)  200 us
    all_to_all x7, blocking collectives, exchanged(): got = lax.all_to_all(parts.reshape(tp, rows // tp, width), 'tp', 0, 0)  95.6 us
    ppermute x3, waiting for transfers between devices, shards(): e = lax.ppermute(e, 'segment', back)  70.9 us
    ppermute x3, starting transfers between devices, shards(): x = lax.ppermute(x, 'segment', onward)  53.2 us
    ppermute x1, starting transfers between devices, shards(): theirs = lax.ppermute(sent, 'segment', swap)  45.3 us
    pallas_call x2, Pallas kernels, ready_weights(): pl.pallas_call(functools.partial(ready_kernel, order=not held), out_shape...  30.8 us
  transfers between devices with their start and end apart: 12, of which 8 were waited for; matrix products, arithmetic and copies ran while one was open for 0% of the time, Pallas kernels for 6%

profile of v4, /device:TPU:1, one launch (start us, length us, event | category | flops | bytes accessed | tf_op | source)
XLA Modules:
  0.0 580.7 jit_solution(691415307500755903)
XLA Ops:
  6.3 7.9 %all-to-all-start.28 = ((bf16[16,8,3072]{2,1,0:T(8,128)(2,1)}), bf16[16,8,3072]{2,1,0:T(8,128)(2,1)S(1)}, u32[]{:S(2)}, u32[]{:S(2)}) async-start(bf16[16,8,3072]{2,1,0:T(8,128)(2,1)} %bitcast.65), calls=%async_computation.28 | async-start | bytes 1572864 | tf_op jit(solution)/shard_map/all_to_all | solution.py:518
  19.0 8.6 %all-to-all-done.28 = bf16[16,8,3072]{2,1,0:T(8,128)(2,1)S(1)} async-done(((bf16[16,8,3072]{2,1,0:T(8,128)(2,1)}), bf16[16,8,3072]{2,1,0:T(8,128)(2,1)S(1)}, u32[]{:S(2)}, u32[]{:S(2)}) %all-to-all-start.28) | async-done | bytes 786464 | tf_op jit(solution)/shard_map/all_to_all | solution.py:518
  28.4 57.0 %conditional.7 = (bf16[8,3072]{1,0:T(8,128)(2,1)S(1)}, bf16[8,3072]{1,0:T(8,128)(2,1)}, bf16[128,3072]{1,0:T(8,128)(2,1)S(1)}, bf16[128,768]{1,0:T(8,128)(2,1)},...) conditional(s32[]{:T(128)} %convert_element_type.12, ...), branch_computations={%region_0.1_spmd, %region_1.2_spmd} | conditional | flops 2415919104 | bytes 23724136 | solution.py:682
  29.0 4.4 block_forward.8
  33.3 17.1 %all_to_all.122 = bf16[16,8,3200]{2,1,0:T(8,128)(2,1)S(1)} all-to-all(bf16[16,8,3200]{2,1,0:T(8,128)(2,1)S(1)} %bitcast.139), channel_id=1, replica_groups=mesh['segment'=8,'tp'=16] {'tp'}, dimensions={0} | all-to-all | bytes 1638400 | tf_op jit(solution)/shard_map/cond/branch_1_fun/all_to_all | solution.py:518
  51.2 14.7 %all_to_all.123 = bf16[16,8,3072]{2,1,0:T(8,128)(2,1)S(1)} all-to-all(bf16[16,8,3072]{2,1,0:T(8,128)(2,1)S(1)} %bitcast.150), channel_id=1, replica_groups=mesh['segment'=8,'tp'=16] {'tp'}, dimensions={0} | all-to-all | bytes 1572864 | tf_op jit(solution)/shard_map/cond/branch_1_fun/all_to_all | solution.py:518
  65.9 4.6 block_forward.9
  70.5 13.9 %all_to_all.124 = bf16[16,8,3200]{2,1,0:T(8,128)(2,1)S(1)} all-to-all(bf16[16,8,3200]{2,1,0:T(8,128)(2,1)S(1)} %bitcast.140), channel_id=1, replica_groups=mesh['segment'=8,'tp'=16] {'tp'}, dimensions={0} | all-to-all | bytes 1638400 | tf_op jit(solution)/shard_map/cond/branch_1_fun/all_to_all | solution.py:518
  85.5 4.1 collective-permute-done.4
  89.6 7.4 %conditional.8 = ((bf16[8,3072]{1,0:T(8,128)(2,1)S(1)}, bf16[8,3072]{1,0:T(8,128)(2,1)}, bf16[128,3072]{1,0:T(8,128)(2,1)S(1)}, bf16[128,768]{1,0:T(8,128)(2,1)}...) conditional(s32[]{:T(128)} %convert_element_type.28, ...), branch_computations={%region_2.3_spmd, %region_3.4_spmd} | conditional | flops 7247757312 | bytes 129106184 | solution.py:682
  97.0 53.0 %collective-permute-start.5 = (bf16[8,3072]{1,0:T(8,128)(2,1)S(1)}, bf16[8,3072]{1,0:T(8,128)(2,1)S(1)}, u32[]{:S(2)}, u32[]{:S(2)}) collective-permute-start(bf16[8,3072]{1,0:T(8,128)(2,1)S(1)} %get-tuple-element.845), channel_id=1, source_target_pairs={{0,32},{16,48},{32,64},{48,80},{64,96},{80,112},{96,0},{112,16},{1... | collective-permute-start | bytes 147464 | tf_op jit(solution)/shard_map/ppermute | solution.py:689
  150.1 30.2 %ready_weights.3 = (bf16[768,3072]{1,0:T(8,128)(2,1)}, bf16[3072,768]{1,0:T(8,128)(2,1)}, bf16[768,3072]{1,0:T(8,128)(2,1)}, bf16[3072,768]{1,0:T(8,128)(2,1)}) custom-call(s32[2]{0:T(128)S(1)} %pad_add_fusion.1.flag_ref, bf16[3072,768]{1,0:T(8,128)(2,1)} %bitcast.165, ...), custom_call_target="tpu_custom_call", output_to_operand_aliasing={{0}: (5, {}), {1}: (6, {}), {2}: (7, {}), {3}: (8, {})} | custom-call | tf_op jit(solution)/shard_map/ready_weights/pallas_call | solution.py:341
  180.4 4.1 collective-permute-done.6
  184.6 14.5 %conditional.10 = (bf16[8,3072]{1,0:T(8,128)(2,1)S(1)}, bf16[8,3072]{1,0:T(8,128)(2,1)}, bf16[128,3072]{1,0:T(8,128)(2,1)S(1)}, bf16[128,768]{1,0:T(8,128)(2,1)}...) conditional(s32[]{:T(128)} %convert_element_type.26, ...), branch_computations={%region_6.7_spmd, %region_7.8_spmd} | conditional | flops 9059696640 | bytes 221741920 | solution.py:701
  199.1 132.2 %collective-permute-start.7 = (bf16[8,3072]{1,0:T(8,128)(2,1)S(1)}, bf16[8,3072]{1,0:T(8,128)(2,1)S(1)}, u32[]{:S(2)}, u32[]{:S(2)}) collective-permute-start(bf16[8,3072]{1,0:T(8,128)(2,1)S(1)} %get-tuple-element.879), channel_id=1, source_target_pairs={{32,0},{48,16},{64,32},{80,48},{96,64},{112,80},{0,96},{16,112},{3... | collective-permute-start | bytes 147464 | tf_op jit(solution)/shard_map/ppermute | solution.py:705
  337.1 64.2 %collective-permute-start.9 = (bf16[8,3072]{1,0:T(8,128)(2,1)S(1)}, bf16[8,3072]{1,0:T(8,128)(2,1)S(1)}, u32[]{:S(2)}, u32[]{:S(2)}) collective-permute-start(bf16[8,3072]{1,0:T(8,128)(2,1)S(1)} %get-tuple-element.913), channel_id=1, source_target_pairs={{32,0},{48,16},{64,32},{80,48},{96,64},{112,80},{0,96},{16,112},{3... | collective-permute-start | bytes 147464 | tf_op jit(solution)/shard_map/ppermute | solution.py:705
  401.3 68.5 %collective-permute-done.9 = bf16[8,3072]{1,0:T(8,128)(2,1)S(1)} collective-permute-done((bf16[8,3072]{1,0:T(8,128)(2,1)S(1)}, bf16[8,3072]{1,0:T(8,128)(2,1)S(1)}, u32[]{:S(2)}, u32[]{:S(2)}) %collective-permute-start.9) | collective-permute-done | bytes 49184 | tf_op jit(solution)/shard_map/ppermute | solution.py:705
  469.8 48.7 %conditional.13 = ((bf16[128,3072]{1,0:T(8,128)(2,1)}, bf16[16,128]{1,0:T(8,128)(2,1)}, f32[16,768]{1,0:T(8,128)}, f32[16,768]{1,0:T(8,128)}, bf16[128,3072]{1,0...) conditional(s32[]{:T(128)} %convert_element_type.12, ...), branch_computations={%region_12.13_spmd, %region_13.14_spmd} | conditional | flops 6643777536 | bytes 109805872 | solution.py:706
  469.9 13.8 %all_to_all.146 = bf16[16,8,3072]{2,1,0:T(8,128)(2,1)S(1)} all-to-all(bf16[16,8,3072]{2,1,0:T(8,128)(2,1)S(1)} %bitcast.160), channel_id=1, replica_groups=mesh['segment'=8,'tp'=16] {'tp'}, dimensions={0} | all-to-all | bytes 1572864 | tf_op jit(solution)/shard_map/cond/branch_1_fun/all_to_all | solution.py:518
  483.7 3.9 block_backward.14
  487.7 13.0 %all_to_all.147 = bf16[16,8,3072]{2,1,0:T(8,128)(2,1)S(1)} all-to-all(bf16[16,8,3072]{2,1,0:T(8,128)(2,1)S(1)} %bitcast.145), channel_id=1, replica_groups=mesh['segment'=8,'tp'=16] {'tp'}, dimensions={0} | all-to-all | bytes 1572864 | tf_op jit(solution)/shard_map/cond/branch_1_fun/all_to_all | solution.py:518
  502.3 13.0 %all_to_all.148 = bf16[16,8,3072]{2,1,0:T(8,128)(2,1)S(1)} all-to-all(bf16[16,8,3072]{2,1,0:T(8,128)(2,1)S(1)} %bitcast.154), channel_id=1, replica_groups=mesh['segment'=8,'tp'=16] {'tp'}, dimensions={0} | all-to-all | bytes 1572864 | tf_op jit(solution)/shard_map/cond/branch_1_fun/all_to_all | solution.py:518
  519.2 10.2 %all_to_all.149 = bf16[16,64,128]{2,1,0:T(8,128)(2,1)S(1)} all-to-all(bf16[16,64,128]{2,1,0:T(8,128)(2,1)S(1)} %bitcast.161), channel_id=1, replica_groups=mesh['segment'=8,'tp'=16] {'tp'}, dimensions={0} | all-to-all | bytes 524288 | tf_op jit(solution)/shard_map/all_to_all | solution.py:518
  531.7 45.3 %collective-permute-start.10 = (f32[16,7680]{1,0:T(8,128)S(1)}, f32[16,7680]{1,0:T(8,128)S(1)}, u32[]{:S(2)}, u32[]{:S(2)}) collective-permute-start(f32[16,7680]{1,0:T(8,128)S(1)} %get-tuple-element.925), channel_id=1, source_target_pairs={{0,16},{16,0},{32,48},{48,32},{64,80},{80,64},{96,112},{112,96},{1... | collective-permute-start | bytes 1474568 | tf_op jit(solution)/shard_map/ppermute | solution.py:723
  (85 shorter events, 36.6 us)
Async XLA Ops:
  0.6 27.0 %collective-permute-start = (bf16[3072,768]{1,0:T(8,128)(2,1)}, bf16[3072,768]{1,0:T(8,128)(2,1)}, u32[]{:S(2)}, u32[]{:S(2)}) collective-permute-start(bf16[3072,768]{1,0:T(8,128)(2,1)} %bitcast.162), channel_id=1, source_target_pairs={{0,16},{16,0},{32,48},{48,32},{64,80},{80,64},{96,112},{112,96},{1... | collective-permute-start | bytes 14155784 | tf_op jit(solution)/shard_map/ppermute | solution.py:553
  2.1 25.5 %collective-permute-start.1 = (bf16[768,3072]{1,0:T(8,128)(2,1)}, bf16[768,3072]{1,0:T(8,128)(2,1)}, u32[]{:S(2)}, u32[]{:S(2)}) collective-permute-start(bf16[768,3072]{1,0:T(8,128)(2,1)} %bitcast.166), channel_id=1, source_target_pairs={{0,16},{16,0},{32,48},{48,32},{64,80},{80,64},{96,112},{112,96},{1... | collective-permute-start | bytes 14155784 | tf_op jit(solution)/shard_map/ppermute | solution.py:554
  6.3 21.3 %all-to-all-start.28 = ((bf16[16,8,3072]{2,1,0:T(8,128)(2,1)}), bf16[16,8,3072]{2,1,0:T(8,128)(2,1)S(1)}, u32[]{:S(2)}, u32[]{:S(2)}) async-start(bf16[16,8,3072]{2,1,0:T(8,128)(2,1)} %bitcast.65), calls=%async_computation.28 | async-start | bytes 1572864 | tf_op jit(solution)/shard_map/all_to_all | solution.py:518
  14.1 3.4 collective-permute-start.2
  17.3 1.6 collective-permute-start.3
  19.0 165.6 %copy-start.43 = (bf16[16,768]{1,0:T(8,128)(2,1)}, bf16[16,768]{1,0:T(8,128)(2,1)S(1)}, u32[]{:S(2)}) copy-start(bf16[16,768]{1,0:T(8,128)(2,1)S(1)} %get-tuple-element.935) | copy-start | bytes 73732
  19.0 165.5 %copy-start.24 = (bf16[16,3072]{1,0:T(8,128)(2,1)}, bf16[16,3072]{1,0:T(8,128)(2,1)S(1)}, u32[]{:S(2)}) copy-start(bf16[16,3072]{1,0:T(8,128)(2,1)S(1)} %get-tuple-element.944) | copy-start | bytes 294916
  19.0 165.5 %copy-start.30 = (bf16[16,3072]{1,0:T(8,128)(2,1)}, bf16[16,3072]{1,0:T(8,128)(2,1)S(1)}, u32[]{:S(2)}) copy-start(bf16[16,3072]{1,0:T(8,128)(2,1)S(1)} %get-tuple-element.945) | copy-start | bytes 294916
  19.0 165.5 %copy-start.38 = (bf16[16,3072]{1,0:T(8,128)(2,1)}, bf16[16,3072]{1,0:T(8,128)(2,1)S(1)}, u32[]{:S(2)}) copy-start(bf16[16,3072]{1,0:T(8,128)(2,1)S(1)} %get-tuple-element.932) | copy-start | bytes 294916
  85.4 4.2 collective-permute-start.4
  97.0 83.3 %collective-permute-start.5 = (bf16[8,3072]{1,0:T(8,128)(2,1)S(1)}, bf16[8,3072]{1,0:T(8,128)(2,1)S(1)}, u32[]{:S(2)}, u32[]{:S(2)}) collective-permute-start(bf16[8,3072]{1,0:T(8,128)(2,1)S(1)} %get-tuple-element.845), channel_id=1, source_target_pairs={{0,32},{16,48},{32,64},{48,80},{64,96},{80,112},{96,0},{112,16},{1... | collective-permute-start | bytes 147464 | tf_op jit(solution)/shard_map/ppermute | solution.py:689
  180.3 4.2 collective-permute-start.6
  199.1 133.4 %collective-permute-start.7 = (bf16[8,3072]{1,0:T(8,128)(2,1)S(1)}, bf16[8,3072]{1,0:T(8,128)(2,1)S(1)}, u32[]{:S(2)}, u32[]{:S(2)}) collective-permute-start(bf16[8,3072]{1,0:T(8,128)(2,1)S(1)} %get-tuple-element.879), channel_id=1, source_target_pairs={{32,0},{48,16},{64,32},{80,48},{96,64},{112,80},{0,96},{16,112},{3... | collective-permute-start | bytes 147464 | tf_op jit(solution)/shard_map/ppermute | solution.py:705
  332.4 4.4 collective-permute-start.8
  337.1 132.7 %collective-permute-start.9 = (bf16[8,3072]{1,0:T(8,128)(2,1)S(1)}, bf16[8,3072]{1,0:T(8,128)(2,1)S(1)}, u32[]{:S(2)}, u32[]{:S(2)}) collective-permute-start(bf16[8,3072]{1,0:T(8,128)(2,1)S(1)} %get-tuple-element.913), channel_id=1, source_target_pairs={{32,0},{48,16},{64,32},{80,48},{96,64},{112,80},{0,96},{16,112},{3... | collective-permute-start | bytes 147464 | tf_op jit(solution)/shard_map/ppermute | solution.py:705
  469.8 13.9 %copy-start.7 = (bf16[3072,768]{1,0:T(8,128)(2,1)S(1)}, bf16[3072,768]{1,0:T(8,128)(2,1)}, u32[]{:S(2)}) copy-start(bf16[3072,768]{1,0:T(8,128)(2,1)} %get-tuple-element.642.refs_4_) | copy-start | bytes 14155780 | tf_op jit(solution)/shard_map/cond
  469.8 13.9 %copy-start.42 = (bf16[16,3072]{1,0:T(8,128)(2,1)S(1)}, bf16[16,3072]{1,0:T(8,128)(2,1)}, u32[]{:S(2)}) copy-start(bf16[16,3072]{1,0:T(8,128)(2,1)} %get-tuple-element.647.refs_9_) | copy-start | bytes 294916 | tf_op jit(solution)/shard_map/cond
  469.8 13.9 %copy-start.47 = (bf16[16,768]{1,0:T(8,128)(2,1)S(1)}, bf16[16,768]{1,0:T(8,128)(2,1)}, u32[]{:S(2)}) copy-start(bf16[16,768]{1,0:T(8,128)(2,1)} %get-tuple-element.645.refs_7_) | copy-start | bytes 73732 | tf_op jit(solution)/shard_map/cond
  483.7 31.7 %slice-start.6 = ((s8[4718592]{0:T(1024)(128)(4,1)}), s8[4194304]{0:T(1024)(128)(4,1)S(1)}, s32[]{:S(2)}) async-start(s8[4718592]{0:T(1024)(128)(4,1)} %bitcast.89), calls=%async_computation.36 | async-start | bytes 8388608 | tf_op jit(solution)/shard_map/cond
  483.7 31.7 %slice-start.7 = ((s8[4718592]{0:T(1024)(128)(4,1)}), s8[524288]{0:T(1024)(128)(4,1)S(1)}, s32[]{:S(2)}) async-start(s8[4718592]{0:T(1024)(128)(4,1)} %bitcast.89), calls=%async_computation.37 | async-start | bytes 1048576 | tf_op jit(solution)/shard_map/cond
  483.7 31.7 %copy-start.29 = (bf16[16,3072]{1,0:T(8,128)(2,1)S(1)}, bf16[16,3072]{1,0:T(8,128)(2,1)}, u32[]{:S(2)}) copy-start(bf16[16,3072]{1,0:T(8,128)(2,1)} %get-tuple-element.656.refs_5_) | copy-start | bytes 294916 | tf_op jit(solution)/shard_map/cond
  483.7 31.6 %copy-start.35 = (bf16[16,3072]{1,0:T(8,128)(2,1)S(1)}, bf16[16,3072]{1,0:T(8,128)(2,1)}, u32[]{:S(2)}) copy-start(bf16[16,3072]{1,0:T(8,128)(2,1)} %get-tuple-element.659.refs_8_) | copy-start | bytes 294916 | tf_op jit(solution)/shard_map/cond
  518.5 60.1 %copy-start.20 = (s32[2]{0:T(128)S(1)}, s32[2]{0:T(128)}, u32[]{:S(2)}) copy-start(s32[2]{0:T(128)} %jobs_ref.3) | copy-start | bytes 28
  531.7 46.8 %collective-permute-start.10 = (f32[16,7680]{1,0:T(8,128)S(1)}, f32[16,7680]{1,0:T(8,128)S(1)}, u32[]{:S(2)}, u32[]{:S(2)}) collective-permute-start(f32[16,7680]{1,0:T(8,128)S(1)} %get-tuple-element.925), channel_id=1, source_target_pairs={{0,16},{16,0},{32,48},{48,32},{64,80},{80,64},{96,112},{112,96},{1... | collective-permute-start | bytes 1474568 | tf_op jit(solution)/shard_map/ppermute | solution.py:723
  (7 other events, 30.5 us)

commit v5 on v4

--- a/solution.py
+++ b/solution.py
@@ -14,7 +14,10 @@
 BF16 = jnp.bfloat16
 PAD = 128
 CUTS = 2
+PARTS = 4
 PAIR = 16
+CROSSED = (0, 1, 0, 1)
+STAGGERED = 0
 VMEM = pl.BlockSpec(memory_space=pltpu.VMEM)
 HBM = pl.BlockSpec(memory_space=pltpu.HBM)
 SMEM = pl.BlockSpec(memory_space=pltpu.SMEM)
@@ -54,8 +57,8 @@
         pltpu.make_async_copy(theirs, buf, sem).start()
 
 
-def cut(c, size):
-    return pl.ds(c * (size // CUTS), size // CUTS)
+def cut(c, size, parts=CUTS):
+    return pl.ds(c * (size // parts), size // parts)
 
 
 def keep(buf, out, sem):
@@ -149,6 +152,7 @@
     slope_copy = keep(slope_in, slope_ref, io_sems.at[1])
     low_in_copy = keep(low_in_in, low_in_ref, io_sems.at[2])
     act_copy = keep(act_in, act_ref, io_sems.at[0])
+    g_copy = keep(g_ref, g_out, io_sems.at[6])
     g_low_out = dot(g_ref[...], uo_ref[...], 1, 1).astype(BF16)
     g_act = dot(g_low_out, do_ref[...], 1, 0)
     for c in range(CUTS if streamed else 1):
@@ -158,7 +162,7 @@
     slope_copy.wait()
     g_pre = (g_act * slope_ref[...]).astype(BF16)
     g_low_ref[...] = dot(ui_ref[...], g_pre, 1, 1).astype(BF16)
-    copies = [keep(g_ref, g_out, io_sems.at[6]), keep(g_low_ref, g_low_out_ref, io_sems.at[3])]
+    copies = [g_copy, keep(g_low_ref, g_low_out_ref, io_sems.at[3])]
     low_in_copy.wait()
     grad_ui[...] = dot(low_in_ref[...], g_pre, 0, 0)
     copies.append(keep(grad_ui, grad_ui_out, io_sems.at[4]))
@@ -167,8 +171,8 @@
     copies.append(keep(grad_do, grad_do_out, io_sems.at[5]))
     if not first:
         g_low_in = dot(g_pre, ui_ref[...], 1, 1).astype(BF16)
-        for c in range(CUTS):
-            at = (slice(None), cut(c, width))
+        for c in range(CUTS if streamed else PARTS):
+            at = (slice(None), cut(c, width, CUTS if streamed else PARTS))
             arrived(wi_hbm, wi_ref, CUTS + c, at)
             part = dot(g_pre, wi_ref[at], 1, 0) + dot(g_low_in, di_ref[at], 1, 0)
             part_ref[at] = part.astype(BF16)
@@ -254,7 +258,7 @@
         ordered, wi_buf, wo_buf, buf_sems = refs[8:12], *refs[-3:]
         refs = refs[:8] + refs[12:-3]
 
-        @pl.when(flag_ref[2] == 1)
+        @pl.when(flag_ref[5] == 1)
         def _():
             order_weights(flag_ref, refs[:4], ordered, (wi_buf, wo_buf), buf_sems)
 
@@ -267,7 +271,7 @@
         for k, (ours, theirs, buf) in enumerate(sources):
             if i:
                 pltpu.make_async_copy(buf, outs[k], sems.at[2 + k]).wait()
-            fetch(flag_ref[1] == i, ours, theirs, buf, sems.at[k])
+            fetch(flag_ref[0] == i, ours, theirs, buf, sems.at[k])
         for k, (ours, theirs, buf) in enumerate(sources):
             pltpu.make_async_copy(ours, buf, sems.at[k]).wait()
             pltpu.make_async_copy(buf, outs[2 * i + k], sems.at[2 + k]).start()
@@ -320,12 +324,14 @@
         going(count - 2, count % 2).wait()
         going(count - 1, 1 - count % 2).wait()
 
-    @pl.when(flag_ref[0] == 1)
-    def _():
-        for i in range(2):
-            own = flag_ref[1] == i
-            turn(own, *sources[:2], outs[2 * i], narrow_buf, wide_buf, True)
-            turn(own, *sources[2:], outs[2 * i + 1], wide_buf, narrow_buf, False)
+    for i in range(2):
+        own = flag_ref[0] == i
+        into = functools.partial(turn, own, *sources[:2], outs[2 * i], narrow_buf, wide_buf, True)
+        pl.when(flag_ref[1 + 2 * i] == 1)(into)
+        out = functools.partial(
+            turn, own, *sources[2:], outs[2 * i + 1], wide_buf, narrow_buf, False
+        )
+        pl.when(flag_ref[2 + 2 * i] == 1)(out)
 
 
 def ready_weights(flag, weights, held):
@@ -377,13 +383,13 @@
 
 
 def first_rows_kernel(ids_ref, counts_ref, x_ref, e_ref, out_ref, x_out, e_out, mask_out):
-    at_start, core, tp_pos = ids_ref[0], ids_ref[1], ids_ref[2]
+    at_start, tp_pos, mb = ids_ref[0], ids_ref[2], ids_ref[3]
     own_rows = x_ref.shape[1]
     row = tp_pos * own_rows + lax.broadcasted_iota(jnp.int32, (own_rows, 1), 0)
-    mask = (row < counts_ref[core]).astype(F32)
+    mask = (row < counts_ref[mb]).astype(F32)
     mask_out[...] = mask
-    x = x_ref[core].astype(F32) * mask
-    e = e_ref[core].astype(F32) * mask
+    x = x_ref[mb].astype(F32) * mask
+    e = e_ref[mb].astype(F32) * mask
     x_out[...] = x.astype(BF16)
     e_out[...] = e.astype(BF16)
     spread(out_ref, jnp.where(at_start == 1, x, e))
@@ -399,9 +405,9 @@
 
 def pack_kernel(ids_ref, jobs_ref, *refs):
     sources, ours, theirs, sems = refs[:-3], refs[-3], refs[-2], refs[-1]
-    core = ids_ref[1]
+    mb = ids_ref[3]
     copies = []
-    for n, (job, out) in enumerate(((jobs_ref[core], ours), (jobs_ref[1 - core], theirs))):
+    for n, (job, out) in enumerate(((jobs_ref[mb], ours), (jobs_ref[1 - mb], theirs))):
         start = 0
         for k, source in enumerate(sources):
             at = pl.ds(start, source.shape[2])
@@ -484,12 +490,12 @@
 
 
 def by_job_kernel(ids_ref, jobs_ref, ours, theirs, di_ref, ui_ref, do_ref, uo_ref):
-    core, tp_pos = ids_ref[1], ids_ref[2]
+    tp_pos, mb = ids_ref[2], ids_ref[3]
     owners, _, width = di_ref.shape
     cols = ui_ref.shape[2]
     for out in (di_ref, ui_ref, do_ref, uo_ref):
         out[...] = jnp.zeros(out.shape, F32)
-    for job, grads in ((jobs_ref[core], ours), (jobs_ref[1 - core], theirs)):
+    for job, grads in ((jobs_ref[mb], ours), (jobs_ref[1 - mb], theirs)):
         ui_ref[job] += grads[:, width : width + cols]
         do_ref[job] += grads[:, width + cols : width + 2 * cols]
         place = job - tp_pos * owners
@@ -544,10 +550,11 @@
     rows = own_rows * tp
     swap = [(s, s ^ 1) for s in range(segments)]
     onward = [(s, (s + 2) % segments) for s in range(segments)]
-    back = [(d, s) for s, d in onward]
+    across = [(s, d ^ 1) for s, d in onward]
     last_plane = planes - 1
 
-    ids = jnp.stack([(plane == 0).astype(jnp.int32), core, tp_pos]).astype(jnp.int32)
+    mb = core ^ sum((plane == p).astype(core.dtype) for p in range(planes) if CROSSED[p])
+    ids = jnp.stack([(plane == 0).astype(jnp.int32), core, tp_pos, mb]).astype(jnp.int32)
     full = shape_of(rows, width)
     some = shape_of(own_rows, width)
     w_first = (w_in[0], lax.ppermute(w_in[0], "segment", swap))
@@ -564,7 +571,7 @@
     )
     ends, ids, mod = lax.optimization_barrier((ends, ids, modulation[0]))
     mod_other = lax.ppermute(mod, "segment", swap)
-    mods = [jnp.where(core == i, mod, mod_other)[core] for i in range(2)]
+    mods = [jnp.where(core == i, mod, mod_other)[mb] for i in range(2)]
 
     adapters = [a[0] for a in (down_in, up_in, down_out, up_out)]
     packed = shape_of(rank, sum(a.shape[2] for a in adapters))
@@ -591,7 +598,8 @@
         flops=16 * rows * width * cols, bytes_accessed=16 * width * cols, transcendentals=rows * width
     )
     owns = [(core == i).astype(jnp.int32).reshape(1) for i in range(2)]
-    flag = jnp.stack([plane >= planes // 2, core, plane > 0]).astype(jnp.int32)
+    late, early = plane >= planes // 2, (plane == 0) & (core == STAGGERED)
+    flag = jnp.stack([core, late | early, late, late, late, plane > 0]).astype(jnp.int32)
     ends, flag = lax.optimization_barrier((ends, flag))
     (turned, ordered), x = lax.optimization_barrier(
         (ready_weights(flag, (*w_first, *w_second), ()), x)
@@ -686,9 +694,10 @@
             x,
             saved,
         )
-        x = lax.ppermute(x, "segment", onward)
+        x = lax.ppermute(x, "segment", across if CROSSED[p] != CROSSED[p + 1] else onward)
         if p == planes // 2 - 1:
-            flag = jnp.stack([plane < planes // 2, core]).astype(jnp.int32)
+            rest = ~late
+            flag = jnp.stack([core, rest & ~early, rest, rest, rest]).astype(jnp.int32)
             (turned, _), x = lax.optimization_barrier(
                 (ready_weights(flag, (*w_first, *w_second), turned), x)
             )
@@ -702,7 +711,8 @@
         plane == last_plane, turn, lambda x, saved, kept: (x, saved, kept), x, saved, kept
     )
     for p in range(last_plane - 1, -1, -1):
-        e = lax.ppermute(e, "segment", back)
+        pairs = across if CROSSED[p] != CROSSED[p + 1] else onward
+        e = lax.ppermute(e, "segment", [(d, s) for s, d in pairs])
         e, kept = lax.cond(
             plane == p,
             lambda e, saved, kept: backward_plane(e, saved, turned, p),

time: 591 us -> 558 us (0.944)
  starting transfers between devices: 308 us -> 278 us
    ppermute x1, starting transfers between devices: 45.3 us -> 12 us  [shards(): theirs = lax.ppermute(sent, 'segment', swap)]
where the time goes in v5:
time: 558 us; the launch traced here: 548 us
  starting transfers between devices  278 us (50%)
  waiting for transfers between devices  93.9 us (17%)
  blocking collectives  90.2 us (16%)
  Pallas kernels  59.4 us (11%)
  loops' own time  16.3 us (3%)
  local copies, waits for them, and re-layouts  9.07 us (2%)
    ppermute x3, starting transfers between devices, shards(): e = lax.ppermute(e, 'segment', [(d, s) for s, d in pairs])  198 us
    all_to_all x7, blocking collectives, exchanged(): got = lax.all_to_all(parts.reshape(tp, rows // tp, width), 'tp', 0, 0)  90.2 us
    ppermute x3, waiting for transfers between devices, shards(): e = lax.ppermute(e, 'segment', [(d, s) for s, d in pairs])  71.8 us
    ppermute x3, starting transfers between devices, shards(): lax.ppermute(x, 'segment', across if CROSSED[p] != CROSSED[p + 1] else on...  57.5 us
    pallas_call x2, Pallas kernels, ready_weights(): pl.pallas_call(functools.partial(ready_kernel, order=not held), out_shape...  30.8 us
    ppermute x1, starting transfers between devices, shards(): theirs = lax.ppermute(sent, 'segment', swap)  12 us
  transfers between devices with their start and end apart: 12, of which 8 were waited for; matrix products, arithmetic and copies ran while one was open for 0% of the time, Pallas kernels for 6%

profile of v5, /device:TPU:1, one launch (start us, length us, event | category | flops | bytes accessed | tf_op | source)
XLA Modules:
  0.0 548.1 jit_solution(4114329702371171003)
XLA Ops:
  6.7 7.9 %all-to-all-start.28 = ((bf16[16,8,3072]{2,1,0:T(8,128)(2,1)}), bf16[16,8,3072]{2,1,0:T(8,128)(2,1)S(1)}, u32[]{:S(2)}, u32[]{:S(2)}) async-start(bf16[16,8,3072]{2,1,0:T(8,128)(2,1)} %bitcast.67), calls=%async_computation.28 | async-start | bytes 1572864 | tf_op jit(solution)/shard_map/all_to_all | solution.py:524
  18.7 9.7 %all-to-all-done.28 = bf16[16,8,3072]{2,1,0:T(8,128)(2,1)S(1)} async-done(((bf16[16,8,3072]{2,1,0:T(8,128)(2,1)}), bf16[16,8,3072]{2,1,0:T(8,128)(2,1)S(1)}, u32[]{:S(2)}, u32[]{:S(2)}) %all-to-all-start.28) | async-done | bytes 786464 | tf_op jit(solution)/shard_map/all_to_all | solution.py:524
  29.2 51.5 %conditional.7 = (bf16[8,3072]{1,0:T(8,128)(2,1)S(1)}, bf16[8,3072]{1,0:T(8,128)(2,1)}, bf16[128,3072]{1,0:T(8,128)(2,1)S(1)}, bf16[128,768]{1,0:T(8,128)(2,1)},...) conditional(s32[]{:T(128)} %convert_element_type.12, ...), branch_computations={%region_0.1_spmd, %region_1.2_spmd} | conditional | flops 2415919104 | bytes 23724136 | solution.py:690
  29.7 4.4 block_forward.8
  34.1 14.1 %all_to_all.122 = bf16[16,8,3200]{2,1,0:T(8,128)(2,1)S(1)} all-to-all(bf16[16,8,3200]{2,1,0:T(8,128)(2,1)S(1)} %bitcast.142), channel_id=1, replica_groups=mesh['segment'=8,'tp'=16] {'tp'}, dimensions={0} | all-to-all | bytes 1638400 | tf_op jit(solution)/shard_map/cond/branch_1_fun/all_to_all | solution.py:524
  49.0 12.9 %all_to_all.123 = bf16[16,8,3072]{2,1,0:T(8,128)(2,1)S(1)} all-to-all(bf16[16,8,3072]{2,1,0:T(8,128)(2,1)S(1)} %bitcast.153), channel_id=1, replica_groups=mesh['segment'=8,'tp'=16] {'tp'}, dimensions={0} | all-to-all | bytes 1572864 | tf_op jit(solution)/shard_map/cond/branch_1_fun/all_to_all | solution.py:524
  61.9 4.6 block_forward.9
  66.5 13.2 %all_to_all.124 = bf16[16,8,3200]{2,1,0:T(8,128)(2,1)S(1)} all-to-all(bf16[16,8,3200]{2,1,0:T(8,128)(2,1)S(1)} %bitcast.143), channel_id=1, replica_groups=mesh['segment'=8,'tp'=16] {'tp'}, dimensions={0} | all-to-all | bytes 1638400 | tf_op jit(solution)/shard_map/cond/branch_1_fun/all_to_all | solution.py:524
  80.8 5.0 collective-permute-done.4
  85.8 7.4 %conditional.8 = ((bf16[8,3072]{1,0:T(8,128)(2,1)S(1)}, bf16[8,3072]{1,0:T(8,128)(2,1)}, bf16[128,3072]{1,0:T(8,128)(2,1)S(1)}, bf16[128,768]{1,0:T(8,128)(2,1)}...) conditional(s32[]{:T(128)} %convert_element_type.13, ...), branch_computations={%region_2.3_spmd, %region_3.4_spmd} | conditional | flops 7247757312 | bytes 129106184 | solution.py:690
  93.3 57.4 %collective-permute-start.5 = (bf16[8,3072]{1,0:T(8,128)(2,1)S(1)}, bf16[8,3072]{1,0:T(8,128)(2,1)S(1)}, u32[]{:S(2)}, u32[]{:S(2)}) collective-permute-start(bf16[8,3072]{1,0:T(8,128)(2,1)S(1)} %get-tuple-element.845), channel_id=1, source_target_pairs={{0,48},{16,32},{32,80},{48,64},{64,112},{80,96},{96,16},{112,0},{1... | collective-permute-start | bytes 147464 | tf_op jit(solution)/shard_map/ppermute | solution.py:697
  150.7 30.2 %ready_weights.3 = (bf16[768,3072]{1,0:T(8,128)(2,1)}, bf16[3072,768]{1,0:T(8,128)(2,1)}, bf16[768,3072]{1,0:T(8,128)(2,1)}, bf16[3072,768]{1,0:T(8,128)(2,1)}) custom-call(s32[5]{0:T(128)S(1)} %stack.66.flag_ref, bf16[3072,768]{1,0:T(8,128)(2,1)} %bitcast.168, ...), custom_call_target="tpu_custom_call", output_to_operand_aliasing={{0}: (5, {}), {1}: (6, {}), {2}: (7, {}), {3}: (8, {})} | custom-call | tf_op jit(solution)/shard_map/ready_weights/pallas_call | solution.py:347
  181.0 4.9 collective-permute-done.6
  185.9 14.1 %conditional.10 = (bf16[8,3072]{1,0:T(8,128)(2,1)S(1)}, bf16[8,3072]{1,0:T(8,128)(2,1)}, bf16[128,3072]{1,0:T(8,128)(2,1)S(1)}, bf16[128,768]{1,0:T(8,128)(2,1)}...) conditional(s32[]{:T(128)} %convert_element_type.14, ...), branch_computations={%region_6.7_spmd, %region_7.8_spmd} | conditional | flops 9059696640 | bytes 221741920 | solution.py:710
  200.0 132.4 %collective-permute-start.7 = (bf16[8,3072]{1,0:T(8,128)(2,1)S(1)}, bf16[8,3072]{1,0:T(8,128)(2,1)S(1)}, u32[]{:S(2)}, u32[]{:S(2)}) collective-permute-start(bf16[8,3072]{1,0:T(8,128)(2,1)S(1)} %get-tuple-element.879), channel_id=1, source_target_pairs={{48,0},{32,16},{80,32},{64,48},{112,64},{96,80},{16,96},{0,112},{4... | collective-permute-start | bytes 147464 | tf_op jit(solution)/shard_map/ppermute | solution.py:715
  338.3 62.2 %collective-permute-start.9 = (bf16[8,3072]{1,0:T(8,128)(2,1)S(1)}, bf16[8,3072]{1,0:T(8,128)(2,1)S(1)}, u32[]{:S(2)}, u32[]{:S(2)}) collective-permute-start(bf16[8,3072]{1,0:T(8,128)(2,1)S(1)} %get-tuple-element.913), channel_id=1, source_target_pairs={{48,0},{32,16},{80,32},{64,48},{112,64},{96,80},{16,96},{0,112},{4... | collective-permute-start | bytes 147464 | tf_op jit(solution)/shard_map/ppermute | solution.py:715
  400.5 69.5 %collective-permute-done.9 = bf16[8,3072]{1,0:T(8,128)(2,1)S(1)} collective-permute-done((bf16[8,3072]{1,0:T(8,128)(2,1)S(1)}, bf16[8,3072]{1,0:T(8,128)(2,1)S(1)}, u32[]{:S(2)}, u32[]{:S(2)}) %collective-permute-start.9) | collective-permute-done | bytes 49184 | tf_op jit(solution)/shard_map/ppermute | solution.py:715
  470.0 49.1 %conditional.13 = ((bf16[128,3072]{1,0:T(8,128)(2,1)}, bf16[16,128]{1,0:T(8,128)(2,1)}, f32[16,768]{1,0:T(8,128)}, f32[16,768]{1,0:T(8,128)}, bf16[128,3072]{1,0...) conditional(s32[]{:T(128)} %convert_element_type.12, ...), branch_computations={%region_12.13_spmd, %region_13.14_spmd} | conditional | flops 6643777536 | bytes 109805872 | solution.py:716
  470.1 13.7 %all_to_all.146 = bf16[16,8,3072]{2,1,0:T(8,128)(2,1)S(1)} all-to-all(bf16[16,8,3072]{2,1,0:T(8,128)(2,1)S(1)} %bitcast.163), channel_id=1, replica_groups=mesh['segment'=8,'tp'=16] {'tp'}, dimensions={0} | all-to-all | bytes 1572864 | tf_op jit(solution)/shard_map/cond/branch_1_fun/all_to_all | solution.py:524
  483.9 3.9 block_backward.14
  487.8 13.0 %all_to_all.147 = bf16[16,8,3072]{2,1,0:T(8,128)(2,1)S(1)} all-to-all(bf16[16,8,3072]{2,1,0:T(8,128)(2,1)S(1)} %bitcast.148), channel_id=1, replica_groups=mesh['segment'=8,'tp'=16] {'tp'}, dimensions={0} | all-to-all | bytes 1572864 | tf_op jit(solution)/shard_map/cond/branch_1_fun/all_to_all | solution.py:524
  502.5 13.0 %all_to_all.148 = bf16[16,8,3072]{2,1,0:T(8,128)(2,1)S(1)} all-to-all(bf16[16,8,3072]{2,1,0:T(8,128)(2,1)S(1)} %bitcast.157), channel_id=1, replica_groups=mesh['segment'=8,'tp'=16] {'tp'}, dimensions={0} | all-to-all | bytes 1572864 | tf_op jit(solution)/shard_map/cond/branch_1_fun/all_to_all | solution.py:524
  519.9 10.2 %all_to_all.149 = bf16[16,64,128]{2,1,0:T(8,128)(2,1)S(1)} all-to-all(bf16[16,64,128]{2,1,0:T(8,128)(2,1)S(1)} %bitcast.164), channel_id=1, replica_groups=mesh['segment'=8,'tp'=16] {'tp'}, dimensions={0} | all-to-all | bytes 524288 | tf_op jit(solution)/shard_map/all_to_all | solution.py:524
  532.4 12.0 %collective-permute-start.10 = (f32[16,7680]{1,0:T(8,128)S(1)}, f32[16,7680]{1,0:T(8,128)S(1)}, u32[]{:S(2)}, u32[]{:S(2)}) collective-permute-start(f32[16,7680]{1,0:T(8,128)S(1)} %get-tuple-element.925), channel_id=1, source_target_pairs={{0,16},{16,0},{32,48},{48,32},{64,80},{80,64},{96,112},{112,96},{1... | collective-permute-start | bytes 1474568 | tf_op jit(solution)/shard_map/ppermute | solution.py:733
  (85 shorter events, 36.6 us)
Async XLA Ops:
  0.6 16.9 %copy-start.50 = (f32[1,2,3,3072]{3,1,2,0:T(2,128)S(1)}, f32[1,2,3,3072]{3,1,2,0:T(2,128)}, u32[]{:S(2)}) copy-start(f32[1,2,3,3072]{3,1,2,0:T(2,128)} %param.29) | copy-start | bytes 221188
  0.6 27.8 %collective-permute-start = (bf16[3072,768]{1,0:T(8,128)(2,1)}, bf16[3072,768]{1,0:T(8,128)(2,1)}, u32[]{:S(2)}, u32[]{:S(2)}) collective-permute-start(bf16[3072,768]{1,0:T(8,128)(2,1)} %bitcast.165), channel_id=1, source_target_pairs={{0,16},{16,0},{32,48},{48,32},{64,80},{80,64},{96,112},{112,96},{1... | collective-permute-start | bytes 14155784 | tf_op jit(solution)/shard_map/ppermute | solution.py:560
  2.1 26.3 %collective-permute-start.1 = (bf16[768,3072]{1,0:T(8,128)(2,1)}, bf16[768,3072]{1,0:T(8,128)(2,1)}, u32[]{:S(2)}, u32[]{:S(2)}) collective-permute-start(bf16[768,3072]{1,0:T(8,128)(2,1)} %bitcast.169), channel_id=1, source_target_pairs={{0,16},{16,0},{32,48},{48,32},{64,80},{80,64},{96,112},{112,96},{1... | collective-permute-start | bytes 14155784 | tf_op jit(solution)/shard_map/ppermute | solution.py:561
  6.3 11.2 %collective-permute-start.2 = (f32[2,3,3072]{2,0,1:T(2,128)}, f32[2,3,3072]{2,0,1:T(2,128)S(1)}, u32[]{:S(2)}, u32[]{:S(2)}) collective-permute-start(f32[2,3,3072]{2,0,1:T(2,128)} %bitcast.179), channel_id=1, source_target_pairs={{0,16},{16,0},{32,48},{48,32},{64,80},{80,64},{96,112},{112,96},{1... | collective-permute-start | bytes 221192 | tf_op jit(solution)/shard_map/ppermute | solution.py:573
  6.7 21.7 %all-to-all-start.28 = ((bf16[16,8,3072]{2,1,0:T(8,128)(2,1)}), bf16[16,8,3072]{2,1,0:T(8,128)(2,1)S(1)}, u32[]{:S(2)}, u32[]{:S(2)}) async-start(bf16[16,8,3072]{2,1,0:T(8,128)(2,1)} %bitcast.67), calls=%async_computation.28 | async-start | bytes 1572864 | tf_op jit(solution)/shard_map/all_to_all | solution.py:524
  17.0 1.6 collective-permute-start.3
  18.6 167.3 %copy-start.43 = (bf16[16,768]{1,0:T(8,128)(2,1)}, bf16[16,768]{1,0:T(8,128)(2,1)S(1)}, u32[]{:S(2)}) copy-start(bf16[16,768]{1,0:T(8,128)(2,1)S(1)} %get-tuple-element.935) | copy-start | bytes 73732
  18.7 167.2 %copy-start.24 = (bf16[16,3072]{1,0:T(8,128)(2,1)}, bf16[16,3072]{1,0:T(8,128)(2,1)S(1)}, u32[]{:S(2)}) copy-start(bf16[16,3072]{1,0:T(8,128)(2,1)S(1)} %get-tuple-element.944) | copy-start | bytes 294916
  18.7 167.2 %copy-start.30 = (bf16[16,3072]{1,0:T(8,128)(2,1)}, bf16[16,3072]{1,0:T(8,128)(2,1)S(1)}, u32[]{:S(2)}) copy-start(bf16[16,3072]{1,0:T(8,128)(2,1)S(1)} %get-tuple-element.945) | copy-start | bytes 294916
  18.7 167.2 %copy-start.38 = (bf16[16,3072]{1,0:T(8,128)(2,1)}, bf16[16,3072]{1,0:T(8,128)(2,1)S(1)}, u32[]{:S(2)}) copy-start(bf16[16,3072]{1,0:T(8,128)(2,1)S(1)} %get-tuple-element.932) | copy-start | bytes 294916
  80.7 5.1 collective-permute-start.4
  93.3 87.6 %collective-permute-start.5 = (bf16[8,3072]{1,0:T(8,128)(2,1)S(1)}, bf16[8,3072]{1,0:T(8,128)(2,1)S(1)}, u32[]{:S(2)}, u32[]{:S(2)}) collective-permute-start(bf16[8,3072]{1,0:T(8,128)(2,1)S(1)} %get-tuple-element.845), channel_id=1, source_target_pairs={{0,48},{16,32},{32,80},{48,64},{64,112},{80,96},{96,16},{112,0},{1... | collective-permute-start | bytes 147464 | tf_op jit(solution)/shard_map/ppermute | solution.py:697
  180.9 5.0 collective-permute-start.6
  200.0 133.6 %collective-permute-start.7 = (bf16[8,3072]{1,0:T(8,128)(2,1)S(1)}, bf16[8,3072]{1,0:T(8,128)(2,1)S(1)}, u32[]{:S(2)}, u32[]{:S(2)}) collective-permute-start(bf16[8,3072]{1,0:T(8,128)(2,1)S(1)} %get-tuple-element.879), channel_id=1, source_target_pairs={{48,0},{32,16},{80,32},{64,48},{112,64},{96,80},{16,96},{0,112},{4... | collective-permute-start | bytes 147464 | tf_op jit(solution)/shard_map/ppermute | solution.py:715
  333.6 4.7 collective-permute-start.8
  338.3 131.7 %collective-permute-start.9 = (bf16[8,3072]{1,0:T(8,128)(2,1)S(1)}, bf16[8,3072]{1,0:T(8,128)(2,1)S(1)}, u32[]{:S(2)}, u32[]{:S(2)}) collective-permute-start(bf16[8,3072]{1,0:T(8,128)(2,1)S(1)} %get-tuple-element.913), channel_id=1, source_target_pairs={{48,0},{32,16},{80,32},{64,48},{112,64},{96,80},{16,96},{0,112},{4... | collective-permute-start | bytes 147464 | tf_op jit(solution)/shard_map/ppermute | solution.py:715
  470.0 13.8 %copy-start.42 = (bf16[16,3072]{1,0:T(8,128)(2,1)S(1)}, bf16[16,3072]{1,0:T(8,128)(2,1)}, u32[]{:S(2)}) copy-start(bf16[16,3072]{1,0:T(8,128)(2,1)} %get-tuple-element.647.refs_9_) | copy-start | bytes 294916 | tf_op jit(solution)/shard_map/cond
  470.0 13.8 %copy-start.47 = (bf16[16,768]{1,0:T(8,128)(2,1)S(1)}, bf16[16,768]{1,0:T(8,128)(2,1)}, u32[]{:S(2)}) copy-start(bf16[16,768]{1,0:T(8,128)(2,1)} %get-tuple-element.645.refs_7_) | copy-start | bytes 73732 | tf_op jit(solution)/shard_map/cond
  483.8 31.7 %slice-start.6 = ((s8[4718592]{0:T(1024)(128)(4,1)}), s8[4194304]{0:T(1024)(128)(4,1)S(1)}, s32[]{:S(2)}) async-start(s8[4718592]{0:T(1024)(128)(4,1)} %bitcast.92), calls=%async_computation.36 | async-start | bytes 8388608 | tf_op jit(solution)/shard_map/cond
  483.8 31.7 %slice-start.7 = ((s8[4718592]{0:T(1024)(128)(4,1)}), s8[524288]{0:T(1024)(128)(4,1)S(1)}, s32[]{:S(2)}) async-start(s8[4718592]{0:T(1024)(128)(4,1)} %bitcast.92), calls=%async_computation.37 | async-start | bytes 1048576 | tf_op jit(solution)/shard_map/cond
  483.9 31.6 %copy-start.29 = (bf16[16,3072]{1,0:T(8,128)(2,1)S(1)}, bf16[16,3072]{1,0:T(8,128)(2,1)}, u32[]{:S(2)}) copy-start(bf16[16,3072]{1,0:T(8,128)(2,1)} %get-tuple-element.656.refs_5_) | copy-start | bytes 294916 | tf_op jit(solution)/shard_map/cond
  483.9 31.6 %copy-start.35 = (bf16[16,3072]{1,0:T(8,128)(2,1)S(1)}, bf16[16,3072]{1,0:T(8,128)(2,1)}, u32[]{:S(2)}) copy-start(bf16[16,3072]{1,0:T(8,128)(2,1)} %get-tuple-element.659.refs_8_) | copy-start | bytes 294916 | tf_op jit(solution)/shard_map/cond
  519.1 26.7 %copy-start.20 = (s32[2]{0:T(128)S(1)}, s32[2]{0:T(128)}, u32[]{:S(2)}) copy-start(s32[2]{0:T(128)} %jobs_ref.3) | copy-start | bytes 28
  532.4 13.5 %collective-permute-start.10 = (f32[16,7680]{1,0:T(8,128)S(1)}, f32[16,7680]{1,0:T(8,128)S(1)}, u32[]{:S(2)}, u32[]{:S(2)}) collective-permute-start(f32[16,7680]{1,0:T(8,128)S(1)} %get-tuple-element.925), channel_id=1, source_target_pairs={{0,16},{16,0},{32,48},{48,32},{64,80},{80,64},{96,112},{112,96},{1... | collective-permute-start | bytes 1474568 | tf_op jit(solution)/shard_map/ppermute | solution.py:733
  (7 other events, 31.6 us)

commit v6 on v5

--- a/solution.py
+++ b/solution.py
@@ -458,51 +458,65 @@
 
 
 def gradients_kernel(ids_ref, got_ref, *refs):
-    per_block, (ours, theirs) = refs[:8], refs[8:]
-    rank, cols = per_block[2].shape
+    per_block, (ours, theirs) = refs[:4], refs[4:]
     width = per_block[0].shape[1]
+    rank = ours.shape[0]
     deep = 4 * rank
     total = None
     for k in range(0, got_ref.shape[0], deep):
         part = got_ref[k : k + deep].astype(F32)
         total = part if total is None else total + part
     for i in range(2):
-        g_ref, u_ref, ui_ref, do_ref = per_block[4 * i : 4 * i + 4]
+        g_ref, u_ref = per_block[2 * i : 2 * i + 2]
         low_out = total[i * rank : (i + 1) * rank].astype(BF16)
         g_low = total[(2 + i) * rank : (3 + i) * rank]
         high = g_low.astype(BF16)
-        rest = (g_low - high.astype(F32)).astype(BF16)
-        grads = (
-            dot(high, u_ref[...], 1, 0) + dot(rest, u_ref[...], 1, 0),
-            ui_ref[...],
-            do_ref[...],
-            dot(low_out, g_ref[...], 1, 0),
-        )
+        rest = g_low - high.astype(F32)
+        both = jnp.concatenate([high.astype(F32), rest], axis=0).astype(BF16)
+        both = dot(both, u_ref[...], 1, 0)
+        grads = (both[:rank] + both[rank:], dot(low_out, g_ref[...], 1, 0))
 
         def put(out, grads=grads):
-            start = 0
-            for grad in grads:
-                out[:, start : start + grad.shape[1]] = grad
-                start += grad.shape[1]
+            for k, grad in enumerate(grads):
+                out[:, k * width : (k + 1) * width] = grad
 
         pl.when(ids_ref[1] == i)(functools.partial(put, ours))
         pl.when(ids_ref[1] != i)(functools.partial(put, theirs))
 
 
-def by_job_kernel(ids_ref, jobs_ref, ours, theirs, di_ref, ui_ref, do_ref, uo_ref):
+def choose_kernel(ids_ref, *refs):
+    blocks, (ours, theirs) = refs[:4], refs[4:]
+    cols = blocks[0].shape[1]
+    for i in range(2):
+
+        def put(out, i=i):
+            for k in range(2):
+                out[:, k * cols : (k + 1) * cols] = blocks[2 * i + k][...]
+
+        pl.when(ids_ref[1] == i)(functools.partial(put, ours))
+        pl.when(ids_ref[1] != i)(functools.partial(put, theirs))
+
+
+def split_kernel(ids_ref, jobs_ref, ours, theirs, ui_ref, do_ref):
+    mb, cols = ids_ref[3], ui_ref.shape[2]
+    for out in (ui_ref, do_ref):
+        out[...] = jnp.zeros(out.shape, F32)
+    for job, grads in ((jobs_ref[mb], ours), (jobs_ref[1 - mb], theirs)):
+        ui_ref[job] += grads[:, :cols]
+        do_ref[job] += grads[:, cols:]
+
+
+def owned_kernel(ids_ref, jobs_ref, ours, theirs, di_ref, uo_ref):
     tp_pos, mb = ids_ref[2], ids_ref[3]
     owners, _, width = di_ref.shape
-    cols = ui_ref.shape[2]
-    for out in (di_ref, ui_ref, do_ref, uo_ref):
+    for out in (di_ref, uo_ref):
         out[...] = jnp.zeros(out.shape, F32)
     for job, grads in ((jobs_ref[mb], ours), (jobs_ref[1 - mb], theirs)):
-        ui_ref[job] += grads[:, width : width + cols]
-        do_ref[job] += grads[:, width + cols : width + 2 * cols]
         place = job - tp_pos * owners
 
         def owned(place=place, grads=grads):
             di_ref[place] += grads[:, :width]
-            uo_ref[place] += grads[:, width + 2 * cols :]
+            uo_ref[place] += grads[:, width:]
 
         pl.when((place >= 0) & (place < owners))(owned)
 
@@ -724,19 +738,33 @@
 
     narrow = (saved[0][3], saved[1][3], kept[0][1], kept[1][1])
     narrow_out = shape_of(tp * 4 * rank, rows)
-    got = exchanged(rows_call(narrow_kernel, narrow_out, *narrow, cost=ahead), tp)
-    wide = [shape_of(*packed.shape, dtype=F32)] * 2
-    per_block = [(*in_vmem(kept[i][0], saved[i][1]), kept[i][2], kept[i][3]) for i in range(2)]
-    mine, sent = rows_call(
-        gradients_kernel, wide, ids, got, *per_block[0], *per_block[1], scalars=1
-    )
+    spread_out = rows_call(narrow_kernel, narrow_out, *narrow, cost=ahead)
+    pair = [shape_of(rank, 2 * cols, dtype=F32)] * 2
+    split_mine, split_sent = rows_call(
+        choose_kernel, pair, ids, *kept[0][2:], *kept[1][2:], scalars=1
+    )
+    split_theirs = lax.ppermute(split_sent, "segment", swap)
+    got = exchanged(spread_out, tp)
+    wide = [shape_of(rank, 2 * width, dtype=F32)] * 2
+    per_block = [a for i in range(2) for a in in_vmem(kept[i][0], saved[i][1])]
+    mine, sent = rows_call(gradients_kernel, wide, ids, got, *per_block, scalars=1)
     theirs = lax.ppermute(sent, "segment", swap)
-    owned = shape_of(jobs // tp, rank, width, dtype=F32)
-    split = shape_of(jobs, rank, cols, dtype=F32)
-    grads = rows_call(
-        by_job_kernel, [owned, split, split, owned], ids, job_ids, mine, theirs, scalars=2
-    )
-    return tuple(grad[None] for grad in grads)
+    split = [shape_of(jobs, rank, cols, dtype=F32)] * 2
+    grad_ui, grad_do = rows_call(
+        split_kernel,
+        split,
+        ids,
+        job_ids,
+        split_mine,
+        split_theirs,
+        scalars=2,
+        cost=pl.CostEstimate(flops=0, bytes_accessed=8 * jobs * rank * cols, transcendentals=0),
+    )
+    owned = [shape_of(jobs // tp, rank, width, dtype=F32)] * 2
+    grad_di, grad_uo = rows_call(
+        owned_kernel, owned, ids, job_ids, mine, theirs, scalars=2
+    )
+    return tuple(grad[None] for grad in (grad_di, grad_ui, grad_do, grad_uo))
 
 
 def solution(mesh):

time: 558 us -> 556 us (level)
    pallas_call x9 -> x11, Pallas kernels: 10.6 us -> 12.3 us  [rows_call(): pl.pallas_call(kernel, out_shape=out, in_specs=[SMEM] * scalars + [VMEM]...]
  transfers between devices with their start and end apart: 12 -> 13, of which waited for: 8 -> 8; matrix products, arithmetic and copies ran while one was open for 0% -> 0% of each run, Pallas kernels for 6% -> 7%
where the time goes in v6:
time: 556 us; the launch traced here: 546 us
  starting transfers between devices  277 us (50%)
  waiting for transfers between devices  93 us (17%)
  blocking collectives  90.2 us (16%)
  Pallas kernels  60.2 us (11%)
  loops' own time  16.3 us (3%)
  local copies, waits for them, and re-layouts  8.2 us (1%)
    ppermute x3, starting transfers between devices, shards(): e = lax.ppermute(e, 'segment', [(d, s) for s, d in pairs])  197 us
    all_to_all x7, blocking collectives, exchanged(): got = lax.all_to_all(parts.reshape(tp, rows // tp, width), 'tp', 0, 0)  90.2 us
    ppermute x3, waiting for transfers between devices, shards(): e = lax.ppermute(e, 'segment', [(d, s) for s, d in pairs])  70.9 us
    ppermute x3, starting transfers between devices, shards(): lax.ppermute(x, 'segment', across if CROSSED[p] != CROSSED[p + 1] else on...  57.5 us
    pallas_call x2, Pallas kernels, ready_weights(): pl.pallas_call(functools.partial(ready_kernel, order=not held), out_shape...  31 us
    pallas_call x11, Pallas kernels, rows_call(): pl.pallas_call(kernel, out_shape=out, in_specs=[SMEM] * scalars + [VMEM]...  12.3 us
    ppermute x1, starting transfers between devices, shards(): theirs = lax.ppermute(sent, 'segment', swap)  12 us
  transfers between devices with their start and end apart: 13, of which 8 were waited for; matrix products, arithmetic and copies ran while one was open for 0% of the time, Pallas kernels for 7%

profile of v6, /device:TPU:1, one launch (start us, length us, event | category | flops | bytes accessed | tf_op | source)
XLA Modules:
  0.0 545.9 jit_solution(9840280111854772306)
XLA Ops:
  6.7 7.9 %all-to-all-start.28 = ((bf16[16,8,3072]{2,1,0:T(8,128)(2,1)}), bf16[16,8,3072]{2,1,0:T(8,128)(2,1)S(1)}, u32[]{:S(2)}, u32[]{:S(2)}) async-start(bf16[16,8,3072]{2,1,0:T(8,128)(2,1)} %bitcast.67), calls=%async_computation.28 | async-start | bytes 1572864 | tf_op jit(solution)/shard_map/all_to_all | solution.py:538
  18.7 9.7 %all-to-all-done.28 = bf16[16,8,3072]{2,1,0:T(8,128)(2,1)S(1)} async-done(((bf16[16,8,3072]{2,1,0:T(8,128)(2,1)}), bf16[16,8,3072]{2,1,0:T(8,128)(2,1)S(1)}, u32[]{:S(2)}, u32[]{:S(2)}) %all-to-all-start.28) | async-done | bytes 786464 | tf_op jit(solution)/shard_map/all_to_all | solution.py:538
  29.2 51.5 %conditional.7 = (bf16[8,3072]{1,0:T(8,128)(2,1)S(1)}, bf16[8,3072]{1,0:T(8,128)(2,1)}, bf16[128,3072]{1,0:T(8,128)(2,1)S(1)}, bf16[128,768]{1,0:T(8,128)(2,1)},...) conditional(s32[]{:T(128)} %convert_element_type.12, ...), branch_computations={%region_0.1_spmd, %region_1.2_spmd} | conditional | flops 2415919104 | bytes 23724136 | solution.py:704
  29.7 4.4 block_forward.8
  34.1 14.1 %all_to_all.122 = bf16[16,8,3200]{2,1,0:T(8,128)(2,1)S(1)} all-to-all(bf16[16,8,3200]{2,1,0:T(8,128)(2,1)S(1)} %bitcast.142), channel_id=1, replica_groups=mesh['segment'=8,'tp'=16] {'tp'}, dimensions={0} | all-to-all | bytes 1638400 | tf_op jit(solution)/shard_map/cond/branch_1_fun/all_to_all | solution.py:538
  49.0 12.9 %all_to_all.123 = bf16[16,8,3072]{2,1,0:T(8,128)(2,1)S(1)} all-to-all(bf16[16,8,3072]{2,1,0:T(8,128)(2,1)S(1)} %bitcast.153), channel_id=1, replica_groups=mesh['segment'=8,'tp'=16] {'tp'}, dimensions={0} | all-to-all | bytes 1572864 | tf_op jit(solution)/shard_map/cond/branch_1_fun/all_to_all | solution.py:538
  61.9 4.6 block_forward.9
  66.5 13.2 %all_to_all.124 = bf16[16,8,3200]{2,1,0:T(8,128)(2,1)S(1)} all-to-all(bf16[16,8,3200]{2,1,0:T(8,128)(2,1)S(1)} %bitcast.143), channel_id=1, replica_groups=mesh['segment'=8,'tp'=16] {'tp'}, dimensions={0} | all-to-all | bytes 1638400 | tf_op jit(solution)/shard_map/cond/branch_1_fun/all_to_all | solution.py:538
  80.8 5.0 collective-permute-done.4
  85.8 7.4 %conditional.8 = ((bf16[8,3072]{1,0:T(8,128)(2,1)S(1)}, bf16[8,3072]{1,0:T(8,128)(2,1)}, bf16[128,3072]{1,0:T(8,128)(2,1)S(1)}, bf16[128,768]{1,0:T(8,128)(2,1)}...) conditional(s32[]{:T(128)} %convert_element_type.13, ...), branch_computations={%region_2.3_spmd, %region_3.4_spmd} | conditional | flops 7247757312 | bytes 129106184 | solution.py:704
  93.3 57.3 %collective-permute-start.5 = (bf16[8,3072]{1,0:T(8,128)(2,1)S(1)}, bf16[8,3072]{1,0:T(8,128)(2,1)S(1)}, u32[]{:S(2)}, u32[]{:S(2)}) collective-permute-start(bf16[8,3072]{1,0:T(8,128)(2,1)S(1)} %get-tuple-element.847), channel_id=1, source_target_pairs={{0,48},{16,32},{32,80},{48,64},{64,112},{80,96},{96,16},{112,0},{1... | collective-permute-start | bytes 147464 | tf_op jit(solution)/shard_map/ppermute | solution.py:711
  150.7 30.3 %ready_weights.3 = (bf16[768,3072]{1,0:T(8,128)(2,1)}, bf16[3072,768]{1,0:T(8,128)(2,1)}, bf16[768,3072]{1,0:T(8,128)(2,1)}, bf16[3072,768]{1,0:T(8,128)(2,1)}) custom-call(s32[5]{0:T(128)S(1)} %stack.66.flag_ref, bf16[3072,768]{1,0:T(8,128)(2,1)} %bitcast.168, ...), custom_call_target="tpu_custom_call", output_to_operand_aliasing={{0}: (5, {}), {1}: (6, {}), {2}: (7, {}), {3}: (8, {})} | custom-call | tf_op jit(solution)/shard_map/ready_weights/pallas_call | solution.py:347
  181.1 5.1 collective-permute-done.6
  186.3 13.2 %conditional.10 = (bf16[8,3072]{1,0:T(8,128)(2,1)S(1)}, bf16[8,3072]{1,0:T(8,128)(2,1)}, bf16[128,3072]{1,0:T(8,128)(2,1)S(1)}, bf16[128,768]{1,0:T(8,128)(2,1)}...) conditional(s32[]{:T(128)} %convert_element_type.14, ...), branch_computations={%region_6.7_spmd, %region_7.8_spmd} | conditional | flops 9059696640 | bytes 218596160 | solution.py:724
  199.5 132.0 %collective-permute-start.7 = (bf16[8,3072]{1,0:T(8,128)(2,1)S(1)}, bf16[8,3072]{1,0:T(8,128)(2,1)S(1)}, u32[]{:S(2)}, u32[]{:S(2)}) collective-permute-start(bf16[8,3072]{1,0:T(8,128)(2,1)S(1)} %get-tuple-element.881), channel_id=1, source_target_pairs={{48,0},{32,16},{80,32},{64,48},{112,64},{96,80},{16,96},{0,112},{4... | collective-permute-start | bytes 147464 | tf_op jit(solution)/shard_map/ppermute | solution.py:729
  337.4 61.2 %collective-permute-start.9 = (bf16[8,3072]{1,0:T(8,128)(2,1)S(1)}, bf16[8,3072]{1,0:T(8,128)(2,1)S(1)}, u32[]{:S(2)}, u32[]{:S(2)}) collective-permute-start(bf16[8,3072]{1,0:T(8,128)(2,1)S(1)} %get-tuple-element.915), channel_id=1, source_target_pairs={{48,0},{32,16},{80,32},{64,48},{112,64},{96,80},{16,96},{0,112},{4... | collective-permute-start | bytes 147464 | tf_op jit(solution)/shard_map/ppermute | solution.py:729
  398.7 68.5 %collective-permute-done.9 = bf16[8,3072]{1,0:T(8,128)(2,1)S(1)} collective-permute-done((bf16[8,3072]{1,0:T(8,128)(2,1)S(1)}, bf16[8,3072]{1,0:T(8,128)(2,1)S(1)}, u32[]{:S(2)}, u32[]{:S(2)}) %collective-permute-start.9) | collective-permute-done | bytes 49184 | tf_op jit(solution)/shard_map/ppermute | solution.py:729
  467.2 48.2 %conditional.13 = ((bf16[128,3072]{1,0:T(8,128)(2,1)S(1)}, bf16[16,128]{1,0:T(8,128)(2,1)}, f32[16,768]{1,0:T(8,128)}, f32[16,768]{1,0:T(8,128)}, bf16[128,3072]...) conditional(s32[]{:T(128)} %convert_element_type.12, ...), branch_computations={%region_12.13_spmd, %region_13.14_spmd} | conditional | flops 6643777536 | bytes 109805872 | solution.py:730
  467.3 13.7 %all_to_all.146 = bf16[16,8,3072]{2,1,0:T(8,128)(2,1)S(1)} all-to-all(bf16[16,8,3072]{2,1,0:T(8,128)(2,1)S(1)} %bitcast.163), channel_id=1, replica_groups=mesh['segment'=8,'tp'=16] {'tp'}, dimensions={0} | all-to-all | bytes 1572864 | tf_op jit(solution)/shard_map/cond/branch_1_fun/all_to_all | solution.py:538
  481.1 3.9 block_backward.14
  485.0 13.0 %all_to_all.147 = bf16[16,8,3072]{2,1,0:T(8,128)(2,1)S(1)} all-to-all(bf16[16,8,3072]{2,1,0:T(8,128)(2,1)S(1)} %bitcast.148), channel_id=1, replica_groups=mesh['segment'=8,'tp'=16] {'tp'}, dimensions={0} | all-to-all | bytes 1572864 | tf_op jit(solution)/shard_map/cond/branch_1_fun/all_to_all | solution.py:538
  499.7 13.0 %all_to_all.148 = bf16[16,8,3072]{2,1,0:T(8,128)(2,1)S(1)} all-to-all(bf16[16,8,3072]{2,1,0:T(8,128)(2,1)S(1)} %bitcast.157), channel_id=1, replica_groups=mesh['segment'=8,'tp'=16] {'tp'}, dimensions={0} | all-to-all | bytes 1572864 | tf_op jit(solution)/shard_map/cond/branch_1_fun/all_to_all | solution.py:538
  516.1 10.2 %all_to_all.149 = bf16[16,64,128]{2,1,0:T(8,128)(2,1)S(1)} all-to-all(bf16[16,64,128]{2,1,0:T(8,128)(2,1)S(1)} %bitcast.164), channel_id=1, replica_groups=mesh['segment'=8,'tp'=16] {'tp'}, dimensions={0} | all-to-all | bytes 524288 | tf_op jit(solution)/shard_map/all_to_all | solution.py:538
  528.2 12.0 %collective-permute-start.10 = (f32[16,6144]{1,0:T(8,128)S(1)}, f32[16,6144]{1,0:T(8,128)S(1)}, u32[]{:S(2)}, u32[]{:S(2)}) collective-permute-start(f32[16,6144]{1,0:T(8,128)S(1)} %get-tuple-element.923), channel_id=1, source_target_pairs={{0,16},{16,0},{32,48},{48,32},{64,80},{80,64},{96,112},{112,96},{1... | collective-permute-start | bytes 1179656 | tf_op jit(solution)/shard_map/ppermute | solution.py:751
  (89 shorter events, 36.4 us)
Async XLA Ops:
  0.6 16.9 %copy-start.49 = (f32[1,2,3,3072]{3,1,2,0:T(2,128)S(1)}, f32[1,2,3,3072]{3,1,2,0:T(2,128)}, u32[]{:S(2)}) copy-start(f32[1,2,3,3072]{3,1,2,0:T(2,128)} %param.29) | copy-start | bytes 221188
  0.6 27.8 %collective-permute-start = (bf16[3072,768]{1,0:T(8,128)(2,1)}, bf16[3072,768]{1,0:T(8,128)(2,1)}, u32[]{:S(2)}, u32[]{:S(2)}) collective-permute-start(bf16[3072,768]{1,0:T(8,128)(2,1)} %bitcast.165), channel_id=1, source_target_pairs={{0,16},{16,0},{32,48},{48,32},{64,80},{80,64},{96,112},{112,96},{1... | collective-permute-start | bytes 14155784 | tf_op jit(solution)/shard_map/ppermute | solution.py:574
  2.1 26.3 %collective-permute-start.1 = (bf16[768,3072]{1,0:T(8,128)(2,1)}, bf16[768,3072]{1,0:T(8,128)(2,1)}, u32[]{:S(2)}, u32[]{:S(2)}) collective-permute-start(bf16[768,3072]{1,0:T(8,128)(2,1)} %bitcast.169), channel_id=1, source_target_pairs={{0,16},{16,0},{32,48},{48,32},{64,80},{80,64},{96,112},{112,96},{1... | collective-permute-start | bytes 14155784 | tf_op jit(solution)/shard_map/ppermute | solution.py:575
  6.3 11.2 %collective-permute-start.2 = (f32[2,3,3072]{2,0,1:T(2,128)}, f32[2,3,3072]{2,0,1:T(2,128)S(1)}, u32[]{:S(2)}, u32[]{:S(2)}) collective-permute-start(f32[2,3,3072]{2,0,1:T(2,128)} %bitcast.179), channel_id=1, source_target_pairs={{0,16},{16,0},{32,48},{48,32},{64,80},{80,64},{96,112},{112,96},{1... | collective-permute-start | bytes 221192 | tf_op jit(solution)/shard_map/ppermute | solution.py:587
  6.7 21.7 %all-to-all-start.28 = ((bf16[16,8,3072]{2,1,0:T(8,128)(2,1)}), bf16[16,8,3072]{2,1,0:T(8,128)(2,1)S(1)}, u32[]{:S(2)}, u32[]{:S(2)}) async-start(bf16[16,8,3072]{2,1,0:T(8,128)(2,1)} %bitcast.67), calls=%async_computation.28 | async-start | bytes 1572864 | tf_op jit(solution)/shard_map/all_to_all | solution.py:538
  17.0 1.6 collective-permute-start.3
  18.6 167.6 %copy-start.42 = (bf16[16,768]{1,0:T(8,128)(2,1)}, bf16[16,768]{1,0:T(8,128)(2,1)S(1)}, u32[]{:S(2)}) copy-start(bf16[16,768]{1,0:T(8,128)(2,1)S(1)} %get-tuple-element.939) | copy-start | bytes 73732
  18.7 167.6 %copy-start.24 = (bf16[16,3072]{1,0:T(8,128)(2,1)}, bf16[16,3072]{1,0:T(8,128)(2,1)S(1)}, u32[]{:S(2)}) copy-start(bf16[16,3072]{1,0:T(8,128)(2,1)S(1)} %get-tuple-element.948) | copy-start | bytes 294916
  18.7 167.6 %copy-start.30 = (bf16[16,3072]{1,0:T(8,128)(2,1)}, bf16[16,3072]{1,0:T(8,128)(2,1)S(1)}, u32[]{:S(2)}) copy-start(bf16[16,3072]{1,0:T(8,128)(2,1)S(1)} %get-tuple-element.949) | copy-start | bytes 294916
  18.7 167.6 %copy-start.37 = (bf16[16,3072]{1,0:T(8,128)(2,1)}, bf16[16,3072]{1,0:T(8,128)(2,1)S(1)}, u32[]{:S(2)}) copy-start(bf16[16,3072]{1,0:T(8,128)(2,1)S(1)} %get-tuple-element.936) | copy-start | bytes 294916
  80.7 5.1 collective-permute-start.4
  93.3 87.7 %collective-permute-start.5 = (bf16[8,3072]{1,0:T(8,128)(2,1)S(1)}, bf16[8,3072]{1,0:T(8,128)(2,1)S(1)}, u32[]{:S(2)}, u32[]{:S(2)}) collective-permute-start(bf16[8,3072]{1,0:T(8,128)(2,1)S(1)} %get-tuple-element.847), channel_id=1, source_target_pairs={{0,48},{16,32},{32,80},{48,64},{64,112},{80,96},{96,16},{112,0},{1... | collective-permute-start | bytes 147464 | tf_op jit(solution)/shard_map/ppermute | solution.py:711
  181.0 5.2 collective-permute-start.6
  199.5 133.2 %collective-permute-start.7 = (bf16[8,3072]{1,0:T(8,128)(2,1)S(1)}, bf16[8,3072]{1,0:T(8,128)(2,1)S(1)}, u32[]{:S(2)}, u32[]{:S(2)}) collective-permute-start(bf16[8,3072]{1,0:T(8,128)(2,1)S(1)} %get-tuple-element.881), channel_id=1, source_target_pairs={{48,0},{32,16},{80,32},{64,48},{112,64},{96,80},{16,96},{0,112},{4... | collective-permute-start | bytes 147464 | tf_op jit(solution)/shard_map/ppermute | solution.py:729
  332.7 4.7 collective-permute-start.8
  337.4 129.8 %collective-permute-start.9 = (bf16[8,3072]{1,0:T(8,128)(2,1)S(1)}, bf16[8,3072]{1,0:T(8,128)(2,1)S(1)}, u32[]{:S(2)}, u32[]{:S(2)}) collective-permute-start(bf16[8,3072]{1,0:T(8,128)(2,1)S(1)} %get-tuple-element.915), channel_id=1, source_target_pairs={{48,0},{32,16},{80,32},{64,48},{112,64},{96,80},{16,96},{0,112},{4... | collective-permute-start | bytes 147464 | tf_op jit(solution)/shard_map/ppermute | solution.py:729
  467.2 13.8 %copy-start.46 = (bf16[16,768]{1,0:T(8,128)(2,1)S(1)}, bf16[16,768]{1,0:T(8,128)(2,1)}, u32[]{:S(2)}) copy-start(bf16[16,768]{1,0:T(8,128)(2,1)} %get-tuple-element.645.refs_7_) | copy-start | bytes 73732 | tf_op jit(solution)/shard_map/cond
  481.0 31.7 %slice-start.6 = ((s8[4718592]{0:T(1024)(128)(4,1)}), s8[4194304]{0:T(1024)(128)(4,1)S(1)}, s32[]{:S(2)}) async-start(s8[4718592]{0:T(1024)(128)(4,1)} %bitcast.92), calls=%async_computation.36 | async-start | bytes 8388608 | tf_op jit(solution)/shard_map/cond
  481.0 31.7 %slice-start.7 = ((s8[4718592]{0:T(1024)(128)(4,1)}), s8[524288]{0:T(1024)(128)(4,1)S(1)}, s32[]{:S(2)}) async-start(s8[4718592]{0:T(1024)(128)(4,1)} %bitcast.92), calls=%async_computation.37 | async-start | bytes 1048576 | tf_op jit(solution)/shard_map/cond
  481.0 31.6 %copy-start.29 = (bf16[16,3072]{1,0:T(8,128)(2,1)S(1)}, bf16[16,3072]{1,0:T(8,128)(2,1)}, u32[]{:S(2)}) copy-start(bf16[16,3072]{1,0:T(8,128)(2,1)} %get-tuple-element.656.refs_5_) | copy-start | bytes 294916 | tf_op jit(solution)/shard_map/cond
  481.1 31.6 %copy-start.35 = (bf16[16,3072]{1,0:T(8,128)(2,1)S(1)}, bf16[16,3072]{1,0:T(8,128)(2,1)}, u32[]{:S(2)}) copy-start(bf16[16,3072]{1,0:T(8,128)(2,1)} %get-tuple-element.659.refs_8_) | copy-start | bytes 294916 | tf_op jit(solution)/shard_map/cond
  515.3 27.2 %copy-start.20 = (s32[2]{0:T(128)S(1)}, s32[2]{0:T(128)}, u32[]{:S(2)}) copy-start(s32[2]{0:T(128)} %jobs_ref.5) | copy-start | bytes 28
  528.2 16.2 %collective-permute-start.10 = (f32[16,6144]{1,0:T(8,128)S(1)}, f32[16,6144]{1,0:T(8,128)S(1)}, u32[]{:S(2)}, u32[]{:S(2)}) collective-permute-start(f32[16,6144]{1,0:T(8,128)S(1)} %get-tuple-element.923), channel_id=1, source_target_pairs={{0,16},{16,0},{32,48},{48,32},{64,80},{80,64},{96,112},{112,96},{1... | collective-permute-start | bytes 1179656 | tf_op jit(solution)/shard_map/ppermute | solution.py:751
  541.1 1.4 collective-permute-start.11
  (8 other events, 45.4 us)

commit v7 on v6

--- a/solution.py
+++ b/solution.py
@@ -665,7 +665,8 @@
             if i == 0:
                 g = exchanged(sent, tp)
             elif p == last_plane:
-                g = rows_call(gate_kernel, full, ends, mods[1])
+                gathered, _ = lax.optimization_barrier((ends, saved[1][3]))
+                g = rows_call(gate_kernel, full, gathered, mods[1])
             else:
                 g = exchanged(rows_call(gate_rows_kernel, full, e, mods[1], cost=ahead), tp)
             x, u, acts, low_part = saved[i]

time: 556 us -> 547 us (0.984)
  starting transfers between devices: 277 us -> 269 us
    ppermute x3, starting transfers between devices: 197 us -> 189 us  [shards(): e = lax.ppermute(e, 'segment', [(d, s) for s, d in pairs])]
where the time goes in v7:
time: 547 us; the launch traced here: 537 us
  starting transfers between devices  269 us (49%)
  waiting for transfers between devices  93.6 us (17%)
  blocking collectives  90 us (16%)
  Pallas kernels  59.3 us (11%)
  loops' own time  16.4 us (3%)
  local copies, waits for them, and re-layouts  8.01 us (1%)
    ppermute x3, starting transfers between devices, shards(): e = lax.ppermute(e, 'segment', [(d, s) for s, d in pairs])  189 us
    all_to_all x7, blocking collectives, exchanged(): got = lax.all_to_all(parts.reshape(tp, rows // tp, width), 'tp', 0, 0)  90 us
    ppermute x3, waiting for transfers between devices, shards(): e = lax.ppermute(e, 'segment', [(d, s) for s, d in pairs])  71.8 us
    ppermute x3, starting transfers between devices, shards(): lax.ppermute(x, 'segment', across if CROSSED[p] != CROSSED[p + 1] else on...  57.6 us
    pallas_call x2, Pallas kernels, ready_weights(): pl.pallas_call(functools.partial(ready_kernel, order=not held), out_shape...  30.9 us
    pallas_call x11, Pallas kernels, rows_call(): pl.pallas_call(kernel, out_shape=out, in_specs=[SMEM] * scalars + [VMEM]...  12.6 us
    ppermute x1, starting transfers between devices, shards(): theirs = lax.ppermute(sent, 'segment', swap)  12.1 us
  transfers between devices with their start and end apart: 13, of which 8 were waited for; matrix products, arithmetic and copies ran while one was open for 0% of the time, Pallas kernels for 7%

profile of v7, /device:TPU:1, one launch (start us, length us, event | category | flops | bytes accessed | tf_op | source)
XLA Modules:
  0.0 537.2 jit_solution(11695569929425463589)
XLA Ops:
  6.7 7.9 %all-to-all-start.28 = ((bf16[16,8,3072]{2,1,0:T(8,128)(2,1)}), bf16[16,8,3072]{2,1,0:T(8,128)(2,1)S(1)}, u32[]{:S(2)}, u32[]{:S(2)}) async-start(bf16[16,8,3072]{2,1,0:T(8,128)(2,1)} %bitcast.67), calls=%async_computation.28 | async-start | bytes 1572864 | tf_op jit(solution)/shard_map/all_to_all | solution.py:538
  18.7 9.7 %all-to-all-done.28 = bf16[16,8,3072]{2,1,0:T(8,128)(2,1)S(1)} async-done(((bf16[16,8,3072]{2,1,0:T(8,128)(2,1)}), bf16[16,8,3072]{2,1,0:T(8,128)(2,1)S(1)}, u32[]{:S(2)}, u32[]{:S(2)}) %all-to-all-start.28) | async-done | bytes 786464 | tf_op jit(solution)/shard_map/all_to_all | solution.py:538
  29.3 51.5 %conditional.7 = (bf16[8,3072]{1,0:T(8,128)(2,1)S(1)}, bf16[8,3072]{1,0:T(8,128)(2,1)}, bf16[128,3072]{1,0:T(8,128)(2,1)S(1)}, bf16[128,768]{1,0:T(8,128)(2,1)},...) conditional(s32[]{:T(128)} %convert_element_type.12, ...), branch_computations={%region_0.1_spmd, %region_1.2_spmd} | conditional | flops 2415919104 | bytes 23724136 | solution.py:705
  29.8 4.4 block_forward.8
  34.3 14.1 %all_to_all.122 = bf16[16,8,3200]{2,1,0:T(8,128)(2,1)S(1)} all-to-all(bf16[16,8,3200]{2,1,0:T(8,128)(2,1)S(1)} %bitcast.148), channel_id=1, replica_groups=mesh['segment'=8,'tp'=16] {'tp'}, dimensions={0} | all-to-all | bytes 1638400 | tf_op jit(solution)/shard_map/cond/branch_1_fun/all_to_all | solution.py:538
  49.2 12.9 %all_to_all.123 = bf16[16,8,3072]{2,1,0:T(8,128)(2,1)S(1)} all-to-all(bf16[16,8,3072]{2,1,0:T(8,128)(2,1)S(1)} %bitcast.160), channel_id=1, replica_groups=mesh['segment'=8,'tp'=16] {'tp'}, dimensions={0} | all-to-all | bytes 1572864 | tf_op jit(solution)/shard_map/cond/branch_1_fun/all_to_all | solution.py:538
  62.1 4.4 block_forward.9
  66.5 13.2 %all_to_all.124 = bf16[16,8,3200]{2,1,0:T(8,128)(2,1)S(1)} all-to-all(bf16[16,8,3200]{2,1,0:T(8,128)(2,1)S(1)} %bitcast.149), channel_id=1, replica_groups=mesh['segment'=8,'tp'=16] {'tp'}, dimensions={0} | all-to-all | bytes 1638400 | tf_op jit(solution)/shard_map/cond/branch_1_fun/all_to_all | solution.py:538
  80.8 5.0 collective-permute-done.4
  85.9 7.5 %conditional.8 = ((bf16[8,3072]{1,0:T(8,128)(2,1)S(1)}, bf16[8,3072]{1,0:T(8,128)(2,1)}, bf16[128,3072]{1,0:T(8,128)(2,1)S(1)}, bf16[128,768]{1,0:T(8,128)(2,1)}...) conditional(s32[]{:T(128)} %convert_element_type.13, ...), branch_computations={%region_2.3_spmd, %region_3.4_spmd} | conditional | flops 7247757312 | bytes 129106184 | solution.py:705
  93.3 57.4 %collective-permute-start.5 = (bf16[8,3072]{1,0:T(8,128)(2,1)S(1)}, bf16[8,3072]{1,0:T(8,128)(2,1)S(1)}, u32[]{:S(2)}, u32[]{:S(2)}) collective-permute-start(bf16[8,3072]{1,0:T(8,128)(2,1)S(1)} %get-tuple-element.848), channel_id=1, source_target_pairs={{0,48},{16,32},{32,80},{48,64},{64,112},{80,96},{96,16},{112,0},{1... | collective-permute-start | bytes 147464 | tf_op jit(solution)/shard_map/ppermute | solution.py:712
  150.8 30.2 %ready_weights.3 = (bf16[768,3072]{1,0:T(8,128)(2,1)}, bf16[3072,768]{1,0:T(8,128)(2,1)}, bf16[768,3072]{1,0:T(8,128)(2,1)}, bf16[3072,768]{1,0:T(8,128)(2,1)}) custom-call(s32[5]{0:T(128)S(1)} %stack.66.flag_ref, bf16[3072,768]{1,0:T(8,128)(2,1)} %bitcast.175, ...), custom_call_target="tpu_custom_call", output_to_operand_aliasing={{0}: (5, {}), {1}: (6, {}), {2}: (7, {}), {3}: (8, {})} | custom-call | tf_op jit(solution)/shard_map/ready_weights/pallas_call | solution.py:347
  181.2 4.8 collective-permute-done.6
  186.0 12.4 %conditional.10 = (bf16[8,3072]{1,0:T(8,128)(2,1)S(1)}, bf16[8,3072]{1,0:T(8,128)(2,1)}, bf16[128,3072]{1,0:T(8,128)(2,1)S(1)}, bf16[128,768]{1,0:T(8,128)(2,1)}...) conditional(s32[]{:T(128)} %convert_element_type.14, ...), branch_computations={%region_6.7_spmd, %region_7.8_spmd} | conditional | flops 9059696640 | bytes 193528608 | solution.py:725
  198.4 123.3 %collective-permute-start.7 = (bf16[8,3072]{1,0:T(8,128)(2,1)S(1)}, bf16[8,3072]{1,0:T(8,128)(2,1)}, u32[]{:S(2)}, u32[]{:S(2)}) collective-permute-start(bf16[8,3072]{1,0:T(8,128)(2,1)S(1)} %get-tuple-element.882), channel_id=1, source_target_pairs={{48,0},{32,16},{80,32},{64,48},{112,64},{96,80},{16,96},{0,112},{4... | collective-permute-start | bytes 147464 | tf_op jit(solution)/shard_map/ppermute | solution.py:730
  323.0 3.7 collective-permute-start.8
  328.1 61.5 %collective-permute-start.9 = (bf16[8,3072]{1,0:T(8,128)(2,1)}, bf16[8,3072]{1,0:T(8,128)(2,1)S(1)}, u32[]{:S(2)}, u32[]{:S(2)}) collective-permute-start(bf16[8,3072]{1,0:T(8,128)(2,1)} %get-tuple-element.916), channel_id=1, source_target_pairs={{48,0},{32,16},{80,32},{64,48},{112,64},{96,80},{16,96},{0,112},{4... | collective-permute-start | bytes 147464 | tf_op jit(solution)/shard_map/ppermute | solution.py:730
  389.6 69.1 %collective-permute-done.9 = bf16[8,3072]{1,0:T(8,128)(2,1)S(1)} collective-permute-done((bf16[8,3072]{1,0:T(8,128)(2,1)}, bf16[8,3072]{1,0:T(8,128)(2,1)S(1)}, u32[]{:S(2)}, u32[]{:S(2)}) %collective-permute-start.9) | collective-permute-done | bytes 49184 | tf_op jit(solution)/shard_map/ppermute | solution.py:730
  458.7 48.5 %conditional.13 = ((bf16[128,3072]{1,0:T(8,128)(2,1)S(1)}, bf16[16,128]{1,0:T(8,128)(2,1)}, f32[16,768]{1,0:T(8,128)}, f32[16,768]{1,0:T(8,128)}, bf16[128,3072]...) conditional(s32[]{:T(128)} %convert_element_type.12, ...), branch_computations={%region_12.13_spmd, %region_13.14_spmd} | conditional | flops 6643777536 | bytes 109707664 | solution.py:731
  460.4 13.6 %all_to_all.147 = bf16[16,8,3072]{2,1,0:T(8,128)(2,1)S(1)} all-to-all(bf16[16,8,3072]{2,1,0:T(8,128)(2,1)S(1)} %bitcast.170), channel_id=1, replica_groups=mesh['segment'=8,'tp'=16] {'tp'}, dimensions={0} | all-to-all | bytes 1572864 | tf_op jit(solution)/shard_map/cond/branch_1_fun/all_to_all | solution.py:538
  476.9 13.0 %all_to_all.148 = bf16[16,8,3072]{2,1,0:T(8,128)(2,1)S(1)} all-to-all(bf16[16,8,3072]{2,1,0:T(8,128)(2,1)S(1)} %bitcast.154), channel_id=1, replica_groups=mesh['segment'=8,'tp'=16] {'tp'}, dimensions={0} | all-to-all | bytes 1572864 | tf_op jit(solution)/shard_map/cond/branch_1_fun/all_to_all | solution.py:538
  491.6 13.0 %all_to_all.149 = bf16[16,8,3072]{2,1,0:T(8,128)(2,1)S(1)} all-to-all(bf16[16,8,3072]{2,1,0:T(8,128)(2,1)S(1)} %bitcast.164), channel_id=1, replica_groups=mesh['segment'=8,'tp'=16] {'tp'}, dimensions={0} | all-to-all | bytes 1572864 | tf_op jit(solution)/shard_map/cond/branch_1_fun/all_to_all | solution.py:538
  508.0 10.2 %all_to_all.150 = bf16[16,64,128]{2,1,0:T(8,128)(2,1)S(1)} all-to-all(bf16[16,64,128]{2,1,0:T(8,128)(2,1)S(1)} %bitcast.171), channel_id=1, replica_groups=mesh['segment'=8,'tp'=16] {'tp'}, dimensions={0} | all-to-all | bytes 524288 | tf_op jit(solution)/shard_map/all_to_all | solution.py:538
  519.4 12.1 %collective-permute-start.10 = (f32[16,6144]{1,0:T(8,128)S(1)}, f32[16,6144]{1,0:T(8,128)S(1)}, u32[]{:S(2)}, u32[]{:S(2)}) collective-permute-start(f32[16,6144]{1,0:T(8,128)S(1)} %get-tuple-element.924), channel_id=1, source_target_pairs={{0,16},{16,0},{32,48},{48,32},{64,80},{80,64},{96,112},{112,96},{1... | collective-permute-start | bytes 1179656 | tf_op jit(solution)/shard_map/ppermute | solution.py:752
  (97 shorter events, 36.0 us)
Async XLA Ops:
  0.6 16.9 %copy-start.50 = (f32[1,2,3,3072]{3,1,2,0:T(2,128)S(1)}, f32[1,2,3,3072]{3,1,2,0:T(2,128)}, u32[]{:S(2)}) copy-start(f32[1,2,3,3072]{3,1,2,0:T(2,128)} %param.29) | copy-start | bytes 221188
  0.6 27.8 %collective-permute-start = (bf16[3072,768]{1,0:T(8,128)(2,1)}, bf16[3072,768]{1,0:T(8,128)(2,1)}, u32[]{:S(2)}, u32[]{:S(2)}) collective-permute-start(bf16[3072,768]{1,0:T(8,128)(2,1)} %bitcast.172), channel_id=1, source_target_pairs={{0,16},{16,0},{32,48},{48,32},{64,80},{80,64},{96,112},{112,96},{1... | collective-permute-start | bytes 14155784 | tf_op jit(solution)/shard_map/ppermute | solution.py:574
  2.1 26.3 %collective-permute-start.1 = (bf16[768,3072]{1,0:T(8,128)(2,1)}, bf16[768,3072]{1,0:T(8,128)(2,1)}, u32[]{:S(2)}, u32[]{:S(2)}) collective-permute-start(bf16[768,3072]{1,0:T(8,128)(2,1)} %bitcast.176), channel_id=1, source_target_pairs={{0,16},{16,0},{32,48},{48,32},{64,80},{80,64},{96,112},{112,96},{1... | collective-permute-start | bytes 14155784 | tf_op jit(solution)/shard_map/ppermute | solution.py:575
  6.3 11.2 %collective-permute-start.2 = (f32[2,3,3072]{2,0,1:T(2,128)}, f32[2,3,3072]{2,0,1:T(2,128)S(1)}, u32[]{:S(2)}, u32[]{:S(2)}) collective-permute-start(f32[2,3,3072]{2,0,1:T(2,128)} %bitcast.186), channel_id=1, source_target_pairs={{0,16},{16,0},{32,48},{48,32},{64,80},{80,64},{96,112},{112,96},{1... | collective-permute-start | bytes 221192 | tf_op jit(solution)/shard_map/ppermute | solution.py:587
  6.7 21.7 %all-to-all-start.28 = ((bf16[16,8,3072]{2,1,0:T(8,128)(2,1)}), bf16[16,8,3072]{2,1,0:T(8,128)(2,1)S(1)}, u32[]{:S(2)}, u32[]{:S(2)}) async-start(bf16[16,8,3072]{2,1,0:T(8,128)(2,1)} %bitcast.67), calls=%async_computation.28 | async-start | bytes 1572864 | tf_op jit(solution)/shard_map/all_to_all | solution.py:538
  17.0 1.6 collective-permute-start.3
  18.6 167.4 %copy-start.25 = (bf16[16,768]{1,0:T(8,128)(2,1)}, bf16[16,768]{1,0:T(8,128)(2,1)S(1)}, u32[]{:S(2)}) copy-start(bf16[16,768]{1,0:T(8,128)(2,1)S(1)} %get-tuple-element.951) | copy-start | bytes 73732
  18.6 167.4 %copy-start.31 = (bf16[16,768]{1,0:T(8,128)(2,1)}, bf16[16,768]{1,0:T(8,128)(2,1)S(1)}, u32[]{:S(2)}) copy-start(bf16[16,768]{1,0:T(8,128)(2,1)S(1)} %get-tuple-element.952) | copy-start | bytes 73732
  18.6 167.4 %copy-start.37 = (bf16[16,768]{1,0:T(8,128)(2,1)}, bf16[16,768]{1,0:T(8,128)(2,1)S(1)}, u32[]{:S(2)}) copy-start(bf16[16,768]{1,0:T(8,128)(2,1)S(1)} %get-tuple-element.939) | copy-start | bytes 73732
  18.7 167.4 %copy-start.42 = (bf16[16,768]{1,0:T(8,128)(2,1)}, bf16[16,768]{1,0:T(8,128)(2,1)S(1)}, u32[]{:S(2)}) copy-start(bf16[16,768]{1,0:T(8,128)(2,1)S(1)} %get-tuple-element.940) | copy-start | bytes 73732
  18.7 167.3 %copy-start.19 = (bf16[16,3072]{1,0:T(8,128)(2,1)}, bf16[16,3072]{1,0:T(8,128)(2,1)S(1)}, u32[]{:S(2)}) copy-start(bf16[16,3072]{1,0:T(8,128)(2,1)S(1)} %get-tuple-element.937) | copy-start | bytes 294916
  80.8 5.1 collective-permute-start.4
  93.3 87.7 %collective-permute-start.5 = (bf16[8,3072]{1,0:T(8,128)(2,1)S(1)}, bf16[8,3072]{1,0:T(8,128)(2,1)S(1)}, u32[]{:S(2)}, u32[]{:S(2)}) collective-permute-start(bf16[8,3072]{1,0:T(8,128)(2,1)S(1)} %get-tuple-element.848), channel_id=1, source_target_pairs={{0,48},{16,32},{32,80},{48,64},{64,112},{80,96},{96,16},{112,0},{1... | collective-permute-start | bytes 147464 | tf_op jit(solution)/shard_map/ppermute | solution.py:712
  181.1 4.9 collective-permute-start.6
  198.4 124.5 %collective-permute-start.7 = (bf16[8,3072]{1,0:T(8,128)(2,1)S(1)}, bf16[8,3072]{1,0:T(8,128)(2,1)}, u32[]{:S(2)}, u32[]{:S(2)}) collective-permute-start(bf16[8,3072]{1,0:T(8,128)(2,1)S(1)} %get-tuple-element.882), channel_id=1, source_target_pairs={{48,0},{32,16},{80,32},{64,48},{112,64},{96,80},{16,96},{0,112},{4... | collective-permute-start | bytes 147464 | tf_op jit(solution)/shard_map/ppermute | solution.py:730
  323.0 5.1 collective-permute-start.8
  328.1 130.6 %collective-permute-start.9 = (bf16[8,3072]{1,0:T(8,128)(2,1)}, bf16[8,3072]{1,0:T(8,128)(2,1)S(1)}, u32[]{:S(2)}, u32[]{:S(2)}) collective-permute-start(bf16[8,3072]{1,0:T(8,128)(2,1)} %get-tuple-element.916), channel_id=1, source_target_pairs={{48,0},{32,16},{80,32},{64,48},{112,64},{96,80},{16,96},{0,112},{4... | collective-permute-start | bytes 147464 | tf_op jit(solution)/shard_map/ppermute | solution.py:730
  474.0 30.6 %slice-start.6 = ((s8[4718592]{0:T(1024)(128)(4,1)}), s8[4194304]{0:T(1024)(128)(4,1)S(1)}, s32[]{:S(2)}) async-start(s8[4718592]{0:T(1024)(128)(4,1)} %bitcast.92), calls=%async_computation.36 | async-start | bytes 8388608 | tf_op jit(solution)/shard_map/cond
  474.1 30.5 %slice-start.7 = ((s8[4718592]{0:T(1024)(128)(4,1)}), s8[524288]{0:T(1024)(128)(4,1)S(1)}, s32[]{:S(2)}) async-start(s8[4718592]{0:T(1024)(128)(4,1)} %bitcast.92), calls=%async_computation.37 | async-start | bytes 1048576 | tf_op jit(solution)/shard_map/cond
  474.1 30.5 %copy-start.30 = (bf16[16,768]{1,0:T(8,128)(2,1)S(1)}, bf16[16,768]{1,0:T(8,128)(2,1)}, u32[]{:S(2)}) copy-start(bf16[16,768]{1,0:T(8,128)(2,1)} %get-tuple-element.658.refs_6_) | copy-start | bytes 73732 | tf_op jit(solution)/shard_map/cond
  474.1 30.5 %copy-start.36 = (bf16[16,768]{1,0:T(8,128)(2,1)S(1)}, bf16[16,768]{1,0:T(8,128)(2,1)}, u32[]{:S(2)}) copy-start(bf16[16,768]{1,0:T(8,128)(2,1)} %get-tuple-element.659.refs_7_) | copy-start | bytes 73732 | tf_op jit(solution)/shard_map/cond
  507.3 26.6 %copy-start.15 = (s32[2]{0:T(128)S(1)}, s32[2]{0:T(128)}, u32[]{:S(2)}) copy-start(s32[2]{0:T(128)} %jobs_ref.5) | copy-start | bytes 28
  519.4 16.2 %collective-permute-start.10 = (f32[16,6144]{1,0:T(8,128)S(1)}, f32[16,6144]{1,0:T(8,128)S(1)}, u32[]{:S(2)}, u32[]{:S(2)}) collective-permute-start(f32[16,6144]{1,0:T(8,128)S(1)} %get-tuple-element.924), channel_id=1, source_target_pairs={{0,16},{16,0},{32,48},{48,32},{64,80},{80,64},{96,112},{112,96},{1... | collective-permute-start | bytes 1179656 | tf_op jit(solution)/shard_map/ppermute | solution.py:752
  532.5 1.4 collective-permute-start.11
  (12 other events, 93.8 us)

commit v8 on v7

--- a/solution.py
+++ b/solution.py
@@ -579,8 +579,7 @@
         [full, some, some, shape_of(own_rows, 1, dtype=F32)],
         ids,
         token_counts,
-        latents,
-        cotangent,
+        *in_hbm(latents, cotangent),
         scalars=2,
     )
     ends, ids, mod = lax.optimization_barrier((ends, ids, modulation[0]))

time: 547 us -> 546 us (level)
  no operation moved by 1% of the time
where the time goes in v8:
time: 546 us; the launch traced here: 536 us
  starting transfers between devices  269 us (49%)
  waiting for transfers between devices  93.5 us (17%)
  blocking collectives  90.1 us (17%)
  Pallas kernels  59.8 us (11%)
  loops' own time  16.4 us (3%)
  local copies, waits for them, and re-layouts  6.22 us (1%)
    ppermute x3, starting transfers between devices, shards(): e = lax.ppermute(e, 'segment', [(d, s) for s, d in pairs])  188 us
    all_to_all x7, blocking collectives, exchanged(): got = lax.all_to_all(parts.reshape(tp, rows // tp, width), 'tp', 0, 0)  90.1 us
    ppermute x3, waiting for transfers between devices, shards(): e = lax.ppermute(e, 'segment', [(d, s) for s, d in pairs])  71.8 us
    ppermute x3, starting transfers between devices, shards(): lax.ppermute(x, 'segment', across if CROSSED[p] != CROSSED[p + 1] else on...  57.5 us
    pallas_call x2, Pallas kernels, ready_weights(): pl.pallas_call(functools.partial(ready_kernel, order=not held), out_shape...  31 us
    pallas_call x11, Pallas kernels, rows_call(): pl.pallas_call(kernel, out_shape=out, in_specs=[SMEM] * scalars + [VMEM]...  13 us
    ppermute x1, starting transfers between devices, shards(): theirs = lax.ppermute(sent, 'segment', swap)  12.1 us
  transfers between devices with their start and end apart: 13, of which 8 were waited for; matrix products, arithmetic and copies ran while one was open for 0% of the time, Pallas kernels for 7%

profile of v8, /device:TPU:1, one launch (start us, length us, event | category | flops | bytes accessed | tf_op | source)
XLA Modules:
  0.0 535.9 jit_solution(5701796224777831766)
XLA Ops:
  5.3 7.9 %all-to-all-start.28 = ((bf16[16,8,3072]{2,1,0:T(8,128)(2,1)}), bf16[16,8,3072]{2,1,0:T(8,128)(2,1)S(1)}, u32[]{:S(2)}, u32[]{:S(2)}) async-start(bf16[16,8,3072]{2,1,0:T(8,128)(2,1)} %bitcast.67), calls=%async_computation.28 | async-start | bytes 1572864 | tf_op jit(solution)/shard_map/all_to_all | solution.py:538
  17.3 9.7 %all-to-all-done.28 = bf16[16,8,3072]{2,1,0:T(8,128)(2,1)S(1)} async-done(((bf16[16,8,3072]{2,1,0:T(8,128)(2,1)}), bf16[16,8,3072]{2,1,0:T(8,128)(2,1)S(1)}, u32[]{:S(2)}, u32[]{:S(2)}) %all-to-all-start.28) | async-done | bytes 786464 | tf_op jit(solution)/shard_map/all_to_all | solution.py:538
  27.9 51.5 %conditional.7 = (bf16[8,3072]{1,0:T(8,128)(2,1)S(1)}, bf16[8,3072]{1,0:T(8,128)(2,1)}, bf16[128,3072]{1,0:T(8,128)(2,1)S(1)}, bf16[128,768]{1,0:T(8,128)(2,1)},...) conditional(s32[]{:T(128)} %convert_element_type.12, ...), branch_computations={%region_0.1_spmd, %region_1.2_spmd} | conditional | flops 2415919104 | bytes 23724136 | solution.py:704
  28.4 4.4 block_forward.8
  32.9 14.1 %all_to_all.122 = bf16[16,8,3200]{2,1,0:T(8,128)(2,1)S(1)} all-to-all(bf16[16,8,3200]{2,1,0:T(8,128)(2,1)S(1)} %bitcast.148), channel_id=1, replica_groups=mesh['segment'=8,'tp'=16] {'tp'}, dimensions={0} | all-to-all | bytes 1638400 | tf_op jit(solution)/shard_map/cond/branch_1_fun/all_to_all | solution.py:538
  47.8 12.9 %all_to_all.123 = bf16[16,8,3072]{2,1,0:T(8,128)(2,1)S(1)} all-to-all(bf16[16,8,3072]{2,1,0:T(8,128)(2,1)S(1)} %bitcast.160), channel_id=1, replica_groups=mesh['segment'=8,'tp'=16] {'tp'}, dimensions={0} | all-to-all | bytes 1572864 | tf_op jit(solution)/shard_map/cond/branch_1_fun/all_to_all | solution.py:538
  60.7 4.4 block_forward.9
  65.2 13.2 %all_to_all.124 = bf16[16,8,3200]{2,1,0:T(8,128)(2,1)S(1)} all-to-all(bf16[16,8,3200]{2,1,0:T(8,128)(2,1)S(1)} %bitcast.149), channel_id=1, replica_groups=mesh['segment'=8,'tp'=16] {'tp'}, dimensions={0} | all-to-all | bytes 1638400 | tf_op jit(solution)/shard_map/cond/branch_1_fun/all_to_all | solution.py:538
  79.5 5.0 collective-permute-done.4
  84.5 7.5 %conditional.8 = ((bf16[8,3072]{1,0:T(8,128)(2,1)S(1)}, bf16[8,3072]{1,0:T(8,128)(2,1)}, bf16[128,3072]{1,0:T(8,128)(2,1)S(1)}, bf16[128,768]{1,0:T(8,128)(2,1)}...) conditional(s32[]{:T(128)} %convert_element_type.13, ...), branch_computations={%region_2.3_spmd, %region_3.4_spmd} | conditional | flops 7247757312 | bytes 129106184 | solution.py:704
  91.9 57.4 %collective-permute-start.5 = (bf16[8,3072]{1,0:T(8,128)(2,1)S(1)}, bf16[8,3072]{1,0:T(8,128)(2,1)S(1)}, u32[]{:S(2)}, u32[]{:S(2)}) collective-permute-start(bf16[8,3072]{1,0:T(8,128)(2,1)S(1)} %get-tuple-element.848), channel_id=1, source_target_pairs={{0,48},{16,32},{32,80},{48,64},{64,112},{80,96},{96,16},{112,0},{1... | collective-permute-start | bytes 147464 | tf_op jit(solution)/shard_map/ppermute | solution.py:711
  149.4 30.3 %ready_weights.3 = (bf16[768,3072]{1,0:T(8,128)(2,1)}, bf16[3072,768]{1,0:T(8,128)(2,1)}, bf16[768,3072]{1,0:T(8,128)(2,1)}, bf16[3072,768]{1,0:T(8,128)(2,1)}) custom-call(s32[5]{0:T(128)S(1)} %stack.66.flag_ref, bf16[3072,768]{1,0:T(8,128)(2,1)} %bitcast.175, ...), custom_call_target="tpu_custom_call", output_to_operand_aliasing={{0}: (5, {}), {1}: (6, {}), {2}: (7, {}), {3}: (8, {})} | custom-call | tf_op jit(solution)/shard_map/ready_weights/pallas_call | solution.py:347
  179.9 4.8 collective-permute-done.6
  184.7 12.4 %conditional.10 = (bf16[8,3072]{1,0:T(8,128)(2,1)S(1)}, bf16[8,3072]{1,0:T(8,128)(2,1)}, bf16[128,3072]{1,0:T(8,128)(2,1)S(1)}, bf16[128,768]{1,0:T(8,128)(2,1)}...) conditional(s32[]{:T(128)} %convert_element_type.14, ...), branch_computations={%region_6.7_spmd, %region_7.8_spmd} | conditional | flops 9059696640 | bytes 193528608 | solution.py:724
  197.1 123.3 %collective-permute-start.7 = (bf16[8,3072]{1,0:T(8,128)(2,1)S(1)}, bf16[8,3072]{1,0:T(8,128)(2,1)}, u32[]{:S(2)}, u32[]{:S(2)}) collective-permute-start(bf16[8,3072]{1,0:T(8,128)(2,1)S(1)} %get-tuple-element.882), channel_id=1, source_target_pairs={{48,0},{32,16},{80,32},{64,48},{112,64},{96,80},{16,96},{0,112},{4... | collective-permute-start | bytes 147464 | tf_op jit(solution)/shard_map/ppermute | solution.py:729
  321.6 3.7 collective-permute-start.8
  326.8 61.5 %collective-permute-start.9 = (bf16[8,3072]{1,0:T(8,128)(2,1)}, bf16[8,3072]{1,0:T(8,128)(2,1)S(1)}, u32[]{:S(2)}, u32[]{:S(2)}) collective-permute-start(bf16[8,3072]{1,0:T(8,128)(2,1)} %get-tuple-element.916), channel_id=1, source_target_pairs={{48,0},{32,16},{80,32},{64,48},{112,64},{96,80},{16,96},{0,112},{4... | collective-permute-start | bytes 147464 | tf_op jit(solution)/shard_map/ppermute | solution.py:729
  388.3 69.1 %collective-permute-done.9 = bf16[8,3072]{1,0:T(8,128)(2,1)S(1)} collective-permute-done((bf16[8,3072]{1,0:T(8,128)(2,1)}, bf16[8,3072]{1,0:T(8,128)(2,1)S(1)}, u32[]{:S(2)}, u32[]{:S(2)}) %collective-permute-start.9) | collective-permute-done | bytes 49184 | tf_op jit(solution)/shard_map/ppermute | solution.py:729
  457.4 48.5 %conditional.13 = ((bf16[128,3072]{1,0:T(8,128)(2,1)S(1)}, bf16[16,128]{1,0:T(8,128)(2,1)}, f32[16,768]{1,0:T(8,128)}, f32[16,768]{1,0:T(8,128)}, bf16[128,3072]...) conditional(s32[]{:T(128)} %convert_element_type.12, ...), branch_computations={%region_12.13_spmd, %region_13.14_spmd} | conditional | flops 6643777536 | bytes 109707664 | solution.py:730
  459.1 13.6 %all_to_all.147 = bf16[16,8,3072]{2,1,0:T(8,128)(2,1)S(1)} all-to-all(bf16[16,8,3072]{2,1,0:T(8,128)(2,1)S(1)} %bitcast.170), channel_id=1, replica_groups=mesh['segment'=8,'tp'=16] {'tp'}, dimensions={0} | all-to-all | bytes 1572864 | tf_op jit(solution)/shard_map/cond/branch_1_fun/all_to_all | solution.py:538
  475.6 13.0 %all_to_all.148 = bf16[16,8,3072]{2,1,0:T(8,128)(2,1)S(1)} all-to-all(bf16[16,8,3072]{2,1,0:T(8,128)(2,1)S(1)} %bitcast.154), channel_id=1, replica_groups=mesh['segment'=8,'tp'=16] {'tp'}, dimensions={0} | all-to-all | bytes 1572864 | tf_op jit(solution)/shard_map/cond/branch_1_fun/all_to_all | solution.py:538
  490.3 13.0 %all_to_all.149 = bf16[16,8,3072]{2,1,0:T(8,128)(2,1)S(1)} all-to-all(bf16[16,8,3072]{2,1,0:T(8,128)(2,1)S(1)} %bitcast.164), channel_id=1, replica_groups=mesh['segment'=8,'tp'=16] {'tp'}, dimensions={0} | all-to-all | bytes 1572864 | tf_op jit(solution)/shard_map/cond/branch_1_fun/all_to_all | solution.py:538
  506.7 10.2 %all_to_all.150 = bf16[16,64,128]{2,1,0:T(8,128)(2,1)S(1)} all-to-all(bf16[16,64,128]{2,1,0:T(8,128)(2,1)S(1)} %bitcast.171), channel_id=1, replica_groups=mesh['segment'=8,'tp'=16] {'tp'}, dimensions={0} | all-to-all | bytes 524288 | tf_op jit(solution)/shard_map/all_to_all | solution.py:538
  518.1 12.1 %collective-permute-start.10 = (f32[16,6144]{1,0:T(8,128)S(1)}, f32[16,6144]{1,0:T(8,128)S(1)}, u32[]{:S(2)}, u32[]{:S(2)}) collective-permute-start(f32[16,6144]{1,0:T(8,128)S(1)} %get-tuple-element.924), channel_id=1, source_target_pairs={{0,16},{16,0},{32,48},{48,32},{64,80},{80,64},{96,112},{112,96},{1... | collective-permute-start | bytes 1179656 | tf_op jit(solution)/shard_map/ppermute | solution.py:751
  (93 shorter events, 34.6 us)
Async XLA Ops:
  0.6 26.4 %collective-permute-start = (bf16[3072,768]{1,0:T(8,128)(2,1)}, bf16[3072,768]{1,0:T(8,128)(2,1)}, u32[]{:S(2)}, u32[]{:S(2)}) collective-permute-start(bf16[3072,768]{1,0:T(8,128)(2,1)} %bitcast.172), channel_id=1, source_target_pairs={{0,16},{16,0},{32,48},{48,32},{64,80},{80,64},{96,112},{112,96},{1... | collective-permute-start | bytes 14155784 | tf_op jit(solution)/shard_map/ppermute | solution.py:574
  2.1 24.9 %collective-permute-start.1 = (bf16[768,3072]{1,0:T(8,128)(2,1)}, bf16[768,3072]{1,0:T(8,128)(2,1)}, u32[]{:S(2)}, u32[]{:S(2)}) collective-permute-start(bf16[768,3072]{1,0:T(8,128)(2,1)} %bitcast.176), channel_id=1, source_target_pairs={{0,16},{16,0},{32,48},{48,32},{64,80},{80,64},{96,112},{112,96},{1... | collective-permute-start | bytes 14155784 | tf_op jit(solution)/shard_map/ppermute | solution.py:575
  4.9 11.2 %collective-permute-start.2 = (f32[2,3,3072]{2,0,1:T(2,128)}, f32[2,3,3072]{2,0,1:T(2,128)S(1)}, u32[]{:S(2)}, u32[]{:S(2)}) collective-permute-start(f32[2,3,3072]{2,0,1:T(2,128)} %bitcast.186), channel_id=1, source_target_pairs={{0,16},{16,0},{32,48},{48,32},{64,80},{80,64},{96,112},{112,96},{1... | collective-permute-start | bytes 221192 | tf_op jit(solution)/shard_map/ppermute | solution.py:586
  5.3 21.7 %all-to-all-start.28 = ((bf16[16,8,3072]{2,1,0:T(8,128)(2,1)}), bf16[16,8,3072]{2,1,0:T(8,128)(2,1)S(1)}, u32[]{:S(2)}, u32[]{:S(2)}) async-start(bf16[16,8,3072]{2,1,0:T(8,128)(2,1)} %bitcast.67), calls=%async_computation.28 | async-start | bytes 1572864 | tf_op jit(solution)/shard_map/all_to_all | solution.py:538
  15.6 1.6 collective-permute-start.3
  17.2 167.5 %copy-start.23 = (bf16[16,768]{1,0:T(8,128)(2,1)}, bf16[16,768]{1,0:T(8,128)(2,1)S(1)}, u32[]{:S(2)}) copy-start(bf16[16,768]{1,0:T(8,128)(2,1)S(1)} %get-tuple-element.951) | copy-start | bytes 73732
  17.3 167.5 %copy-start.29 = (bf16[16,768]{1,0:T(8,128)(2,1)}, bf16[16,768]{1,0:T(8,128)(2,1)S(1)}, u32[]{:S(2)}) copy-start(bf16[16,768]{1,0:T(8,128)(2,1)S(1)} %get-tuple-element.952) | copy-start | bytes 73732
  17.3 167.4 %copy-start.35 = (bf16[16,768]{1,0:T(8,128)(2,1)}, bf16[16,768]{1,0:T(8,128)(2,1)S(1)}, u32[]{:S(2)}) copy-start(bf16[16,768]{1,0:T(8,128)(2,1)S(1)} %get-tuple-element.939) | copy-start | bytes 73732
  17.3 167.4 %copy-start.40 = (bf16[16,768]{1,0:T(8,128)(2,1)}, bf16[16,768]{1,0:T(8,128)(2,1)S(1)}, u32[]{:S(2)}) copy-start(bf16[16,768]{1,0:T(8,128)(2,1)S(1)} %get-tuple-element.940) | copy-start | bytes 73732
  17.3 167.4 %copy-start.17 = (bf16[16,3072]{1,0:T(8,128)(2,1)}, bf16[16,3072]{1,0:T(8,128)(2,1)S(1)}, u32[]{:S(2)}) copy-start(bf16[16,3072]{1,0:T(8,128)(2,1)S(1)} %get-tuple-element.937) | copy-start | bytes 294916
  79.4 5.1 collective-permute-start.4
  91.9 87.8 %collective-permute-start.5 = (bf16[8,3072]{1,0:T(8,128)(2,1)S(1)}, bf16[8,3072]{1,0:T(8,128)(2,1)S(1)}, u32[]{:S(2)}, u32[]{:S(2)}) collective-permute-start(bf16[8,3072]{1,0:T(8,128)(2,1)S(1)} %get-tuple-element.848), channel_id=1, source_target_pairs={{0,48},{16,32},{32,80},{48,64},{64,112},{80,96},{96,16},{112,0},{1... | collective-permute-start | bytes 147464 | tf_op jit(solution)/shard_map/ppermute | solution.py:711
  179.8 4.9 collective-permute-start.6
  197.1 124.5 %collective-permute-start.7 = (bf16[8,3072]{1,0:T(8,128)(2,1)S(1)}, bf16[8,3072]{1,0:T(8,128)(2,1)}, u32[]{:S(2)}, u32[]{:S(2)}) collective-permute-start(bf16[8,3072]{1,0:T(8,128)(2,1)S(1)} %get-tuple-element.882), channel_id=1, source_target_pairs={{48,0},{32,16},{80,32},{64,48},{112,64},{96,80},{16,96},{0,112},{4... | collective-permute-start | bytes 147464 | tf_op jit(solution)/shard_map/ppermute | solution.py:729
  321.6 5.1 collective-permute-start.8
  326.8 130.6 %collective-permute-start.9 = (bf16[8,3072]{1,0:T(8,128)(2,1)}, bf16[8,3072]{1,0:T(8,128)(2,1)S(1)}, u32[]{:S(2)}, u32[]{:S(2)}) collective-permute-start(bf16[8,3072]{1,0:T(8,128)(2,1)} %get-tuple-element.916), channel_id=1, source_target_pairs={{48,0},{32,16},{80,32},{64,48},{112,64},{96,80},{16,96},{0,112},{4... | collective-permute-start | bytes 147464 | tf_op jit(solution)/shard_map/ppermute | solution.py:729
  472.7 30.6 %slice-start.6 = ((s8[4718592]{0:T(1024)(128)(4,1)}), s8[4194304]{0:T(1024)(128)(4,1)S(1)}, s32[]{:S(2)}) async-start(s8[4718592]{0:T(1024)(128)(4,1)} %bitcast.92), calls=%async_computation.36 | async-start | bytes 8388608 | tf_op jit(solution)/shard_map/cond
  472.7 15.9 %copy-start.47 = (bf16[8,3072]{1,0:T(8,128)(2,1)S(1)}, bf16[8,3072]{1,0:T(8,128)(2,1)}, u32[]{:S(2)}) copy-start(bf16[8,3072]{1,0:T(8,128)(2,1)} %copy-done.46) | copy-start | bytes 147460 | tf_op jit(solution)/shard_map/cond
  472.7 30.5 %slice-start.7 = ((s8[4718592]{0:T(1024)(128)(4,1)}), s8[524288]{0:T(1024)(128)(4,1)S(1)}, s32[]{:S(2)}) async-start(s8[4718592]{0:T(1024)(128)(4,1)} %bitcast.92), calls=%async_computation.37 | async-start | bytes 1048576 | tf_op jit(solution)/shard_map/cond
  472.8 30.5 %copy-start.28 = (bf16[16,768]{1,0:T(8,128)(2,1)S(1)}, bf16[16,768]{1,0:T(8,128)(2,1)}, u32[]{:S(2)}) copy-start(bf16[16,768]{1,0:T(8,128)(2,1)} %get-tuple-element.658.refs_6_) | copy-start | bytes 73732 | tf_op jit(solution)/shard_map/cond
  472.8 30.5 %copy-start.34 = (bf16[16,768]{1,0:T(8,128)(2,1)S(1)}, bf16[16,768]{1,0:T(8,128)(2,1)}, u32[]{:S(2)}) copy-start(bf16[16,768]{1,0:T(8,128)(2,1)} %get-tuple-element.659.refs_7_) | copy-start | bytes 73732 | tf_op jit(solution)/shard_map/cond
  505.9 26.6 %copy-start.13 = (s32[2]{0:T(128)S(1)}, s32[2]{0:T(128)}, u32[]{:S(2)}) copy-start(s32[2]{0:T(128)} %jobs_ref.5) | copy-start | bytes 28
  518.1 16.2 %collective-permute-start.10 = (f32[16,6144]{1,0:T(8,128)S(1)}, f32[16,6144]{1,0:T(8,128)S(1)}, u32[]{:S(2)}, u32[]{:S(2)}) collective-permute-start(f32[16,6144]{1,0:T(8,128)S(1)} %get-tuple-element.924), channel_id=1, source_target_pairs={{0,16},{16,0},{32,48},{48,32},{64,80},{80,64},{96,112},{112,96},{1... | collective-permute-start | bytes 1179656 | tf_op jit(solution)/shard_map/ppermute | solution.py:751
  531.2 1.4 collective-permute-start.11
  (10 other events, 91.6 us)
